TPU v7x, 256 devices: a whole 4x4x8 slice. The times are simulated.
256 devices in a mesh: seq: 64 (over z_hi, y, x, core), tp: 4 (over z_lo).
Axes of the slice: x: 4, y: 4, z: 8 (z_hi: 2, z_lo: 4; z = z_hi * 4 + z_lo), core: 2. Of those that a mesh axis runs over, the one named last changes fastest.
Arguments:
- tokens: bfloat16 [8192, 4096], P('seq', 'tp'), may hold values from -6 to 6
- in_weight: bfloat16 [3, 4096, 2048], P(None, 'seq', 'tp'), may hold values from -0.09375 to 0.09375
- short_weight: float32 [3, 3, 2048], P(None, None, 'tp'), may hold values from -3 to 3
- residues: float32 [2048, 8], P('tp'), may hold values from -0.6 to 0.6
- decay_rates: float32 [2048, 8], P('tp'), may hold values from 0.00012207031 to 0.0625
- skip_gain: float32 [2048], P('tp'), may hold values from -2 to 2
- out_weight: bfloat16 [2048, 4096], P('tp', 'seq'), may hold values from -0.125 to 0.125
Outputs:
- layer_out: bfloat16 [8192, 4096], P('seq', 'tp')
All inputs are finite; a program needn't handle non-finite values.
Results may differ from a plain program's by a relative error of at most 0.005.
The roundings to bfloat16 on the way count: a program that leaves them out, or rounds other values in their place, can miss the bound.
Values may be sent and summed in bfloat16 or wider, within the bound.
No kernel may reach another device: no remote copies, remote signals or barrier semaphores. Data moves between devices by JAX's collectives and lax.ppermute only.
A program may use at most 64 MiB of HBM per device.

v0:
```python
import math

import jax
import jax.numpy as jnp
from jax import lax
from jax.sharding import PartitionSpec as P

SHORT = 3


full_turn = 2.0 * math.pi
precise_mode = lax.Precision.HIGHEST


def passed_along(block, axis, distance):
    devices = range(lax.axis_size(axis))
    route = [(i - distance, i) for i in devices if i - distance in devices]
    return lax.ppermute(block, axis, route)


def angle_table(left_index, right_index, period):
    product = left_index[:, None] * right_index[None, :] % period
    angles = product.astype(jnp.float32) * (full_turn / period)
    return (jnp.cos(angles), jnp.sin(angles))


def column_section(columns, seq_index, seq_count, fft_length):
    row_block = columns.shape[1]
    frequencies = jnp.arange(2 * seq_count, dtype=jnp.int32)
    sources = jnp.arange(seq_count, dtype=jnp.int32)
    cos_table, sin_table = angle_table(frequencies, sources, 2 * seq_count)
    real_part = jnp.einsum("kq,qrc->krc", cos_table, columns, precision=precise_mode)
    imag_part = -jnp.einsum("kq,qrc->krc", sin_table, columns, precision=precise_mode)
    local_rows = seq_index * row_block + jnp.arange(row_block, dtype=jnp.int32)
    cos_twist, sin_twist = angle_table(frequencies, local_rows, fft_length)
    cos_twist = cos_twist[:, :, None]
    sin_twist = sin_twist[:, :, None]
    return jnp.stack(
        [
            real_part * cos_twist + imag_part * sin_twist,
            imag_part * cos_twist - real_part * sin_twist,
        ]
    )


def contract(table, values):
    return jnp.einsum("ab,kbc->kac", table, values, precision=precise_mode)


def row_forward(real_part, imag_part):
    row_count = real_part.shape[1]
    row_index = jnp.arange(row_count, dtype=jnp.int32)
    cos_table, sin_table = angle_table(row_index, row_index, row_count)
    return (
        contract(cos_table, real_part) + contract(sin_table, imag_part),
        contract(cos_table, imag_part) - contract(sin_table, real_part),
    )


def row_inverse(real_part, imag_part):
    row_count = real_part.shape[1]
    row_index = jnp.arange(row_count, dtype=jnp.int32)
    cos_table, sin_table = angle_table(row_index, row_index, row_count)
    return (
        contract(cos_table, real_part) - contract(sin_table, imag_part),
        contract(cos_table, imag_part) + contract(sin_table, real_part),
    )


def transform_convolve(gated_input, residues, decay_rates, seq_index, seq_count, tok_rows):
    row_block = tok_rows // seq_count
    fft_length = 2 * seq_count * tok_rows
    positions = (seq_index * tok_rows + jnp.arange(tok_rows, dtype=jnp.int32)).astype(jnp.float32)
    response = jnp.sum(
        residues[None] * jnp.exp(-decay_rates[None] * positions[:, None, None]), axis=2
    )
    data_columns, filter_columns = (
        lax.all_to_all(gated_input[None], "seq", split_axis=1, concat_axis=0, tiled=True),
        lax.all_to_all(response[None], "seq", split_axis=1, concat_axis=0, tiled=True),
    )
    data_spec, filter_spec = (
        lax.all_to_all(
            column_section(data_columns, seq_index, seq_count, fft_length),
            "seq",
            split_axis=1,
            concat_axis=2,
            tiled=True,
        ),
        lax.all_to_all(
            column_section(filter_columns, seq_index, seq_count, fft_length),
            "seq",
            split_axis=1,
            concat_axis=2,
            tiled=True,
        ),
    )
    data_real, data_imag = row_forward(data_spec[0], data_spec[1])
    filter_real, filter_imag = row_forward(filter_spec[0], filter_spec[1])
    prod_real = data_real * filter_real - data_imag * filter_imag
    prod_imag = data_real * filter_imag + data_imag * filter_real
    back_real, back_imag = row_inverse(prod_real, prod_imag)
    regrouped = lax.all_to_all(
        jnp.stack([back_real, back_imag]), "seq", split_axis=2, concat_axis=1, tiled=True
    )
    frequencies = jnp.arange(2 * seq_count, dtype=jnp.int32)
    sources = jnp.arange(seq_count, dtype=jnp.int32)
    local_rows = seq_index * row_block + jnp.arange(row_block, dtype=jnp.int32)
    cos_twist, sin_twist = angle_table(frequencies, local_rows, fft_length)
    cos_twist = cos_twist[:, :, None]
    sin_twist = sin_twist[:, :, None]
    turn_real = regrouped[0] * cos_twist - regrouped[1] * sin_twist
    turn_imag = regrouped[1] * cos_twist + regrouped[0] * sin_twist
    cos_table, sin_table = angle_table(frequencies, sources, 2 * seq_count)
    values = jnp.einsum("kq,krc->qrc", cos_table, turn_real, precision=precise_mode) - jnp.einsum(
        "kq,krc->qrc", sin_table, turn_imag, precision=precise_mode
    )
    restored = lax.all_to_all(values, "seq", split_axis=0, concat_axis=1, tiled=True)[0]
    return restored / fft_length


def shards(tokens, in_weight, short_weight, residues, decay_rates, skip_gain, out_weight):
    seq_count = lax.axis_size("seq")
    seq_index = lax.axis_index("seq")
    tok_rows = tokens.shape[0]
    channels = short_weight.shape[2]
    features = lax.all_gather(tokens, "tp", axis=1, tiled=True)
    projected = jnp.einsum(
        "td,sdc->stc",
        features,
        lax.all_gather(in_weight, "seq", axis=1, tiled=True),
        preferred_element_type=jnp.float32,
    ).astype(jnp.bfloat16)
    projected = lax.optimization_barrier(projected)
    earlier = passed_along(projected[:, tok_rows - (SHORT - 1) :, :], "seq", 1)
    extended = jnp.concatenate([earlier, projected], axis=1).astype(jnp.float32)
    streams = jnp.zeros((3, tok_rows, channels), jnp.float32)
    for tap_index in range(SHORT):
        lead_rows = SHORT - 1 - tap_index
        streams = (
            streams
            + short_weight[:, tap_index, None, :] * extended[:, lead_rows : lead_rows + tok_rows, :]
        )
    gated_input = streams[0] * streams[2]
    convolved = transform_convolve(
        gated_input, residues, decay_rates, seq_index, seq_count, tok_rows
    )
    mixed = convolved + skip_gain * gated_input
    gate_out = (streams[1] * mixed).astype(jnp.bfloat16)
    partials = jnp.dot(
        gate_out,
        lax.all_gather(out_weight, "seq", axis=1, tiled=True),
        preferred_element_type=jnp.float32,
    )
    return lax.psum_scatter(partials, "tp", scatter_dimension=1, tiled=True).astype(jnp.bfloat16)


def solution(mesh):
    return jax.shard_map(
        shards,
        mesh=mesh,
        in_specs=(
            P("seq", "tp"),
            P(None, "seq", "tp"),
            P(None, None, "tp"),
            P("tp", None),
            P("tp", None),
            P("tp"),
            P("tp", "seq"),
        ),
        out_specs=P("seq", "tp"),
        check_vma=False,
    )
```

profile of v0, /device:TPU:1, one launch (start us, length us, event | category | flops | bytes accessed | tf_op | source)
XLA Modules:
  0.0 450.0 jit_solution(11456859701648269457)
XLA Ops:
  6.5 0.7 all-gather.6.cloned.1.call-update
  7.3 0.7 all-gather.4.cloned.1.call-update
  8.0 0.7 neg.11
  8.7 1.5 multiply_reduce_fusion
  10.3 1.0 copy.72
  11.3 15.6 %all-to-all-start.2 = ((f32[1,128,512]{2,0,1:T(1,128)}), f32[1,128,512]{2,0,1:T(1,128)S(1)}, u32[]{:S(2)}, u32[]{:S(2)}) async-start(f32[1,128,512]{2,0,1:T(1,128)} %copy.72), calls=%async_computation.2 | async-start | bytes 524288 | tf_op jit(solution)/shard_map/all_to_all | solution.py:79
  26.9 24.8 %all-gather.6.cloned.1.call-done = bf16[128,4096]{1,0:T(8,128)(2,1)} async-done(((bf16[128,1024]{1,0:T(8,128)(2,1)}), bf16[128,4096]{1,0:T(8,128)(2,1)}) %all-gather.6.cloned.1.call-update) | async-done | bytes 1048592 | tf_op jit(solution)/shard_map/all_gather | solution.py:126
  51.8 137.9 %all-gather.4.cloned.1.call-done = bf16[3,4096,512]{2,1,0:T(8,128)(2,1)} async-done(((bf16[3,64,512]{2,1,0:T(8,128)(2,1)}), bf16[3,4096,512]{2,1,0:T(8,128)(2,1)}) %all-gather.4.cloned.1.call-update) | async-done | bytes 12582928 | tf_op jit(solution)/shard_map/all_gather | solution.py:130
  189.6 8.3 %fusion.2 = bf16[3,128,512]{1,2,0:T(8,128)(2,1)S(1)} fusion(bf16[3,4096,512]{2,1,0:T(8,128)(2,1)} %all-gather.4.cloned.1.call-done, bf16[128,4096]{1,0:T(8,128)(2,1)} %all-gather.6.cloned.1.call-done), kind=kOutput, calls=%fused_computation.12 | convolution fusion | flops 1610809344 | bytes 14024704 | tf_op jit(solution)/shard_map/td,sdc->stc/dot_general | solution.py:127
  198.1 3.0 collective-permute-start
  201.1 4.7 %collective-permute-done = bf16[3,2,512]{1,2,0:T(8,128)(2,1)S(1)} collective-permute-done((bf16[3,2,512]{1,2,0:T(8,128)(2,1)S(1)}, bf16[3,2,512]{1,2,0:T(8,128)(2,1)S(1)}, u32[]{:S(2)}, u32[]{:S(2)}) %collective-permute-start) | collective-permute-done | bytes 6176 | tf_op jit(solution)/shard_map/ppermute | solution.py:18
  206.1 1.2 fusion.4
  207.3 0.8 copy.65
  208.1 10.3 %all-to-all-start = ((f32[1,128,512]{2,0,1:T(1,128)}), f32[1,128,512]{2,0,1:T(1,128)S(1)}, u32[]{:S(2)}, u32[]{:S(2)}) async-start(f32[1,128,512]{2,0,1:T(1,128)} %copy.65), calls=%async_computation | async-start | bytes 524288 | tf_op jit(solution)/shard_map/all_to_all | solution.py:78
  219.3 0.8 convolution_negate_fusion
  220.1 0.7 fusion.27
  220.9 11.1 %all-to-all-done = f32[1,128,512]{2,0,1:T(1,128)S(1)} async-done(((f32[1,128,512]{2,0,1:T(1,128)}), f32[1,128,512]{2,0,1:T(1,128)S(1)}, u32[]{:S(2)}, u32[]{:S(2)}) %all-to-all-start) | async-done | bytes 262176 | tf_op jit(solution)/shard_map/all_to_all | solution.py:78
  232.7 0.8 convolution_negate_fusion.1
  233.5 1.9 add_bitcast_fusion
  235.5 1.8 copy.75
  237.3 4.5 %all-to-all-start.3 = ((f32[2,128,2,512]{3,2,0,1:T(2,128)}), f32[2,128,2,512]{3,2,0,1:T(2,128)S(1)}, u32[]{:S(2)}, u32[]{:S(2)}) async-start(f32[2,128,2,512]{3,2,0,1:T(2,128)} %copy.75), calls=%async_computation.3 | async-start | bytes 2097152 | tf_op jit(solution)/shard_map/all_to_all | solution.py:89
  241.9 1.8 copy.68
  243.7 19.2 %all-to-all-done.3 = f32[2,128,2,512]{3,2,0,1:T(2,128)S(1)} async-done(((f32[2,128,2,512]{3,2,0,1:T(2,128)}), f32[2,128,2,512]{3,2,0,1:T(2,128)S(1)}, u32[]{:S(2)}, u32[]{:S(2)}) %all-to-all-start.3) | async-done | bytes 1048608 | tf_op jit(solution)/shard_map/all_to_all | solution.py:89
  262.9 15.7 %all-to-all-start.1 = ((f32[2,128,2,512]{3,2,0,1:T(2,128)}), f32[2,128,2,512]{3,2,0,1:T(2,128)S(1)}, u32[]{:S(2)}, u32[]{:S(2)}) async-start(f32[2,128,2,512]{3,2,0,1:T(2,128)} %copy.68), calls=%async_computation.1 | async-start | bytes 2097152 | tf_op jit(solution)/shard_map/all_to_all | solution.py:82
  278.7 0.7 all-gather.8.cloned.1.call-update
  280.4 1.2 fusion.169
  281.8 1.2 copy.77
  283.1 16.5 %all-to-all-done.1 = f32[2,128,2,512]{3,2,0,1:T(2,128)S(1)} async-done(((f32[2,128,2,512]{3,2,0,1:T(2,128)}), f32[2,128,2,512]{3,2,0,1:T(2,128)S(1)}, u32[]{:S(2)}, u32[]{:S(2)}) %all-to-all-start.1) | async-done | bytes 1048608 | tf_op jit(solution)/shard_map/all_to_all | solution.py:82
  300.1 1.2 fusion.170
  301.5 1.3 copy.71
  302.8 0.8 fusion.50
  303.6 0.8 fusion.46
  304.4 0.8 fusion.48
  305.2 0.8 fusion.52
  306.1 0.8 convolution_add_fusion.1
  306.9 0.8 convolution_subtract_fusion.1
  307.7 0.8 convolution_add_fusion.2
  308.5 0.9 multiply_subtract_fusion
  309.4 0.8 fusion.10
  310.3 0.8 fusion.1
  311.1 0.8 fusion.6
  311.9 1.0 fusion
  313.6 48.8 %all_to_all.78 = f32[2,2,128,512]{3,1,0,2:T(2,128)S(1)} all-to-all(f32[2,2,128,512]{3,1,0,2:T(2,128)S(1)} %copy.83), channel_id=1, replica_groups=mesh['seq'=64,'tp'=4] {'seq'}, dimensions={2} | all-to-all | bytes 2097152 | tf_op jit(solution)/shard_map/all_to_all | solution.py:102
  365.4 21.5 %all_to_all.79 = f32[64,2,512]{2,1,0:T(2,128)S(1)} all-to-all(f32[64,2,512]{2,1,0:T(2,128)S(1)} %copy.87), channel_id=1, replica_groups=mesh['seq'=64,'tp'=4] {'seq'}, dimensions={0} | all-to-all | bytes 524288 | tf_op jit(solution)/shard_map/all_to_all | solution.py:117
  387.3 1.1 all-gather.8.cloned.1.call-done
  388.4 5.2 %fusion.32 = f32[128,4096]{1,0:T(8,128)} fusion(bf16[512,4096]{0,1:T(8,128)(2,1)} %all-gather.8.cloned.1.call-done, f32[3,128,512]{1,2,0:T(8,128)S(1)} %fusion.4, f32[128,512]{0,1:T(8,128)S(1)} %copy.88, f32[1,128,512]{1,2,0:T(8,128)S(1)} %slice_multiply_fusion.3, f32[512]{0:T(512)S(1)} %copy-done.3), kind=kOutput, calls=%fused_computation.61 | convolution fusion | flops 537133056 | bytes 7079936 | tf_op jit(solution)/shard_map/dot_general | solution.py:149
  393.6 47.9 %reduce-scatter.2.cloned.1.call-done = f32[128,1024]{1,0:T(8,128)} async-done(((f32[128,4096]{1,0:T(8,128)}), f32[128,1024]{1,0:T(8,128)}) %reduce-scatter.2.cloned.1.call-update) | async-done | bytes 524304 | tf_op jit(solution)/shard_map/reduce_scatter | solution.py:154
  441.5 1.8 convert_element_type.84
  (47 shorter events, 8.5 us)
Async XLA Ops:
  6.5 20.4 %copy-start.2 = (f32[3,3,512]{2,1,0:T(4,128)S(1)}, f32[3,3,512]{2,1,0:T(4,128)}, u32[]{:S(2)}) copy-start(f32[3,3,512]{2,1,0:T(4,128)} %param.9) | copy-start | bytes 55300
  6.5 45.2 %all-gather.6.cloned.1.call-start = ((), (), s32[]{:S(2)}) async-start(), calls=%async_computation.8 | async-start | bytes 1310720 | tf_op jit(solution)/shard_map/all_gather | solution.py:126
  7.3 182.4 %all-gather.4.cloned.1.call-start = ((), (), s32[]{:S(2)}) async-start(), calls=%async_computation.7 | async-start | bytes 12779520 | tf_op jit(solution)/shard_map/all_gather | solution.py:130
  11.3 196.9 %all-to-all-start.2 = ((f32[1,128,512]{2,0,1:T(1,128)}), f32[1,128,512]{2,0,1:T(1,128)S(1)}, u32[]{:S(2)}, u32[]{:S(2)}) async-start(f32[1,128,512]{2,0,1:T(1,128)} %copy.72), calls=%async_computation.2 | async-start | bytes 524288 | tf_op jit(solution)/shard_map/all_to_all | solution.py:79
  198.1 7.7 %collective-permute-start = (bf16[3,2,512]{1,2,0:T(8,128)(2,1)S(1)}, bf16[3,2,512]{1,2,0:T(8,128)(2,1)S(1)}, u32[]{:S(2)}, u32[]{:S(2)}) collective-permute-start(bf16[3,2,512]{1,2,0:T(8,128)(2,1)S(1)} %slice.72), channel_id=1, source_target_pairs={{0,4},{4,8},{8,12},{12,16},{16,20},{20,24},{24,28},{28,32},{32,36}... | collective-permute-start | bytes 18440 | tf_op jit(solution)/shard_map/ppermute | solution.py:18
  208.1 23.8 %all-to-all-start = ((f32[1,128,512]{2,0,1:T(1,128)}), f32[1,128,512]{2,0,1:T(1,128)S(1)}, u32[]{:S(2)}, u32[]{:S(2)}) async-start(f32[1,128,512]{2,0,1:T(1,128)} %copy.65), calls=%async_computation | async-start | bytes 524288 | tf_op jit(solution)/shard_map/all_to_all | solution.py:78
  235.5 6.3 %copy-start = (f32[1,128,2,512]{3,1,2,0:T(8,128)S(1)}, f32[1,128,2,512]{3,1,2,0:T(8,128)}, u32[]{:S(2)}) copy-start(f32[1,128,2,512]{3,1,2,0:T(8,128)} %get-tuple-element.20) | copy-start | bytes 1572868
  235.5 6.3 %copy-start.1 = (f32[1,128,2,512]{3,1,2,0:T(8,128)S(1)}, f32[1,128,2,512]{3,1,2,0:T(8,128)}, u32[]{:S(2)}) copy-start(f32[1,128,2,512]{3,1,2,0:T(8,128)} %get-tuple-element.21) | copy-start | bytes 1572868
  237.3 25.6 %all-to-all-start.3 = ((f32[2,128,2,512]{3,2,0,1:T(2,128)}), f32[2,128,2,512]{3,2,0,1:T(2,128)S(1)}, u32[]{:S(2)}, u32[]{:S(2)}) async-start(f32[2,128,2,512]{3,2,0,1:T(2,128)} %copy.75), calls=%async_computation.3 | async-start | bytes 2097152 | tf_op jit(solution)/shard_map/all_to_all | solution.py:89
  262.9 36.7 %all-to-all-start.1 = ((f32[2,128,2,512]{3,2,0,1:T(2,128)}), f32[2,128,2,512]{3,2,0,1:T(2,128)S(1)}, u32[]{:S(2)}, u32[]{:S(2)}) async-start(f32[2,128,2,512]{3,2,0,1:T(2,128)} %copy.68), calls=%async_computation.1 | async-start | bytes 2097152 | tf_op jit(solution)/shard_map/all_to_all | solution.py:82
  278.6 109.8 %all-gather.8.cloned.1.call-start = ((), (), s32[]{:S(2)}) async-start(), calls=%async_computation.9 | async-start | bytes 4259840 | tf_op jit(solution)/shard_map/all_gather | solution.py:151
  279.4 162.1 %reduce-scatter.2.cloned.1.call-start = ((), (), s32[]{:S(2)}) async-start(), calls=%async_computation.10 | async-start | bytes 2621440 | tf_op jit(solution)/shard_map/reduce_scatter | solution.py:154
  364.5 23.9 %copy-start.3 = (f32[512]{0:T(512)S(1)}, f32[512]{0:T(512)}, u32[]{:S(2)}) copy-start(f32[512]{0:T(512)} %param.12) | copy-start | bytes 6148
Sparse Core Ops, SparseCore 0:
  9.2 42.5 all-gather.5
  55.5 134.0 all-gather.3
  283.0 105.3 all-gather.7
  393.7 47.7 reduce-scatter.1
where the time goes:
time: 457 us; the launch traced here: 450 us
  waiting for transfers between devices  265 us (58%)
  blocking collectives  70.3 us (15%)
  starting transfers between devices  49.7 us (11%)
  matrix products  28.9 us (6%)
  local copies, waits for them, and re-layouts  14.9 us (3%)
  between operations  13.8 us (3%)
  other arithmetic  7.29 us (2%)
    all_gather x1, waiting for transfers between devices, shards(): lax.all_gather(in_weight, 'seq', axis=1, tiled=True)  138 us
    all_to_all x1, blocking collectives, transform_convolve(): lax.all_to_all(jnp.stack([back_real, back_imag]), 'seq', split_axis=2, co...  48.8 us
    reduce_scatter x1, waiting for transfers between devices, shards(): lax.psum_scatter(partials, 'tp', scatter_dimension=1, tiled=True)  47.9 us
    all_gather x1, waiting for transfers between devices, shards(): features = lax.all_gather(tokens, 'tp', axis=1, tiled=True)  24.8 us
    all_to_all x1, blocking collectives, transform_convolve(): lax.all_to_all(values, 'seq', split_axis=0, concat_axis=1, tiled=True)[0]  21.5 us
    all_to_all x1, waiting for transfers between devices, transform_convolve(): lax.all_to_all(column_section(filter_columns, seq_index, seq_count, fft_l...  19.2 us
    all_to_all x1, waiting for transfers between devices, transform_convolve(): lax.all_to_all(column_section(data_columns, seq_index, seq_count, fft_len...  16.5 us
    all_to_all x1, starting transfers between devices, transform_convolve(): lax.all_to_all(column_section(data_columns, seq_index, seq_count, fft_len...  15.7 us
  transfers between devices with their start and end apart: 9, of which 8 were waited for; matrix products, arithmetic and copies ran while one was open for 9% of the time, Pallas kernels for 0%

commit v1 on v0

v1 whole, which is shorter than its diff:
```python
import functools

import jax
import jax.numpy as jnp
import numpy as np
from jax import lax
from jax.experimental import pallas as pl
from jax.experimental.pallas import tpu as pltpu
from jax.sharding import Mesh, PartitionSpec as P

AXES = ("zh", "y", "x", "c", "zl")
SIZES = (2, 4, 4, 2, 4)
SEQ = ("zh", "y", "x", "c")
CHIPS = 16
BLOCK = 256
HALF = 128
LANES = 128
WIDE = 3 * LANES
MODES = 8
SUB = 8
STEPS = BLOCK // SUB
HALO = 16
GROUP = 64
F32 = jnp.float32
BF16 = jnp.bfloat16


def shifted(block, axis, distance):
    count = lax.axis_size(axis)
    return lax.ppermute(block, axis, [(i, (i + distance) % count) for i in range(count)])


def ring(block, axis):
    half = block.shape[0] // 2
    low = shifted(block, axis, 1)
    high = shifted(block, axis, -1)
    far_low = shifted(low[:half], axis, 1)
    far_high = shifted(high[half:], axis, -1)
    return [block, low, high, far_low, far_high]


RING_OFFSETS = ((0, None), (-1, None), (1, None), (2, 0), (2, 1))


def ring_pieces(pieces):
    half = len(pieces) // 2
    arrays = []
    for offset, part in RING_OFFSETS:
        kept = pieces if part is None else pieces[part * half : (part + 1) * half]
        arrays.append([(offset, piece) for piece in kept])
    return arrays


def front_kernel(
    pos,
    slabs,
    a0, a1, a2, a3, a4,
    b0, b1, b2, b3, b4,
    taps,
    rates,
    residues,
    skip,
    y_out,
    gate_out,
    sub_out,
    total_out,
    lhs,
    rhs,
    proj,
    gated,
    weight_sem,
    token_sem,
):
    own_y, own_x, own_zh, own_c = pos[0], pos[1], pos[2], pos[3]
    copies = []
    count = 0
    for kz, arrays in ((0, (a0, a1, a2, a3, a4)), (1, (b0, b1, b2, b3, b4))):
        first = [piece for array in ring_pieces([0, 1]) for piece in array]
        for ref, pieces in zip(arrays, ring_pieces(first)):
            for place, (outer, (inner, kc)) in enumerate(pieces):
                dy, dx = (outer, inner) if kz == 0 else (inner, outer)
                at_y = lax.rem(own_y + (dy + 4), 4)
                at_x = lax.rem(own_x + (dx + 4), 4)
                at_zh = own_zh if kz == 0 else 1 - own_zh
                at_c = own_c if kc == 0 else 1 - own_c
                row = (((at_zh * 4 + at_y) * 4 + at_x) * 2 + at_c) * GROUP
                copies.append(
                    pltpu.make_async_copy(
                        ref.at[pl.ds(place * GROUP, GROUP)],
                        rhs.at[pl.ds(pl.multiple_of(row, GROUP), GROUP)],
                        weight_sem.at[count],
                    )
                )
                count += 1
    for zh in range(2):
        for zl in range(4):
            for c in range(2):
                skipped = HALO * c
                rows = HALO + HALF - skipped
                copies.append(
                    pltpu.make_async_copy(
                        slabs.at[(zh * 4 + zl) * 2 + c, pl.ds(skipped, rows)],
                        lhs.at[
                            pl.ds(zh * (HALO + BLOCK) + c * (HALO + HALF), rows),
                            pl.ds(zl * 1024, 1024),
                        ],
                        token_sem.at[(zh * 4 + zl) * 2 + c],
                    )
                )
    for copy in copies:
        copy.start()
    for copy in copies:
        copy.wait()
    proj[...] = (
        jnp.dot(lhs[...], rhs[...], preferred_element_type=F32).astype(BF16).astype(F32)
    )
    gain = skip[...]
    for zh in range(2):
        base = zh * (HALO + BLOCK) + HALO
        streams = []
        for s in range(3):
            total = jnp.zeros((BLOCK, LANES), F32)
            for m in range(3):
                tap = taps[3 * s + m : 3 * s + m + 1, :]
                total = total + tap * proj[base - m : base - m + BLOCK, s * LANES : (s + 1) * LANES]
            streams.append(total)
        gated[zh * BLOCK : (zh + 1) * BLOCK, :] = streams[0] * streams[2]
        gate_out[zh * BLOCK : (zh + 1) * BLOCK, :] = streams[1]
    rate = rates[...]
    decay = jnp.exp(-rate)
    weight = residues[...]
    decays = [jnp.broadcast_to(decay[m : m + 1], (SUB, LANES)) for m in range(MODES)]
    weights = [jnp.broadcast_to(weight[m : m + 1], (SUB, LANES)) for m in range(MODES)]
    gain = jnp.broadcast_to(gain, (SUB, LANES))
    long_decay = jnp.exp(-rate * float(STEPS))
    for zh in range(2):
        state = [jnp.zeros((SUB, LANES), F32) for _ in range(MODES)]
        for i in range(STEPS):
            rows = pl.ds(zh * BLOCK + i, SUB, stride=STEPS)
            entry = gated[rows, :]
            state = [decays[m] * state[m] + entry for m in range(MODES)]
            terms = [weights[m] * state[m] for m in range(MODES)]
            while len(terms) > 1:
                terms = [terms[k] + terms[k + 1] for k in range(0, len(terms), 2)]
            y_out[rows, :] = terms[0] + gain * entry
        for m in range(MODES):
            sub_out[pl.ds(zh * SUB * MODES + m, SUB, stride=MODES), :] = state[m]
        total = jnp.zeros((MODES, LANES), F32)
        for sub in range(SUB):
            start = zh * SUB * MODES + sub * MODES
            total = long_decay * total + sub_out[start : start + MODES, :]
        total_out[zh * MODES : (zh + 1) * MODES, :] = total


def front(pos, slabs, a, b, taps, rates, residues, skip):
    hbm = pl.BlockSpec(memory_space=pl.ANY)
    vmem = pl.BlockSpec(memory_space=pltpu.VMEM)
    smem = pl.BlockSpec(memory_space=pltpu.SMEM)
    rows = 2 * (HALO + BLOCK)
    return pl.pallas_call(
        front_kernel,
        out_shape=(
            jax.ShapeDtypeStruct((2 * BLOCK, LANES), F32),
            jax.ShapeDtypeStruct((2 * BLOCK, LANES), F32),
            jax.ShapeDtypeStruct((2 * SUB * MODES, LANES), F32),
            jax.ShapeDtypeStruct((2 * MODES, LANES), F32),
        ),
        in_specs=[smem] + [hbm] * 11 + [vmem] * 4,
        out_specs=(vmem,) * 4,
        scratch_shapes=[
            pltpu.VMEM((rows, 4096), BF16),
            pltpu.VMEM((4096, WIDE), BF16),
            pltpu.VMEM((rows, WIDE), F32),
            pltpu.VMEM((2 * BLOCK, LANES), F32),
            pltpu.SemaphoreType.DMA((64,)),
            pltpu.SemaphoreType.DMA((16,)),
        ],
        compiler_params=pltpu.CompilerParams(vmem_limit_bytes=40 * 1024 * 1024),
        cost_estimate=pl.CostEstimate(
            flops=2 * rows * 4096 * WIDE, bytes_accessed=6_000_000, transcendentals=0
        ),
    )(pos, slabs, *a, *b, taps, rates, residues, skip)


def back_kernel(pos, totals, sub_states, y_in, gate_in, rates, residues, out, carried, mixed):
    block = pos[0] * 4 + pos[1]
    rate = rates[...]
    weight = residues[...]
    decay = jnp.exp(-rate)
    long_decay = jnp.exp(-rate * float(STEPS))
    carry = [jnp.zeros((MODES, LANES), F32) for _ in range(2)]
    for other in range(CHIPS):
        distance = block - 1 - other
        span = jnp.maximum(distance, 0).astype(F32) * float(BLOCK)
        near = jnp.where(distance >= 0, jnp.exp(-rate * span), 0.0)
        far = jnp.exp(-rate * ((distance + CHIPS).astype(F32) * float(BLOCK)))
        first = totals[2 * MODES * other : 2 * MODES * other + MODES, :]
        second = totals[2 * MODES * other + MODES : 2 * MODES * (other + 1), :]
        carry[0] = carry[0] + near * first
        carry[1] = carry[1] + near * second + far * first
    decays = [jnp.broadcast_to(decay[m : m + 1], (SUB, LANES)) for m in range(MODES)]
    for zh in range(2):
        state = carry[zh]
        for sub in range(SUB):
            start = zh * SUB * MODES + sub * MODES
            carried[start : start + MODES, :] = weight * state
            state = long_decay * state + sub_states[start : start + MODES, :]
        terms = [
            carried[pl.ds(zh * SUB * MODES + m, SUB, stride=MODES), :] for m in range(MODES)
        ]
        for i in range(STEPS):
            rows = pl.ds(zh * BLOCK + i, SUB, stride=STEPS)
            terms = [decays[m] * terms[m] for m in range(MODES)]
            sums = terms
            while len(sums) > 1:
                sums = [sums[k] + sums[k + 1] for k in range(0, len(sums), 2)]
            mixed[rows, :] = gate_in[rows, :] * (y_in[rows, :] + sums[0])
    out[...] = mixed[...].astype(BF16)


def back(pos, totals, sub_states, y, gate, rates, residues):
    vmem = pl.BlockSpec(memory_space=pltpu.VMEM)
    smem = pl.BlockSpec(memory_space=pltpu.SMEM)
    return pl.pallas_call(
        back_kernel,
        out_shape=jax.ShapeDtypeStruct((2 * BLOCK, LANES), BF16),
        in_specs=[smem] + [vmem] * 6,
        out_specs=vmem,
        scratch_shapes=[
            pltpu.VMEM((2 * SUB * MODES, LANES), F32),
            pltpu.VMEM((2 * BLOCK, LANES), F32),
        ],
        compiler_params=pltpu.CompilerParams(vmem_limit_bytes=16 * 1024 * 1024),
        cost_estimate=pl.CostEstimate(
            flops=4_000_000, bytes_accessed=800_000, transcendentals=40_000
        ),
    )(pos, totals, sub_states, y, gate, rates, residues)


def out_kernel(pos, gates, weights, out, held, sem):
    own_zh = pos[2]
    copies = []
    for k in range(2):
        for half in range(2):
            place = (own_zh if k == 0 else 1 - own_zh) * 2 + half
            copies.append(
                pltpu.make_async_copy(
                    weights.at[pl.ds(16 * half, 16), k], held.at[place], sem.at[2 * k + half]
                )
            )
    for copy in copies:
        copy.start()
    for copy in copies:
        copy.wait()
    total = jnp.zeros((HALF, 1024), F32)
    for zl in range(4):
        parts = [gates[(2 * zh + c) * 4 + zl] for zh in range(2) for c in range(2)]
        total = total + lax.dot_general(
            jnp.concatenate(parts, axis=1),
            held[zl].reshape(1024, 512),
            (((1,), (1,)), ((), ())),
            preferred_element_type=F32,
        )
    out[...] = total.astype(BF16)


def project_out(pos, gates, weights):
    hbm = pl.BlockSpec(memory_space=pl.ANY)
    vmem = pl.BlockSpec(memory_space=pltpu.VMEM)
    smem = pl.BlockSpec(memory_space=pltpu.SMEM)
    return pl.pallas_call(
        out_kernel,
        out_shape=jax.ShapeDtypeStruct((HALF, 1024), BF16),
        in_specs=[smem, vmem, hbm],
        out_specs=vmem,
        scratch_shapes=[
            pltpu.VMEM((4, 16, 64, 512), BF16),
            pltpu.SemaphoreType.DMA((4,)),
        ],
        compiler_params=pltpu.CompilerParams(vmem_limit_bytes=32 * 1024 * 1024),
        cost_estimate=pl.CostEstimate(
            flops=2 * HALF * 2048 * 1024, bytes_accessed=5_000_000, transcendentals=0
        ),
    )(pos, gates, weights)


def transposed_routes():
    near, far = [], []
    for zh, y, x, c, zl in np.ndindex(*SIZES):
        source = int(np.ravel_multi_index((zh, y, x, c, zl), SIZES))
        for route, to_zh in ((near, zl // 2), (far, 1 - zl // 2)):
            target = (to_zh, (zl % 2) * 2 + y % 2, x, c, zh * 2 + y // 2)
            route.append((source, int(np.ravel_multi_index(target, SIZES))))
    return near, far


def shards(tokens, in_weight, short_weight, residues, decay_rates, skip_gain, out_weight):
    zh, y, x, c = (lax.axis_index(axis) for axis in SEQ)
    pos = jnp.stack([y, x, zh, c]).astype(jnp.int32)
    group = zh * 2 + c

    halo = lax.ppermute(tokens[HALF - HALO :], SEQ, [(i, i + 1) for i in range(63)])
    slab = jnp.concatenate([halo, tokens], axis=0)
    slabs = lax.all_gather(slab, ("zh", "zl", "c"), axis=0, tiled=False)

    quarters = in_weight.reshape(3, GROUP, 4, LANES).transpose(2, 1, 0, 3).reshape(4, GROUP, WIDE)

    def quarter(flip):
        part = lax.dynamic_index_in_dim(quarters, group ^ flip, 0, keepdims=False)
        if flip == 0:
            return part
        return lax.ppermute(part, ("zh", "c"), [(i, i ^ flip) for i in range(4)])

    near = jnp.concatenate([quarter(0), quarter(1)], axis=0)
    far = jnp.concatenate([quarter(2), quarter(3)], axis=0)
    a = ring(jnp.concatenate(ring(near, "x"), axis=0), "y")
    b = ring(jnp.concatenate(ring(far, "y"), axis=0), "x")

    columns = out_weight.T
    routes = transposed_routes()
    gathered = lax.all_gather(
        jnp.stack([lax.ppermute(columns, AXES, route) for route in routes]),
        ("y", "x", "c"),
        axis=0,
        tiled=False,
    )

    def own_channels(table, axis):
        return lax.dynamic_slice_in_dim(table, group * LANES, LANES, axis)

    taps = own_channels(short_weight, 2).reshape(9, LANES)
    rates = own_channels(decay_rates, 0).T
    weights = own_channels(residues, 0).T
    skip = own_channels(skip_gain, 0)[None]
    mixed, gate, sub_states, totals = front(pos, slabs, a, b, taps, rates, weights, skip)
    every = lax.all_to_all(
        jnp.broadcast_to(totals[None], (CHIPS,) + totals.shape),
        ("y", "x"),
        split_axis=0,
        concat_axis=0,
        tiled=True,
    ).reshape(CHIPS * 2 * MODES, LANES)
    gate_out = back(pos, every, sub_states, mixed, gate, rates, weights)
    sent = jnp.broadcast_to(gate_out.reshape(4, 1, HALF, LANES), (4, 4, HALF, LANES))
    gates = lax.all_to_all(
        sent.reshape(16, HALF, LANES), ("zh", "c", "zl"), split_axis=0, concat_axis=0, tiled=True
    )
    return project_out(pos, gates, gathered)


def solution(mesh):
    split_mesh = Mesh(mesh.devices.reshape(SIZES), AXES)
    return jax.shard_map(
        shards,
        mesh=split_mesh,
        in_specs=(
            P(SEQ, "zl"),
            P(None, SEQ, "zl"),
            P(None, None, "zl"),
            P("zl", None),
            P("zl", None),
            P("zl"),
            P("zl", SEQ),
        ),
        out_specs=P(SEQ, "zl"),
        check_vma=False,
    )
```

time: 457 us -> 152 us (0.33); the launches traced: 450 us -> 151 us
  waiting for transfers between devices: 265 us -> 27 us
  blocking collectives: 70.3 us -> 11.8 us
  matrix products: 28.9 us -> 0 us
  starting transfers between devices: 49.7 us -> 72.3 us
  Pallas kernels: 0 us -> 14.1 us
  local copies, waits for them, and re-layouts: 14.9 us -> 9.41 us
  other arithmetic: 7.29 us -> 2.43 us
    all_gather x3 -> x2, waiting for transfers between devices: 164 us -> 0.01 us  [the longest x1 0.01 us: shards(): lax.all_gather(jnp.stack([lax.ppermute(columns, AXES, route) for route in...]
    all_to_all x2 -> x1, blocking collectives: 70.3 us -> 11.8 us  [shards(): lax.all_to_all(jnp.broadcast_to(totals[None], (CHIPS,) + totals.shape), (...]
    ppermute x1 -> x22, starting transfers between devices: 2.96 us -> 53 us  [the longest x16 22.4 us: shifted(): lax.ppermute(block, axis, [(i, (i + distance) % count) for i in range(cou...]
    reduce_scatter x1 -> x0, waiting for transfers between devices: 47.9 us -> none  [shards(): lax.psum_scatter(partials, 'tp', scatter_dimension=1, tiled=True)]
    all_to_all x4 -> x1, waiting for transfers between devices: 46.8 us -> 14.5 us  [shards(): lax.all_to_all(sent.reshape(16, HALF, LANES), ('zh', 'c', 'zl'), split_ax...]
    dot_general x20 -> x0, matrix products: 28.9 us -> none  [the longest x12 10.1 us: contract(): return jnp.einsum('ab,kbc->kac', table, values, precision=precise_mode)]
    all_to_all x4 -> x1, starting transfers between devices: 46.1 us -> 19.2 us  [shards(): lax.all_to_all(sent.reshape(16, HALF, LANES), ('zh', 'c', 'zl'), split_ax...]
    pallas_call x0 -> x3, Pallas kernels: none -> 14.1 us  [the longest x1 9.99 us: front(): pl.pallas_call(front_kernel, out_shape=(jax.ShapeDtypeStruct((2 * BLOCK,...]
  transfers between devices with their start and end apart: 9 -> 25, of which waited for: 8 -> 7; matrix products, arithmetic and copies ran while one was open for 9% -> 3% of each run, Pallas kernels for 0% -> 7%
where the time goes in v1:
time: 152 us; the launch traced here: 151 us
  starting transfers between devices  72.3 us (48%)
  waiting for transfers between devices  27 us (18%)
  Pallas kernels  14.1 us (9%)
  between operations  13.8 us (9%)
  blocking collectives  11.8 us (8%)
  local copies, waits for them, and re-layouts  9.41 us (6%)
  other arithmetic  2.43 us (2%)
    ppermute x16, starting transfers between devices, shifted(): lax.ppermute(block, axis, [(i, (i + distance) % count) for i in range(cou...  22.4 us
    all_to_all x1, starting transfers between devices, shards(): lax.all_to_all(sent.reshape(16, HALF, LANES), ('zh', 'c', 'zl'), split_ax...  19.2 us
    ppermute x3, starting transfers between devices, quarter(): return lax.ppermute(part, ('zh', 'c'), [(i, i ^ flip) for i in range(4)])  17.3 us
    all_to_all x1, waiting for transfers between devices, shards(): lax.all_to_all(sent.reshape(16, HALF, LANES), ('zh', 'c', 'zl'), split_ax...  14.5 us
    all_to_all x1, blocking collectives, shards(): lax.all_to_all(jnp.broadcast_to(totals[None], (CHIPS,) + totals.shape), (...  11.8 us
    pallas_call x1, Pallas kernels, front(): pl.pallas_call(front_kernel, out_shape=(jax.ShapeDtypeStruct((2 * BLOCK,...  9.99 us
    ppermute x2, starting transfers between devices, shards(): lax.ppermute(columns, AXES, route)  8.92 us
    ppermute x16, waiting for transfers between devices, shifted(): lax.ppermute(block, axis, [(i, (i + distance) % count) for i in range(cou...  5.77 us
  transfers between devices with their start and end apart: 25, of which 7 were waited for; matrix products, arithmetic and copies ran while one was open for 3% of the time, Pallas kernels for 7%

profile of v1, /device:TPU:1, one launch (start us, length us, event | category | flops | bytes accessed | tf_op | source)
XLA Modules:
  0.0 150.8 jit_solution(13311452913327789615)
XLA Ops:
  6.5 0.8 slice.27
  7.3 4.5 %collective-permute-start = (bf16[16,1024]{1,0:T(8,128)(2,1)S(1)}, bf16[16,1024]{1,0:T(8,128)(2,1)S(1)}, u32[]{:S(2)}, u32[]{:S(2)}) collective-permute-start(bf16[16,1024]{1,0:T(8,128)(2,1)S(1)} %slice.27), channel_id=1, source_target_pairs={{0,4},{4,8},{8,12},{12,16},{16,20},{20,24},{24,28},{28,32},{32,36}... | collective-permute-start | bytes 98312 | tf_op jit(solution)/shard_map/ppermute | solution.py:302
  11.8 1.0 collective-permute-done
  12.8 1.7 %pad_maximum_fusion = bf16[144,1024]{1,0:T(8,128)(2,1)} fusion(bf16[128,1024]{1,0:T(8,128)(2,1)} %param.7, bf16[16,1024]{1,0:T(8,128)(2,1)S(1)} %collective-permute-done), kind=kLoop, calls=%fused_computation | loop fusion | flops 589824 | bytes 589824 | tf_op jit(solution)/shard_map/concatenate | solution.py:303
  14.5 0.0 all-gather.5.cloned.1.call-update
  14.5 0.0 all-gather.7.cloned.1.call-start
  14.6 1.5 collective-permute-start.20
  16.1 7.4 %collective-permute-start.21 = (bf16[64,512]{1,0:T(8,128)(2,1)}, bf16[64,512]{1,0:T(8,128)(2,1)S(1)}, u32[]{:S(2)}, u32[]{:S(2)}) collective-permute-start(bf16[64,512]{1,0:T(8,128)(2,1)} %bitcast.38), channel_id=1, source_target_pairs={{0,128},{1,192},{2,0},{3,64},{4,132},{5,196},{6,4},{7,68},{8,136},... | collective-permute-start | bytes 196616 | tf_op jit(solution)/shard_map/ppermute | solution.py:322
  23.5 2.1 %collective-permute-done.21 = bf16[64,512]{1,0:T(8,128)(2,1)S(1)} collective-permute-done((bf16[64,512]{1,0:T(8,128)(2,1)}, bf16[64,512]{1,0:T(8,128)(2,1)S(1)}, u32[]{:S(2)}, u32[]{:S(2)}) %collective-permute-start.21) | collective-permute-done | bytes 65568 | tf_op jit(solution)/shard_map/ppermute | solution.py:322
  25.6 0.7 pad_maximum_fusion.1
  26.4 1.0 reshape.18
  27.3 0.2 copy.12
  27.5 0.2 reshape.19
  27.7 5.3 %collective-permute-start.10 = (bf16[64,384]{1,0:T(8,128)(2,1)S(1)}, bf16[64,384]{1,0:T(8,128)(2,1)S(1)}, u32[]{:S(2)}, u32[]{:S(2)}) collective-permute-start(bf16[64,384]{1,0:T(8,128)(2,1)S(1)} %get-tuple-element.16), channel_id=1, source_target_pairs={{0,128},{4,132},{128,0},{132,4},{1,129},{5,133},{129,1},{133,5},{2... | collective-permute-start | bytes 147464 | tf_op jit(solution)/shard_map/ppermute | solution.py:312
  33.0 11.7 %collective-permute-start.11 = (bf16[64,384]{1,0:T(8,128)(2,1)S(1)}, bf16[64,384]{1,0:T(8,128)(2,1)S(1)}, u32[]{:S(2)}, u32[]{:S(2)}) collective-permute-start(bf16[64,384]{1,0:T(8,128)(2,1)S(1)} %get-tuple-element.15), channel_id=1, source_target_pairs={{0,132},{4,128},{128,4},{132,0},{1,133},{5,129},{129,5},{133,1},{2... | collective-permute-start | bytes 147464 | tf_op jit(solution)/shard_map/ppermute | solution.py:312
  44.7 0.3 collective-permute-start.1
  45.0 3.6 %collective-permute-done.11 = bf16[64,384]{1,0:T(8,128)(2,1)S(1)} collective-permute-done((bf16[64,384]{1,0:T(8,128)(2,1)S(1)}, bf16[64,384]{1,0:T(8,128)(2,1)S(1)}, u32[]{:S(2)}, u32[]{:S(2)}) %collective-permute-start.11) | collective-permute-done | bytes 49184 | tf_op jit(solution)/shard_map/ppermute | solution.py:312
  48.7 0.1 collective-permute-start.12
  48.8 2.7 %collective-permute-start.13 = (bf16[128,384]{1,0:T(8,128)(2,1)S(1)}, bf16[128,384]{1,0:T(8,128)(2,1)S(1)}, u32[]{:S(2)}, u32[]{:S(2)}) collective-permute-start(bf16[128,384]{1,0:T(8,128)(2,1)S(1)} %get-tuple-element.18), channel_id=1, source_target_pairs={{0,96},{32,0},{64,32},{96,64},{1,97},{33,1},{65,33},{97,65},{2,98}... | collective-permute-start | bytes 294920 | tf_op jit(solution)/shard_map/ppermute | solution.py:30
  51.4 0.1 collective-permute-start.2
  51.5 2.7 %collective-permute-start.3 = (bf16[128,384]{1,0:T(8,128)(2,1)S(1)}, bf16[128,384]{1,0:T(8,128)(2,1)S(1)}, u32[]{:S(2)}, u32[]{:S(2)}) collective-permute-start(bf16[128,384]{1,0:T(8,128)(2,1)S(1)} %pad_maximum_fusion.2), channel_id=1, source_target_pairs={{0,24},{8,0},{16,8},{24,16},{1,25},{9,1},{17,9},{25,17},{2,26},{10... | collective-permute-start | bytes 294920 | tf_op jit(solution)/shard_map/ppermute | solution.py:30
  54.2 0.1 collective-permute-start.14
  54.3 2.7 %collective-permute-start.15 = (bf16[64,384]{1,0:T(8,128)(2,1)S(1)}, bf16[64,384]{1,0:T(8,128)(2,1)S(1)}, u32[]{:S(2)}, u32[]{:S(2)}) collective-permute-start(bf16[64,384]{1,0:T(8,128)(2,1)S(1)} %slice.41), channel_id=1, source_target_pairs={{0,96},{32,0},{64,32},{96,64},{1,97},{33,1},{65,33},{97,65},{2,98}... | collective-permute-start | bytes 147464 | tf_op jit(solution)/shard_map/ppermute | solution.py:30
  57.1 0.1 collective-permute-start.4
  57.2 2.7 %collective-permute-start.5 = (bf16[64,384]{1,0:T(8,128)(2,1)S(1)}, bf16[64,384]{1,0:T(8,128)(2,1)S(1)}, u32[]{:S(2)}, u32[]{:S(2)}) collective-permute-start(bf16[64,384]{1,0:T(8,128)(2,1)S(1)} %slice.37), channel_id=1, source_target_pairs={{0,24},{8,0},{16,8},{24,16},{1,25},{9,1},{17,9},{25,17},{2,26},{10... | collective-permute-start | bytes 147464 | tf_op jit(solution)/shard_map/ppermute | solution.py:30
  60.1 0.1 collective-permute-start.16
  60.2 2.7 %collective-permute-start.17 = (bf16[512,384]{1,0:T(8,128)(2,1)S(1)}, bf16[512,384]{1,0:T(8,128)(2,1)S(1)}, u32[]{:S(2)}, u32[]{:S(2)}) collective-permute-start(bf16[512,384]{1,0:T(8,128)(2,1)S(1)} %constant_dynamic-update-slice_fusion.8.b0), channel_id=1, source_target_pairs={{0,24},{8,0},{16,8},{24,16},{1,25},{9,1},{17,9},{25,17},{2,26},{10... | collective-permute-start | bytes 1179656 | tf_op jit(solution)/shard_map/ppermute | solution.py:30
  62.9 0.1 collective-permute-start.6
  63.0 2.7 %collective-permute-start.7 = (bf16[512,384]{1,0:T(8,128)(2,1)S(1)}, bf16[512,384]{1,0:T(8,128)(2,1)S(1)}, u32[]{:S(2)}, u32[]{:S(2)}) collective-permute-start(bf16[512,384]{1,0:T(8,128)(2,1)S(1)} %constant_dynamic-update-slice_fusion.a0), channel_id=1, source_target_pairs={{0,96},{32,0},{64,32},{96,64},{1,97},{33,1},{65,33},{97,65},{2,98}... | collective-permute-start | bytes 1179656 | tf_op jit(solution)/shard_map/ppermute | solution.py:30
  65.7 0.8 dynamic-slice_bitcast_fusion.6.skip
  66.4 1.6 %collective-permute-done.16.b1 = bf16[512,384]{1,0:T(8,128)(2,1)S(1)} collective-permute-done((bf16[512,384]{1,0:T(8,128)(2,1)S(1)}, bf16[512,384]{1,0:T(8,128)(2,1)S(1)}, u32[]{:S(2)}, u32[]{:S(2)}) %collective-permute-start.16) | collective-permute-done | bytes 393248 | tf_op jit(solution)/shard_map/ppermute | solution.py:30
  68.0 0.1 collective-permute-start.18
  68.2 2.7 %collective-permute-start.19 = (bf16[256,384]{1,0:T(8,128)(2,1)S(1)}, bf16[256,384]{1,0:T(8,128)(2,1)S(1)}, u32[]{:S(2)}, u32[]{:S(2)}) collective-permute-start(bf16[256,384]{1,0:T(8,128)(2,1)S(1)} %slice.43), channel_id=1, source_target_pairs={{0,24},{8,0},{16,8},{24,16},{1,25},{9,1},{17,9},{25,17},{2,26},{10... | collective-permute-start | bytes 589832 | tf_op jit(solution)/shard_map/ppermute | solution.py:30
  70.9 0.1 collective-permute-start.8
  71.0 2.8 %collective-permute-start.9 = (bf16[256,384]{1,0:T(8,128)(2,1)S(1)}, bf16[256,384]{1,0:T(8,128)(2,1)S(1)}, u32[]{:S(2)}, u32[]{:S(2)}) collective-permute-start(bf16[256,384]{1,0:T(8,128)(2,1)S(1)} %slice.39), channel_id=1, source_target_pairs={{0,96},{32,0},{64,32},{96,64},{1,97},{33,1},{65,33},{97,65},{2,98}... | collective-permute-start | bytes 589832 | tf_op jit(solution)/shard_map/ppermute | solution.py:30
  73.9 0.1 pad_add_fusion.pos
  74.0 0.7 dynamic-slice_bitcast_fusion.4
  74.7 1.6 %collective-permute-done.18.b3 = bf16[256,384]{1,0:T(8,128)(2,1)S(1)} collective-permute-done((bf16[256,384]{1,0:T(8,128)(2,1)S(1)}, bf16[256,384]{1,0:T(8,128)(2,1)S(1)}, u32[]{:S(2)}, u32[]{:S(2)}) %collective-permute-start.18) | collective-permute-done | bytes 196640 | tf_op jit(solution)/shard_map/ppermute | solution.py:30
  76.2 2.6 %collective-permute-done.8.a3 = bf16[256,384]{1,0:T(8,128)(2,1)S(1)} collective-permute-done((bf16[256,384]{1,0:T(8,128)(2,1)S(1)}, bf16[256,384]{1,0:T(8,128)(2,1)S(1)}, u32[]{:S(2)}, u32[]{:S(2)}) %collective-permute-start.8) | collective-permute-done | bytes 196640 | tf_op jit(solution)/shard_map/ppermute | solution.py:30
  78.8 2.4 %copy-done.1 = bf16[2304,1024]{1,0:T(8,128)(2,1)S(1)} copy-done((bf16[2304,1024]{1,0:T(8,128)(2,1)S(1)}, bf16[2304,1024]{1,0:T(8,128)(2,1)}, u32[]{:S(2)}) %copy-start.1) | copy-done | bytes 4718616
  81.3 10.0 %shard_map.73 = (f32[512,128]{1,0:T(8,128)S(1)}, f32[512,128]{1,0:T(8,128)S(1)}, f32[128,128]{1,0:T(8,128)S(1)}, f32[16,128]{1,0:T(8,128)S(1)}) custom-call(s32[4]{0:T(128)S(1)} %pad_add_fusion.pos, bf16[16,144,1024]{2,1,0:T(8,128)(2,1)S(1)} %bitcast.30, bf16[512,384]{1,0:T(8,128)(2,1)S(1)} %constant_dynamic-update-slice_fusion.a0, ...), custom_call_target="tpu_custom_call" | custom-call | flops 1711276032 | bytes 6000000 | tf_op jit(solution)/shard_map/pallas_call | solution.py:160
  91.3 11.8 %all_to_all.10 = f32[16,16,128]{2,1,0:T(8,128)S(1)} all-to-all(f32[16,16,128]{2,1,0:T(8,128)S(1)} %broadcast_in_dim.17), channel_id=1, replica_groups=mesh['zh'=2,'y'=4,'x'=4,'c'=2,'zl'=4] {'y','x'}, dimensions={0} | all-to-all | bytes 262144 | tf_op jit(solution)/shard_map/all_to_all | solution.py:336
  103.1 1.1 shard_map.74
  104.1 0.9 broadcast_in_dim.19
  105.0 19.2 %all-to-all-start.1 = ((bf16[16,128,128]{2,1,0:T(8,128)(2,1)}), bf16[16,128,128]{2,1,0:T(8,128)(2,1)S(1)}, u32[]{:S(2)}, u32[]{:S(2)}) async-start(bf16[16,128,128]{2,1,0:T(8,128)(2,1)} %bitcast.15), calls=%async_computation.1 | async-start | bytes 1048576 | tf_op jit(solution)/shard_map/all_to_all | solution.py:345
  124.3 14.5 %all-to-all-done.1.gates = bf16[16,128,128]{2,1,0:T(8,128)(2,1)S(1)} async-done(((bf16[16,128,128]{2,1,0:T(8,128)(2,1)}), bf16[16,128,128]{2,1,0:T(8,128)(2,1)S(1)}, u32[]{:S(2)}, u32[]{:S(2)}) %all-to-all-start.1) | async-done | bytes 524320 | tf_op jit(solution)/shard_map/all_to_all | solution.py:345
  138.7 2.2 %copy-done.2 = bf16[64,64,512]{2,1,0:T(8,128)(2,1)S(1)} copy-done((bf16[64,64,512]{2,1,0:T(8,128)(2,1)S(1)}, bf16[64,64,512]{2,1,0:T(8,128)(2,1)}, u32[]{:S(2)}) %copy-start.2) | copy-done | bytes 4194328
  140.9 3.0 %shard_map.75 = bf16[128,1024]{1,0:T(8,128)(2,1)} custom-call(s32[4]{0:T(128)S(1)} %pad_add_fusion.pos, bf16[16,128,128]{2,1,0:T(8,128)(2,1)S(1)} %all-to-all-done.1.gates, bf16[32,2,64,512]{3,2,1,0:T(8,128)(2,1)S(1)} %bitcast.31), custom_call_target="tpu_custom_call" | custom-call | flops 536870912 | bytes 5000000 | tf_op jit(solution)/shard_map/pallas_call | solution.py:271
  (49 shorter events, 0.4 us)
Async XLA Ops:
  6.5 59.1 %copy-start = (f32[3,3,512]{2,1,0:T(4,128)S(1)}, f32[3,3,512]{2,1,0:T(4,128)}, u32[]{:S(2)}) copy-start(f32[3,3,512]{2,1,0:T(4,128)} %param.9) | copy-start | bytes 55300
  6.5 72.3 %all-gather.5.cloned.1.call-start = ((), (), s32[]{:S(2)}) async-start(), calls=%async_computation.2 | async-start | bytes 5013504 | tf_op jit(solution)/shard_map/all_gather | solution.py:304
  7.3 5.5 %collective-permute-start = (bf16[16,1024]{1,0:T(8,128)(2,1)S(1)}, bf16[16,1024]{1,0:T(8,128)(2,1)S(1)}, u32[]{:S(2)}, u32[]{:S(2)}) collective-permute-start(bf16[16,1024]{1,0:T(8,128)(2,1)S(1)} %slice.27), channel_id=1, source_target_pairs={{0,4},{4,8},{8,12},{12,16},{16,20},{20,24},{24,28},{28,32},{32,36}... | collective-permute-start | bytes 98312 | tf_op jit(solution)/shard_map/ppermute | solution.py:302
  14.5 109.7 %all-gather.7.cloned.1.call-start = ((), (), s32[]{:S(2)}) async-start(), calls=%async_computation.3 | async-start | bytes 4325376 | tf_op jit(solution)/shard_map/all_gather | solution.py:321
  14.6 8.9 %collective-permute-start.20 = (bf16[64,512]{1,0:T(8,128)(2,1)}, bf16[64,512]{1,0:T(8,128)(2,1)S(1)}, u32[]{:S(2)}, u32[]{:S(2)}) collective-permute-start(bf16[64,512]{1,0:T(8,128)(2,1)} %bitcast.37), channel_id=1, source_target_pairs={{0,0},{1,64},{2,128},{3,192},{4,4},{5,68},{6,132},{7,196},{8,8},{9... | collective-permute-start | bytes 196616 | tf_op jit(solution)/shard_map/ppermute | solution.py:322
  16.1 9.6 %collective-permute-start.21 = (bf16[64,512]{1,0:T(8,128)(2,1)}, bf16[64,512]{1,0:T(8,128)(2,1)S(1)}, u32[]{:S(2)}, u32[]{:S(2)}) collective-permute-start(bf16[64,512]{1,0:T(8,128)(2,1)} %bitcast.38), channel_id=1, source_target_pairs={{0,128},{1,192},{2,0},{3,64},{4,132},{5,196},{6,4},{7,68},{8,136},... | collective-permute-start | bytes 196616 | tf_op jit(solution)/shard_map/ppermute | solution.py:322
  27.7 17.3 %collective-permute-start.10 = (bf16[64,384]{1,0:T(8,128)(2,1)S(1)}, bf16[64,384]{1,0:T(8,128)(2,1)S(1)}, u32[]{:S(2)}, u32[]{:S(2)}) collective-permute-start(bf16[64,384]{1,0:T(8,128)(2,1)S(1)} %get-tuple-element.16), channel_id=1, source_target_pairs={{0,128},{4,132},{128,0},{132,4},{1,129},{5,133},{129,1},{133,5},{2... | collective-permute-start | bytes 147464 | tf_op jit(solution)/shard_map/ppermute | solution.py:312
  33.0 15.6 %collective-permute-start.11 = (bf16[64,384]{1,0:T(8,128)(2,1)S(1)}, bf16[64,384]{1,0:T(8,128)(2,1)S(1)}, u32[]{:S(2)}, u32[]{:S(2)}) collective-permute-start(bf16[64,384]{1,0:T(8,128)(2,1)S(1)} %get-tuple-element.15), channel_id=1, source_target_pairs={{0,132},{4,128},{128,4},{132,0},{1,133},{5,129},{129,5},{133,1},{2... | collective-permute-start | bytes 147464 | tf_op jit(solution)/shard_map/ppermute | solution.py:312
  44.7 6.7 %collective-permute-start.1 = (bf16[64,384]{1,0:T(8,128)(2,1)S(1)}, bf16[64,384]{1,0:T(8,128)(2,1)S(1)}, u32[]{:S(2)}, u32[]{:S(2)}) collective-permute-start(bf16[64,384]{1,0:T(8,128)(2,1)S(1)} %get-tuple-element.17), channel_id=1, source_target_pairs={{0,4},{4,0},{128,132},{132,128},{1,5},{5,1},{129,133},{133,129},{2... | collective-permute-start | bytes 147464 | tf_op jit(solution)/shard_map/ppermute | solution.py:312
  48.7 5.5 %collective-permute-start.12 = (bf16[128,384]{1,0:T(8,128)(2,1)S(1)}, bf16[128,384]{1,0:T(8,128)(2,1)S(1)}, u32[]{:S(2)}, u32[]{:S(2)}) collective-permute-start(bf16[128,384]{1,0:T(8,128)(2,1)S(1)} %get-tuple-element.18), channel_id=1, source_target_pairs={{0,32},{32,64},{64,96},{96,0},{1,33},{33,65},{65,97},{97,1},{2,34}... | collective-permute-start | bytes 294920 | tf_op jit(solution)/shard_map/ppermute | solution.py:30
  48.8 5.6 %collective-permute-start.13 = (bf16[128,384]{1,0:T(8,128)(2,1)S(1)}, bf16[128,384]{1,0:T(8,128)(2,1)S(1)}, u32[]{:S(2)}, u32[]{:S(2)}) collective-permute-start(bf16[128,384]{1,0:T(8,128)(2,1)S(1)} %get-tuple-element.18), channel_id=1, source_target_pairs={{0,96},{32,0},{64,32},{96,64},{1,97},{33,1},{65,33},{97,65},{2,98}... | collective-permute-start | bytes 294920 | tf_op jit(solution)/shard_map/ppermute | solution.py:30
  51.4 5.6 %collective-permute-start.2 = (bf16[128,384]{1,0:T(8,128)(2,1)S(1)}, bf16[128,384]{1,0:T(8,128)(2,1)S(1)}, u32[]{:S(2)}, u32[]{:S(2)}) collective-permute-start(bf16[128,384]{1,0:T(8,128)(2,1)S(1)} %pad_maximum_fusion.2), channel_id=1, source_target_pairs={{0,8},{8,16},{16,24},{24,0},{1,9},{9,17},{17,25},{25,1},{2,10},{10... | collective-permute-start | bytes 294920 | tf_op jit(solution)/shard_map/ppermute | solution.py:30
  51.5 5.7 %collective-permute-start.3 = (bf16[128,384]{1,0:T(8,128)(2,1)S(1)}, bf16[128,384]{1,0:T(8,128)(2,1)S(1)}, u32[]{:S(2)}, u32[]{:S(2)}) collective-permute-start(bf16[128,384]{1,0:T(8,128)(2,1)S(1)} %pad_maximum_fusion.2), channel_id=1, source_target_pairs={{0,24},{8,0},{16,8},{24,16},{1,25},{9,1},{17,9},{25,17},{2,26},{10... | collective-permute-start | bytes 294920 | tf_op jit(solution)/shard_map/ppermute | solution.py:30
  54.2 5.8 %collective-permute-start.14 = (bf16[64,384]{1,0:T(8,128)(2,1)S(1)}, bf16[64,384]{1,0:T(8,128)(2,1)S(1)}, u32[]{:S(2)}, u32[]{:S(2)}) collective-permute-start(bf16[64,384]{1,0:T(8,128)(2,1)S(1)} %slice.40), channel_id=1, source_target_pairs={{0,32},{32,64},{64,96},{96,0},{1,33},{33,65},{65,97},{97,1},{2,34}... | collective-permute-start | bytes 147464 | tf_op jit(solution)/shard_map/ppermute | solution.py:30
  54.3 5.7 %collective-permute-start.15 = (bf16[64,384]{1,0:T(8,128)(2,1)S(1)}, bf16[64,384]{1,0:T(8,128)(2,1)S(1)}, u32[]{:S(2)}, u32[]{:S(2)}) collective-permute-start(bf16[64,384]{1,0:T(8,128)(2,1)S(1)} %slice.41), channel_id=1, source_target_pairs={{0,96},{32,0},{64,32},{96,64},{1,97},{33,1},{65,33},{97,65},{2,98}... | collective-permute-start | bytes 147464 | tf_op jit(solution)/shard_map/ppermute | solution.py:30
  57.1 5.8 %collective-permute-start.4 = (bf16[64,384]{1,0:T(8,128)(2,1)S(1)}, bf16[64,384]{1,0:T(8,128)(2,1)S(1)}, u32[]{:S(2)}, u32[]{:S(2)}) collective-permute-start(bf16[64,384]{1,0:T(8,128)(2,1)S(1)} %slice.36), channel_id=1, source_target_pairs={{0,8},{8,16},{16,24},{24,0},{1,9},{9,17},{17,25},{25,1},{2,10},{10... | collective-permute-start | bytes 147464 | tf_op jit(solution)/shard_map/ppermute | solution.py:30
  57.2 5.7 %collective-permute-start.5 = (bf16[64,384]{1,0:T(8,128)(2,1)S(1)}, bf16[64,384]{1,0:T(8,128)(2,1)S(1)}, u32[]{:S(2)}, u32[]{:S(2)}) collective-permute-start(bf16[64,384]{1,0:T(8,128)(2,1)S(1)} %slice.37), channel_id=1, source_target_pairs={{0,24},{8,0},{16,8},{24,16},{1,25},{9,1},{17,9},{25,17},{2,26},{10... | collective-permute-start | bytes 147464 | tf_op jit(solution)/shard_map/ppermute | solution.py:30
  60.1 7.9 %collective-permute-start.16 = (bf16[512,384]{1,0:T(8,128)(2,1)S(1)}, bf16[512,384]{1,0:T(8,128)(2,1)S(1)}, u32[]{:S(2)}, u32[]{:S(2)}) collective-permute-start(bf16[512,384]{1,0:T(8,128)(2,1)S(1)} %constant_dynamic-update-slice_fusion.8.b0), channel_id=1, source_target_pairs={{0,8},{8,16},{16,24},{24,0},{1,9},{9,17},{17,25},{25,1},{2,10},{10... | collective-permute-start | bytes 1179656 | tf_op jit(solution)/shard_map/ppermute | solution.py:30
  60.2 7.9 %collective-permute-start.17 = (bf16[512,384]{1,0:T(8,128)(2,1)S(1)}, bf16[512,384]{1,0:T(8,128)(2,1)S(1)}, u32[]{:S(2)}, u32[]{:S(2)}) collective-permute-start(bf16[512,384]{1,0:T(8,128)(2,1)S(1)} %constant_dynamic-update-slice_fusion.8.b0), channel_id=1, source_target_pairs={{0,24},{8,0},{16,8},{24,16},{1,25},{9,1},{17,9},{25,17},{2,26},{10... | collective-permute-start | bytes 1179656 | tf_op jit(solution)/shard_map/ppermute | solution.py:30
  62.9 8.0 %collective-permute-start.6 = (bf16[512,384]{1,0:T(8,128)(2,1)S(1)}, bf16[512,384]{1,0:T(8,128)(2,1)S(1)}, u32[]{:S(2)}, u32[]{:S(2)}) collective-permute-start(bf16[512,384]{1,0:T(8,128)(2,1)S(1)} %constant_dynamic-update-slice_fusion.a0), channel_id=1, source_target_pairs={{0,32},{32,64},{64,96},{96,0},{1,33},{33,65},{65,97},{97,1},{2,34}... | collective-permute-start | bytes 1179656 | tf_op jit(solution)/shard_map/ppermute | solution.py:30
  63.0 8.0 %collective-permute-start.7 = (bf16[512,384]{1,0:T(8,128)(2,1)S(1)}, bf16[512,384]{1,0:T(8,128)(2,1)S(1)}, u32[]{:S(2)}, u32[]{:S(2)}) collective-permute-start(bf16[512,384]{1,0:T(8,128)(2,1)S(1)} %constant_dynamic-update-slice_fusion.a0), channel_id=1, source_target_pairs={{0,96},{32,0},{64,32},{96,64},{1,97},{33,1},{65,33},{97,65},{2,98}... | collective-permute-start | bytes 1179656 | tf_op jit(solution)/shard_map/ppermute | solution.py:30
  68.0 8.2 %collective-permute-start.18 = (bf16[256,384]{1,0:T(8,128)(2,1)S(1)}, bf16[256,384]{1,0:T(8,128)(2,1)S(1)}, u32[]{:S(2)}, u32[]{:S(2)}) collective-permute-start(bf16[256,384]{1,0:T(8,128)(2,1)S(1)} %slice.42), channel_id=1, source_target_pairs={{0,8},{8,16},{16,24},{24,0},{1,9},{9,17},{17,25},{25,1},{2,10},{10... | collective-permute-start | bytes 589832 | tf_op jit(solution)/shard_map/ppermute | solution.py:30
  68.2 8.1 %collective-permute-start.19 = (bf16[256,384]{1,0:T(8,128)(2,1)S(1)}, bf16[256,384]{1,0:T(8,128)(2,1)S(1)}, u32[]{:S(2)}, u32[]{:S(2)}) collective-permute-start(bf16[256,384]{1,0:T(8,128)(2,1)S(1)} %slice.43), channel_id=1, source_target_pairs={{0,24},{8,0},{16,8},{24,16},{1,25},{9,1},{17,9},{25,17},{2,26},{10... | collective-permute-start | bytes 589832 | tf_op jit(solution)/shard_map/ppermute | solution.py:30
  70.9 7.9 %collective-permute-start.8 = (bf16[256,384]{1,0:T(8,128)(2,1)S(1)}, bf16[256,384]{1,0:T(8,128)(2,1)S(1)}, u32[]{:S(2)}, u32[]{:S(2)}) collective-permute-start(bf16[256,384]{1,0:T(8,128)(2,1)S(1)} %slice.38), channel_id=1, source_target_pairs={{0,32},{32,64},{64,96},{96,0},{1,33},{33,65},{65,97},{97,1},{2,34}... | collective-permute-start | bytes 589832 | tf_op jit(solution)/shard_map/ppermute | solution.py:30
  71.0 7.8 %collective-permute-start.9 = (bf16[256,384]{1,0:T(8,128)(2,1)S(1)}, bf16[256,384]{1,0:T(8,128)(2,1)S(1)}, u32[]{:S(2)}, u32[]{:S(2)}) collective-permute-start(bf16[256,384]{1,0:T(8,128)(2,1)S(1)} %slice.39), channel_id=1, source_target_pairs={{0,96},{32,0},{64,32},{96,64},{1,97},{33,1},{65,33},{97,65},{2,98}... | collective-permute-start | bytes 589832 | tf_op jit(solution)/shard_map/ppermute | solution.py:30
  78.8 2.4 %copy-start.1 = (bf16[2304,1024]{1,0:T(8,128)(2,1)S(1)}, bf16[2304,1024]{1,0:T(8,128)(2,1)}, u32[]{:S(2)}) copy-start(bf16[2304,1024]{1,0:T(8,128)(2,1)} %all-gather.5.cloned.1.call-done) | copy-start | bytes 14155780
  105.0 33.7 %all-to-all-start.1 = ((bf16[16,128,128]{2,1,0:T(8,128)(2,1)}), bf16[16,128,128]{2,1,0:T(8,128)(2,1)S(1)}, u32[]{:S(2)}, u32[]{:S(2)}) async-start(bf16[16,128,128]{2,1,0:T(8,128)(2,1)} %bitcast.15), calls=%async_computation.1 | async-start | bytes 1048576 | tf_op jit(solution)/shard_map/all_to_all | solution.py:345
  138.7 2.2 %copy-start.2 = (bf16[64,64,512]{2,1,0:T(8,128)(2,1)S(1)}, bf16[64,64,512]{2,1,0:T(8,128)(2,1)}, u32[]{:S(2)}) copy-start(bf16[64,64,512]{2,1,0:T(8,128)(2,1)} %all-gather.7.cloned.1.call-done) | copy-start | bytes 12582916
Sparse Core Ops, SparseCore 0:
  14.6 52.7 all-gather.4
  70.0 50.2 all-gather.6

commit v2 on v1

v2 whole, which is shorter than its diff:
```python
import functools

import jax
import jax.numpy as jnp
import numpy as np
from jax import lax
from jax.experimental import pallas as pl
from jax.experimental.pallas import tpu as pltpu
from jax.sharding import Mesh, PartitionSpec as P

AXES = ("zh", "y", "x", "c", "zl")
SIZES = (2, 4, 4, 2, 4)
SEQ = ("zh", "y", "x", "c")
CHIPS = 16
BLOCK = 256
HALF = 128
LANES = 128
WIDE = 3 * LANES
MODES = 8
SUB = 8
STEPS = BLOCK // SUB
EDGE = 2 * MODES
EDGE_ROWS = 40
GROUP = 64
F32 = jnp.float32
BF16 = jnp.bfloat16


def crossed(block, phase, distance):
    route = []
    for y, x, c in np.ndindex(4, 4, 2):
        target = (y, (x + distance) % 4, c) if c == phase else ((y + distance) % 4, x, c)
        route.append((int(np.ravel_multi_index((y, x, c), (4, 4, 2))), int(np.ravel_multi_index(target, (4, 4, 2)))))
    return lax.ppermute(block, ("y", "x", "c"), route)


def ring(block, phase):
    half = block.shape[0] // 2
    low = crossed(block, phase, 1)
    high = crossed(block, phase, -1)
    far_low = crossed(low[:half], phase, 1)
    far_high = crossed(high[half:], phase, -1)
    return [block, low, high, far_low, far_high]


RING_ORDER = (0, -1, 1, 2)


def front_kernel(
    pos,
    slabs,
    w0, w1, w2, w3, w4,
    taps,
    rates,
    residues,
    skip,
    y_out,
    gate_out,
    sub_out,
    edge_out,
    proj,
    gated,
):
    own_y, own_x, own_zh, own_c = pos[0], pos[1], pos[2], pos[3]

    def features(outer, inner, half):
        first = RING_ORDER[outer] + 4
        second = RING_ORDER[inner] + 4
        at_y = lax.rem(own_y + jnp.where(own_c == 0, first, second), 4)
        at_x = lax.rem(own_x + jnp.where(own_c == 0, second, first), 4)
        at_zh = own_zh if half == 0 else 1 - own_zh
        zl = at_zh * 2 + at_y // 2
        lane = pl.multiple_of((lax.rem(at_y, 2) * 4 + at_x) * 128, 128)
        return slabs[:, pl.ds(zl, 1), :, :, pl.ds(lane, 128)].reshape(2 * BLOCK, 128)

    total = None
    place = 0
    for array in (w0, w1, w2, w3, w4):
        count = array.shape[0] // 256
        parts = [
            features((place + k) // 4, (place + k) % 4, half)
            for k in range(count)
            for half in range(2)
        ]
        part = jnp.dot(jnp.concatenate(parts, axis=1), array[...], preferred_element_type=F32)
        total = part if total is None else total + part
        place += count
    proj[:, 0:8, :] = jnp.zeros((2, 8, WIDE), F32)
    proj[:, 8:, :] = total.astype(BF16).astype(F32).reshape(2, BLOCK, WIDE)
    gain = skip[...]
    for zh in range(2):
        streams = []
        edges = []
        for s in range(3):
            lanes = slice(s * LANES, (s + 1) * LANES)
            tap = [taps[3 * s + m : 3 * s + m + 1, :] for m in range(3)]
            total = jnp.zeros((BLOCK, LANES), F32)
            for m in range(3):
                total = total + tap[m] * proj[zh, 8 - m : 8 - m + BLOCK, lanes]
            streams.append(total)
            before = proj[zh, BLOCK + 6 : BLOCK + 7, lanes]
            last = proj[zh, BLOCK + 7 : BLOCK + 8, lanes]
            edges.append([tap[1] * last + tap[2] * before, tap[2] * last])
        gated[zh * BLOCK : (zh + 1) * BLOCK, :] = streams[0] * streams[2]
        gate_out[zh * BLOCK : (zh + 1) * BLOCK, :] = streams[1]
        rows = [streams[0][0:1], streams[0][1:2], streams[2][0:1], streams[2][1:2]]
        rows = rows + edges[0] + edges[2] + edges[1]
        for chip in range(CHIPS):
            for k, row in enumerate(rows):
                edge_out[chip, EDGE + zh * 10 + k : EDGE + zh * 10 + k + 1, :] = row
    rate = rates[...]
    decay = jnp.exp(-rate)
    weight = residues[...]
    decays = [jnp.broadcast_to(decay[m : m + 1], (SUB, LANES)) for m in range(MODES)]
    weights = [jnp.broadcast_to(weight[m : m + 1], (SUB, LANES)) for m in range(MODES)]
    gain = jnp.broadcast_to(gain, (SUB, LANES))
    long_decay = jnp.exp(-rate * float(STEPS))
    for zh in range(2):
        state = [jnp.zeros((SUB, LANES), F32) for _ in range(MODES)]
        for i in range(STEPS):
            rows = pl.ds(zh * BLOCK + i, SUB, stride=STEPS)
            entry = gated[rows, :]
            state = [decays[m] * state[m] + entry for m in range(MODES)]
            terms = [weights[m] * state[m] for m in range(MODES)]
            while len(terms) > 1:
                terms = [terms[k] + terms[k + 1] for k in range(0, len(terms), 2)]
            y_out[rows, :] = terms[0] + gain * entry
        for m in range(MODES):
            sub_out[pl.ds(zh * SUB * MODES + m, SUB, stride=MODES), :] = state[m]
        total = jnp.zeros((MODES, LANES), F32)
        for sub in range(SUB):
            start = zh * SUB * MODES + sub * MODES
            total = long_decay * total + sub_out[start : start + MODES, :]
        for chip in range(CHIPS):
            edge_out[chip, zh * MODES : (zh + 1) * MODES, :] = total


def front(pos, slabs, weights, taps, rates, residues, skip):
    vmem = pl.BlockSpec(memory_space=pltpu.VMEM)
    smem = pl.BlockSpec(memory_space=pltpu.SMEM)
    return pl.pallas_call(
        front_kernel,
        out_shape=(
            jax.ShapeDtypeStruct((2 * BLOCK, LANES), F32),
            jax.ShapeDtypeStruct((2 * BLOCK, LANES), F32),
            jax.ShapeDtypeStruct((2 * SUB * MODES, LANES), F32),
            jax.ShapeDtypeStruct((CHIPS, EDGE_ROWS, LANES), F32),
        ),
        in_specs=[smem] + [vmem] * 10,
        out_specs=(vmem,) * 4,
        scratch_shapes=[
            pltpu.VMEM((2, 8 + BLOCK, WIDE), F32),
            pltpu.VMEM((2 * BLOCK, LANES), F32),
        ],
        compiler_params=pltpu.CompilerParams(vmem_limit_bytes=40 * 1024 * 1024),
        cost_estimate=pl.CostEstimate(
            flops=4 * BLOCK * 4096 * WIDE, bytes_accessed=6_000_000, transcendentals=0
        ),
    )(pos, slabs, *weights, taps, rates, residues, skip)


def back_kernel(
    pos, edges, sub_states, y_in, gate_in, rates, residues, skip, out, carried, mixed, head
):
    block = pos[0] * 4 + pos[1]
    rate = rates[...]
    weight = residues[...]
    decay = jnp.exp(-rate)
    long_decay = jnp.exp(-rate * float(STEPS))
    last = [jnp.exp(-rate * float(BLOCK - 1)), jnp.exp(-rate * float(BLOCK - 2))]

    def rows(chip, zh, start, count):
        return edges[chip, EDGE + 10 * zh + start : EDGE + 10 * zh + start + count, :]

    def late(chip, zh, tails):
        first, second = rows(chip, zh, 0, 2), rows(chip, zh, 2, 2)
        return (first + tails[0:2]) * (second + tails[2:4]) - first * second

    carry = [jnp.zeros((MODES, LANES), F32) for _ in range(2)]
    for other in range(CHIPS):
        distance = block - 1 - other
        span = jnp.maximum(distance, 0).astype(F32) * float(BLOCK)
        near = jnp.where(distance >= 0, jnp.exp(-rate * span), 0.0)
        far = jnp.exp(-rate * ((distance + CHIPS).astype(F32) * float(BLOCK)))
        states = []
        for zh in range(2):
            state = edges[other, zh * MODES : (zh + 1) * MODES, :]
            if other > 0 or zh == 1:
                ahead = (other - 1, zh) if other > 0 else (CHIPS - 1, 0)
                added = late(other, zh, rows(*ahead, 4, 4))
                state = state + last[0] * added[0:1] + last[1] * added[1:2]
            states.append(state)
        carry[0] = carry[0] + near * states[0]
        carry[1] = carry[1] + near * states[1] + far * states[0]
    decays = [jnp.broadcast_to(decay[m : m + 1], (SUB, LANES)) for m in range(MODES)]
    growth = jnp.exp(rate)
    gain = skip[...]
    ahead = jnp.maximum(block - 1, 0)
    for zh in range(2):
        tails = rows(ahead, zh, 4, 6)
        if zh == 0:
            tails = jnp.where(block == 0, 0.0, tails)
        else:
            tails = jnp.where(block == 0, rows(CHIPS - 1, 0, 4, 6), tails)
        added = late(block, zh, tails)
        state = carry[zh] + growth * (added[0:1] + growth * added[1:2])
        for sub in range(SUB):
            start = zh * SUB * MODES + sub * MODES
            carried[start : start + MODES, :] = weight * state
            state = long_decay * state + sub_states[start : start + MODES, :]
        terms = [
            carried[pl.ds(zh * SUB * MODES + m, SUB, stride=MODES), :] for m in range(MODES)
        ]
        for i in range(STEPS):
            at = pl.ds(zh * BLOCK + i, SUB, stride=STEPS)
            terms = [decays[m] * terms[m] for m in range(MODES)]
            sums = terms
            while len(sums) > 1:
                sums = [sums[k] + sums[k + 1] for k in range(0, len(sums), 2)]
            mixed[at, :] = y_in[at, :] + sums[0]
        early = jnp.sum(weight * growth, axis=0, keepdims=True) * added[1:2]
        start = zh * BLOCK
        mixed[start : start + 1, :] = mixed[start : start + 1, :] + gain * added[0:1] - early
        mixed[start + 1 : start + 2, :] = mixed[start + 1 : start + 2, :] + gain * added[1:2]
        head[...] = gate_in[start : start + 16, :]
        head[0:2, :] = head[0:2, :] + tails[4:6]
        for c in range(2):
            at = slice(start + c * HALF, start + (c + 1) * HALF)
            gate_rows = (gate_in[at, :] * mixed[at, :]).astype(BF16)
            for zl in range(4):
                out[(2 * zh + c) * 4 + zl] = gate_rows
        first_rows = (head[...] * mixed[start : start + 16, :]).astype(BF16)
        for zl in range(4):
            out[2 * zh * 4 + zl, 0:16, :] = first_rows


def back(pos, edges, sub_states, y, gate, rates, residues, skip):
    vmem = pl.BlockSpec(memory_space=pltpu.VMEM)
    smem = pl.BlockSpec(memory_space=pltpu.SMEM)
    return pl.pallas_call(
        back_kernel,
        out_shape=jax.ShapeDtypeStruct((16, HALF, LANES), BF16),
        in_specs=[smem] + [vmem] * 7,
        out_specs=vmem,
        scratch_shapes=[
            pltpu.VMEM((2 * SUB * MODES, LANES), F32),
            pltpu.VMEM((2 * BLOCK, LANES), F32),
            pltpu.VMEM((16, LANES), F32),
        ],
        compiler_params=pltpu.CompilerParams(vmem_limit_bytes=16 * 1024 * 1024),
        cost_estimate=pl.CostEstimate(
            flops=4_000_000, bytes_accessed=800_000, transcendentals=40_000
        ),
    )(pos, edges, sub_states, y, gate, rates, residues, skip)


def out_kernel(pos, gates, weights, out):
    own_zh = pos[2]
    total = jnp.zeros((HALF, 1024), F32)
    for k in range(2):
        for half in range(2):
            zl = (own_zh if k == 0 else 1 - own_zh) * 2 + half
            parts = [gates[(2 * zh + c) * 4 + zl] for zh in range(2) for c in range(2)]
            total = total + lax.dot_general(
                jnp.concatenate(parts, axis=1),
                weights[16 * half : 16 * (half + 1), k].reshape(1024, 512),
                (((1,), (1,)), ((), ())),
                preferred_element_type=F32,
            )
    out[...] = total.astype(BF16)


def project_out(pos, gates, weights):
    vmem = pl.BlockSpec(memory_space=pltpu.VMEM)
    smem = pl.BlockSpec(memory_space=pltpu.SMEM)
    return pl.pallas_call(
        out_kernel,
        out_shape=jax.ShapeDtypeStruct((HALF, 1024), BF16),
        in_specs=[smem, vmem, vmem],
        out_specs=vmem,
        compiler_params=pltpu.CompilerParams(vmem_limit_bytes=32 * 1024 * 1024),
        cost_estimate=pl.CostEstimate(
            flops=2 * HALF * 2048 * 1024, bytes_accessed=5_000_000, transcendentals=0
        ),
    )(pos, gates, weights)


def transposed_routes():
    near, far = [], []
    for zh, y, x, c, zl in np.ndindex(*SIZES):
        source = int(np.ravel_multi_index((zh, y, x, c, zl), SIZES))
        for route, to_zh in ((near, zl // 2), (far, 1 - zl // 2)):
            target = (to_zh, (zl % 2) * 2 + y % 2, x, c, zh * 2 + y // 2)
            route.append((source, int(np.ravel_multi_index(target, SIZES))))
    return near, far


def shards(tokens, in_weight, short_weight, residues, decay_rates, skip_gain, out_weight):
    zh, y, x, c = (lax.axis_index(axis) for axis in SEQ)
    pos = jnp.stack([y, x, zh, c]).astype(jnp.int32)
    group = zh * 2 + c

    slabs = lax.all_gather(tokens, ("zh", "zl", "c"), axis=0, tiled=False)
    slabs = slabs.reshape(2, 4, 2, HALF, 1024)

    quarters = in_weight.reshape(3, GROUP, 4, LANES).transpose(2, 1, 0, 3).reshape(4, GROUP, WIDE)

    def quarter(flip):
        part = lax.dynamic_index_in_dim(quarters, group ^ flip, 0, keepdims=False)
        if flip == 0:
            return part
        return lax.ppermute(part, ("zh", "c"), [(i, i ^ flip) for i in range(4)])

    def in_order(own, other):
        first = jnp.where(c == 0, own, other)
        second = jnp.where(c == 0, other, own)
        return jnp.concatenate([first, second], axis=0)

    far = in_order(quarter(2), quarter(3))
    near = in_order(quarter(0), quarter(1))
    gathered_once = jnp.concatenate(ring(jnp.concatenate([near, far], axis=0), 0), axis=0)
    in_weights = ring(gathered_once, 1)

    moved = [lax.ppermute(out_weight.T, AXES, route) for route in transposed_routes()]
    moved[0], moved[1], in_weights[1], in_weights[2] = lax.optimization_barrier(
        (moved[0], moved[1], in_weights[1], in_weights[2])
    )
    gathered = lax.all_gather(
        jnp.stack(moved),
        ("y", "x", "c"),
        axis=0,
        tiled=False,
    )

    def own_channels(table, axis):
        return lax.dynamic_slice_in_dim(table, group * LANES, LANES, axis)

    taps = own_channels(short_weight, 2).reshape(9, LANES)
    rates = own_channels(decay_rates, 0).T
    weights = own_channels(residues, 0).T
    skip = own_channels(skip_gain, 0)[None]
    mixed, gate, sub_states, edges = front(pos, slabs, in_weights, taps, rates, weights, skip)
    edges = lax.all_to_all(edges, ("y", "x"), split_axis=0, concat_axis=0, tiled=True)
    gate_out = back(pos, edges, sub_states, mixed, gate, rates, weights, skip)
    gates = lax.all_to_all(gate_out, ("zh", "c", "zl"), split_axis=0, concat_axis=0, tiled=True)
    return project_out(pos, gates, gathered)


def solution(mesh):
    split_mesh = Mesh(mesh.devices.reshape(SIZES), AXES)
    return jax.shard_map(
        shards,
        mesh=split_mesh,
        in_specs=(
            P(SEQ, "zl"),
            P(None, SEQ, "zl"),
            P(None, None, "zl"),
            P("zl", None),
            P("zl", None),
            P("zl"),
            P("zl", SEQ),
        ),
        out_specs=P(SEQ, "zl"),
        check_vma=False,
    )
```

time: 152 us -> 125 us (0.82)
  starting transfers between devices: 72.3 us -> 27.2 us
  blocking collectives: 11.8 us -> 44.3 us
  Pallas kernels: 14.1 us -> 7.26 us
  waiting for transfers between devices: 27 us -> 22.2 us
  other arithmetic: 2.43 us -> 0.87 us
    all_to_all x1 -> x2, blocking collectives: 11.8 us -> 44.3 us  [the longest x1 24.7 us: shards(): lax.all_to_all(gate_out, ('zh', 'c', 'zl'), split_axis=0, concat_axis=0,...]
    all_to_all x1 -> x0, starting transfers between devices: 19.2 us -> none  [shards(): lax.all_to_all(sent.reshape(16, HALF, LANES), ('zh', 'c', 'zl'), split_ax...]
    ppermute x19 -> x10, starting transfers between devices: 35.8 us -> 18.2 us  [the longest x8 11.3 us: crossed(): return lax.ppermute(block, ('y', 'x', 'c'), route)]
    all_to_all x1 -> x0, waiting for transfers between devices: 14.5 us -> none  [shards(): lax.all_to_all(sent.reshape(16, HALF, LANES), ('zh', 'c', 'zl'), split_ax...]
    ppermute x3, starting transfers between devices: 17.3 us -> 8.97 us  [quarter(): return lax.ppermute(part, ('zh', 'c'), [(i, i ^ flip) for i in range(4)])]
    pallas_call x1, Pallas kernels: 9.99 us -> 3.55 us  [front(): pl.pallas_call(front_kernel, out_shape=(jax.ShapeDtypeStruct((2 * BLOCK,...]
    ppermute x3, waiting for transfers between devices: 3.6 us -> 7.22 us  [quarter(): return lax.ppermute(part, ('zh', 'c'), [(i, i ^ flip) for i in range(4)])]
    ppermute x19 -> x10, waiting for transfers between devices: 8.92 us -> 11.9 us  [the longest x8 9.21 us: crossed(): return lax.ppermute(block, ('y', 'x', 'c'), route)]
  transfers between devices with their start and end apart: 25 -> 15, of which waited for: 7 -> 9; matrix products, arithmetic and copies ran while one was open for 3% -> 4% of each run, Pallas kernels for 7% -> 4%
where the time goes in v2:
time: 125 us; the launch traced here: 124 us
  blocking collectives  44.3 us (35%)
  starting transfers between devices  27.2 us (22%)
  waiting for transfers between devices  22.2 us (18%)
  between operations  13.6 us (11%)
  local copies, waits for them, and re-layouts  8.98 us (7%)
  Pallas kernels  7.26 us (6%)
    all_to_all x1, blocking collectives, shards(): lax.all_to_all(gate_out, ('zh', 'c', 'zl'), split_axis=0, concat_axis=0,...  24.7 us
    all_to_all x1, blocking collectives, shards(): lax.all_to_all(edges, ('y', 'x'), split_axis=0, concat_axis=0, tiled=True)  19.6 us
    ppermute x8, starting transfers between devices, crossed(): return lax.ppermute(block, ('y', 'x', 'c'), route)  11.3 us
    ppermute x8, waiting for transfers between devices, crossed(): return lax.ppermute(block, ('y', 'x', 'c'), route)  9.21 us
    ppermute x3, starting transfers between devices, quarter(): return lax.ppermute(part, ('zh', 'c'), [(i, i ^ flip) for i in range(4)])  8.97 us
    ppermute x3, waiting for transfers between devices, quarter(): return lax.ppermute(part, ('zh', 'c'), [(i, i ^ flip) for i in range(4)])  7.22 us
    ppermute x2, starting transfers between devices, shards(): lax.ppermute(out_weight.T, AXES, route)  6.9 us
    unnamed x11, local copies, waits for them, and re-layouts  4.47 us
  transfers between devices with their start and end apart: 15, of which 9 were waited for; matrix products, arithmetic and copies ran while one was open for 4% of the time, Pallas kernels for 4%

profile of v2, /device:TPU:1, one launch (start us, length us, event | category | flops | bytes accessed | tf_op | source)
XLA Modules:
  0.0 124.3 jit_solution(15703053831083135859)
XLA Ops:
  6.5 0.0 copy-start
  6.5 0.7 all-gather.5.cloned.1.call-update
  7.3 0.0 all-gather.7.cloned.1.call-start
  7.3 1.0 reshape.13
  8.3 0.2 copy.12
  8.5 0.2 reshape.14
  8.7 3.3 %collective-permute-start = (bf16[64,384]{1,0:T(8,128)(2,1)S(1)}, bf16[64,384]{1,0:T(8,128)(2,1)S(1)}, u32[]{:S(2)}, u32[]{:S(2)}) collective-permute-start(bf16[64,384]{1,0:T(8,128)(2,1)S(1)} %get-tuple-element.31), channel_id=1, source_target_pairs={{0,4},{4,0},{128,132},{132,128},{1,5},{5,1},{129,133},{133,129},{2... | collective-permute-start | bytes 147464 | tf_op jit(solution)/shard_map/ppermute | solution.py:312
  12.0 5.2 %collective-permute-start.1 = (bf16[64,384]{1,0:T(8,128)(2,1)S(1)}, bf16[64,384]{1,0:T(8,128)(2,1)S(1)}, u32[]{:S(2)}, u32[]{:S(2)}) collective-permute-start(bf16[64,384]{1,0:T(8,128)(2,1)S(1)} %get-tuple-element.30), channel_id=1, source_target_pairs={{0,128},{4,132},{128,0},{132,4},{1,129},{5,133},{129,1},{133,5},{2... | collective-permute-start | bytes 147464 | tf_op jit(solution)/shard_map/ppermute | solution.py:312
  17.2 0.4 collective-permute-start.2
  17.7 0.0 collective-permute-done
  17.7 1.3 %collective-permute-done.1 = bf16[64,384]{1,0:T(8,128)(2,1)S(1)} collective-permute-done((bf16[64,384]{1,0:T(8,128)(2,1)S(1)}, bf16[64,384]{1,0:T(8,128)(2,1)S(1)}, u32[]{:S(2)}, u32[]{:S(2)}) %collective-permute-start.1) | collective-permute-done | bytes 49184 | tf_op jit(solution)/shard_map/ppermute | solution.py:312
  19.0 5.9 %collective-permute-done.2 = bf16[64,384]{1,0:T(8,128)(2,1)S(1)} collective-permute-done((bf16[64,384]{1,0:T(8,128)(2,1)S(1)}, bf16[64,384]{1,0:T(8,128)(2,1)S(1)}, u32[]{:S(2)}, u32[]{:S(2)}) %collective-permute-start.2) | collective-permute-done | bytes 49184 | tf_op jit(solution)/shard_map/ppermute | solution.py:312
  25.0 1.5 %collective-permute-start.3 = (bf16[256,384]{1,0:T(8,128)(2,1)S(1)}, bf16[256,384]{1,0:T(8,128)(2,1)S(1)}, u32[]{:S(2)}, u32[]{:S(2)}) collective-permute-start(bf16[256,384]{1,0:T(8,128)(2,1)S(1)} %pad_maximum_fusion), channel_id=1, source_target_pairs={{0,8},{4,36},{8,16},{12,44},{16,24},{20,52},{24,0},{28,60},{32,40}... | collective-permute-start | bytes 589832 | tf_op jit(solution)/shard_map/ppermute | solution.py:34
  26.6 1.5 %collective-permute-start.4 = (bf16[256,384]{1,0:T(8,128)(2,1)S(1)}, bf16[256,384]{1,0:T(8,128)(2,1)S(1)}, u32[]{:S(2)}, u32[]{:S(2)}) collective-permute-start(bf16[256,384]{1,0:T(8,128)(2,1)S(1)} %pad_maximum_fusion), channel_id=1, source_target_pairs={{0,24},{4,100},{8,0},{12,108},{16,8},{20,116},{24,16},{28,124},{32... | collective-permute-start | bytes 589832 | tf_op jit(solution)/shard_map/ppermute | solution.py:34
  28.1 3.3 %collective-permute-done.3 = bf16[256,384]{1,0:T(8,128)(2,1)S(1)} collective-permute-done((bf16[256,384]{1,0:T(8,128)(2,1)S(1)}, bf16[256,384]{1,0:T(8,128)(2,1)S(1)}, u32[]{:S(2)}, u32[]{:S(2)}) %collective-permute-start.3) | collective-permute-done | bytes 196640 | tf_op jit(solution)/shard_map/ppermute | solution.py:34
  31.4 0.2 collective-permute-start.5
  31.6 0.0 collective-permute-done.4
  31.6 2.6 %collective-permute-start.6 = (bf16[128,384]{1,0:T(8,128)(2,1)S(1)}, bf16[128,384]{1,0:T(8,128)(2,1)S(1)}, u32[]{:S(2)}, u32[]{:S(2)}) collective-permute-start(bf16[128,384]{1,0:T(8,128)(2,1)S(1)} %slice.17), channel_id=1, source_target_pairs={{0,24},{4,100},{8,0},{12,108},{16,8},{20,116},{24,16},{28,124},{32... | collective-permute-start | bytes 294920 | tf_op jit(solution)/shard_map/ppermute | solution.py:34
  34.3 2.2 %collective-permute-done.5 = bf16[128,384]{1,0:T(8,128)(2,1)S(1)} collective-permute-done((bf16[128,384]{1,0:T(8,128)(2,1)S(1)}, bf16[128,384]{1,0:T(8,128)(2,1)S(1)}, u32[]{:S(2)}, u32[]{:S(2)}) %collective-permute-start.5) | collective-permute-done | bytes 98336 | tf_op jit(solution)/shard_map/ppermute | solution.py:34
  36.6 0.0 collective-permute-done.6
  36.6 1.1 collective-permute-start.9
  37.7 1.7 %collective-permute-start.10 = (bf16[1024,384]{1,0:T(8,128)(2,1)S(1)}, bf16[1024,384]{1,0:T(8,128)(2,1)S(1)}, u32[]{:S(2)}, u32[]{:S(2)}) collective-permute-start(bf16[1024,384]{1,0:T(8,128)(2,1)S(1)} %constant_dynamic-update-slice_fusion.w0), channel_id=1, source_target_pairs={{0,96},{4,28},{8,104},{12,4},{16,112},{20,12},{24,120},{28,20},{32... | collective-permute-start | bytes 2359304 | tf_op jit(solution)/shard_map/ppermute | solution.py:34
  39.3 0.7 collective-permute-start.7
  40.0 6.2 %collective-permute-start.8 = (bf16[64,512]{1,0:T(8,128)(2,1)S(1)}, bf16[64,512]{1,0:T(8,128)(2,1)S(1)}, u32[]{:S(2)}, u32[]{:S(2)}) collective-permute-start(bf16[64,512]{1,0:T(8,128)(2,1)S(1)} %bitcast.35), channel_id=1, source_target_pairs={{0,128},{1,192},{2,0},{3,64},{4,132},{5,196},{6,4},{7,68},{8,136},... | collective-permute-start | bytes 196616 | tf_op jit(solution)/shard_map/ppermute | solution.py:324
  46.3 0.0 collective-permute-done.7
  46.3 2.7 %collective-permute-done.8 = bf16[64,512]{1,0:T(8,128)(2,1)S(1)} collective-permute-done((bf16[64,512]{1,0:T(8,128)(2,1)S(1)}, bf16[64,512]{1,0:T(8,128)(2,1)S(1)}, u32[]{:S(2)}, u32[]{:S(2)}) %collective-permute-start.8) | collective-permute-done | bytes 65568 | tf_op jit(solution)/shard_map/ppermute | solution.py:324
  49.0 0.1 collective-permute-done.9.w1
  49.1 0.0 collective-permute-done.10.w2
  49.1 0.7 pad_maximum_fusion.1
  49.8 0.0 all-gather.7.cloned.1.call-update
  49.8 0.8 slice.18
  50.7 1.0 collective-permute-start.11
  51.6 0.8 slice.19
  52.5 1.7 %collective-permute-start.12 = (bf16[512,384]{1,0:T(8,128)(2,1)}, bf16[512,384]{1,0:T(8,128)(2,1)S(1)}, u32[]{:S(2)}, u32[]{:S(2)}) collective-permute-start(bf16[512,384]{1,0:T(8,128)(2,1)} %slice.19), channel_id=1, source_target_pairs={{0,96},{4,28},{8,104},{12,4},{16,112},{20,12},{24,120},{28,20},{32... | collective-permute-start | bytes 1179656 | tf_op jit(solution)/shard_map/ppermute | solution.py:34
  54.2 0.0 copy-done
  54.2 0.8 dynamic-slice_bitcast_fusion.5.skip
  54.9 0.1 pad_add_fusion.pos
  55.0 0.7 dynamic-slice_bitcast_fusion.3
  55.7 3.0 %collective-permute-done.11.w3 = bf16[512,384]{1,0:T(8,128)(2,1)S(1)} collective-permute-done((bf16[512,384]{1,0:T(8,128)(2,1)}, bf16[512,384]{1,0:T(8,128)(2,1)S(1)}, u32[]{:S(2)}, u32[]{:S(2)}) %collective-permute-start.11) | collective-permute-done | bytes 393248 | tf_op jit(solution)/shard_map/ppermute | solution.py:34
  58.7 0.6 collective-permute-done.12.w4
  59.3 2.2 %copy-done.2 = bf16[2048,1024]{1,0:T(8,128)(2,1)S(1)} copy-done((bf16[2048,1024]{1,0:T(8,128)(2,1)S(1)}, bf16[2048,1024]{1,0:T(8,128)(2,1)}, u32[]{:S(2)}) %copy-start.2) | copy-done | bytes 4194328
  61.5 3.5 %shard_map.73 = (f32[512,128]{1,0:T(8,128)S(1)}, f32[512,128]{1,0:T(8,128)S(1)}, f32[128,128]{1,0:T(8,128)S(1)}, f32[16,40,128]{2,1,0:T(8,128)S(1)}) custom-call(s32[4]{0:T(128)S(1)} %pad_add_fusion.pos, bf16[2,4,2,128,1024]{4,3,2,1,0:T(8,128)(2,1)S(1)} %bitcast.30, bf16[1024,384]{1,0:T(8,128)(2,1)S(1)} %constant_dynamic-update-slice_fusion.w0, ...), custom_call_target="tpu_custom_call" | custom-call | flops 1610612736 | bytes 6000000 | tf_op jit(solution)/shard_map/pallas_call | solution.py:141
  65.0 19.6 %all_to_all.10.edges = f32[16,40,128]{2,1,0:T(8,128)S(1)} all-to-all(f32[16,40,128]{2,1,0:T(8,128)S(1)} %get-tuple-element.15), channel_id=1, replica_groups=mesh['zh'=2,'y'=4,'x'=4,'c'=2,'zl'=4] {'y','x'}, dimensions={0} | all-to-all | bytes 655360 | tf_op jit(solution)/shard_map/all_to_all | solution.py:343
  84.6 1.0 shard_map.74
  85.6 24.7 %all_to_all.11.gates = bf16[16,128,128]{2,1,0:T(8,128)(2,1)S(1)} all-to-all(bf16[16,128,128]{2,1,0:T(8,128)(2,1)S(1)} %shard_map.74), channel_id=1, replica_groups=mesh['zh'=2,'y'=4,'x'=4,'c'=2,'zl'=4] {'zh','c','zl'}, dimensions={0} | all-to-all | bytes 1048576 | tf_op jit(solution)/shard_map/all_to_all | solution.py:345
  110.3 2.3 %all-gather.7.cloned.1.call-done = bf16[64,64,512]{2,1,0:T(8,128)(2,1)} async-done(((bf16[2,64,512]{2,1,0:T(8,128)(2,1)}), bf16[64,64,512]{2,1,0:T(8,128)(2,1)}) %all-gather.7.cloned.1.call-update) | async-done | bytes 4194320 | tf_op jit(solution)/shard_map/all_gather | solution.py:328
  112.6 2.2 %copy-done.1 = bf16[64,64,512]{2,1,0:T(8,128)(2,1)S(1)} copy-done((bf16[64,64,512]{2,1,0:T(8,128)(2,1)S(1)}, bf16[64,64,512]{2,1,0:T(8,128)(2,1)}, u32[]{:S(2)}) %copy-start.1) | copy-done | bytes 4194328
  114.8 2.7 %shard_map.75 = bf16[128,1024]{1,0:T(8,128)(2,1)} custom-call(s32[4]{0:T(128)S(1)} %pad_add_fusion.pos, bf16[16,128,128]{2,1,0:T(8,128)(2,1)S(1)} %all_to_all.11.gates, bf16[32,2,64,512]{3,2,1,0:T(8,128)(2,1)S(1)} %bitcast.29), custom_call_target="tpu_custom_call" | custom-call | flops 536870912 | bytes 5000000 | tf_op jit(solution)/shard_map/pallas_call | solution.py:276
  (20 shorter events, 0.3 us)
Async XLA Ops:
  6.5 47.6 %copy-start = (f32[3,3,512]{2,1,0:T(4,128)S(1)}, f32[3,3,512]{2,1,0:T(4,128)}, u32[]{:S(2)}) copy-start(f32[3,3,512]{2,1,0:T(4,128)} %param.9) | copy-start | bytes 55300
  6.5 32.8 %copy-start.3 = (bf16[512,64]{0,1:T(8,128)(2,1)S(1)}, bf16[512,64]{0,1:T(8,128)(2,1)}, u32[]{:S(2)}) copy-start(bf16[512,64]{0,1:T(8,128)(2,1)} %param.13) | copy-start | bytes 196612
  6.5 52.8 %all-gather.5.cloned.1.call-start = ((), (), s32[]{:S(2)}) async-start(), calls=%async_computation.2 | async-start | bytes 4456448 | tf_op jit(solution)/shard_map/all_gather | solution.py:303
  7.3 105.3 %all-gather.7.cloned.1.call-start = ((), (), s32[]{:S(2)}) async-start(), calls=%async_computation.3 | async-start | bytes 4325376 | tf_op jit(solution)/shard_map/all_gather | solution.py:328
  8.7 9.0 %collective-permute-start = (bf16[64,384]{1,0:T(8,128)(2,1)S(1)}, bf16[64,384]{1,0:T(8,128)(2,1)S(1)}, u32[]{:S(2)}, u32[]{:S(2)}) collective-permute-start(bf16[64,384]{1,0:T(8,128)(2,1)S(1)} %get-tuple-element.31), channel_id=1, source_target_pairs={{0,4},{4,0},{128,132},{132,128},{1,5},{5,1},{129,133},{133,129},{2... | collective-permute-start | bytes 147464 | tf_op jit(solution)/shard_map/ppermute | solution.py:312
  12.0 7.0 %collective-permute-start.1 = (bf16[64,384]{1,0:T(8,128)(2,1)S(1)}, bf16[64,384]{1,0:T(8,128)(2,1)S(1)}, u32[]{:S(2)}, u32[]{:S(2)}) collective-permute-start(bf16[64,384]{1,0:T(8,128)(2,1)S(1)} %get-tuple-element.30), channel_id=1, source_target_pairs={{0,128},{4,132},{128,0},{132,4},{1,129},{5,133},{129,1},{133,5},{2... | collective-permute-start | bytes 147464 | tf_op jit(solution)/shard_map/ppermute | solution.py:312
  17.2 7.7 %collective-permute-start.2 = (bf16[64,384]{1,0:T(8,128)(2,1)S(1)}, bf16[64,384]{1,0:T(8,128)(2,1)S(1)}, u32[]{:S(2)}, u32[]{:S(2)}) collective-permute-start(bf16[64,384]{1,0:T(8,128)(2,1)S(1)} %get-tuple-element.29), channel_id=1, source_target_pairs={{0,132},{4,128},{128,4},{132,0},{1,133},{5,129},{129,5},{133,1},{2... | collective-permute-start | bytes 147464 | tf_op jit(solution)/shard_map/ppermute | solution.py:312
  25.0 6.3 %collective-permute-start.3 = (bf16[256,384]{1,0:T(8,128)(2,1)S(1)}, bf16[256,384]{1,0:T(8,128)(2,1)S(1)}, u32[]{:S(2)}, u32[]{:S(2)}) collective-permute-start(bf16[256,384]{1,0:T(8,128)(2,1)S(1)} %pad_maximum_fusion), channel_id=1, source_target_pairs={{0,8},{4,36},{8,16},{12,44},{16,24},{20,52},{24,0},{28,60},{32,40}... | collective-permute-start | bytes 589832 | tf_op jit(solution)/shard_map/ppermute | solution.py:34
  26.6 5.0 %collective-permute-start.4 = (bf16[256,384]{1,0:T(8,128)(2,1)S(1)}, bf16[256,384]{1,0:T(8,128)(2,1)S(1)}, u32[]{:S(2)}, u32[]{:S(2)}) collective-permute-start(bf16[256,384]{1,0:T(8,128)(2,1)S(1)} %pad_maximum_fusion), channel_id=1, source_target_pairs={{0,24},{4,100},{8,0},{12,108},{16,8},{20,116},{24,16},{28,124},{32... | collective-permute-start | bytes 589832 | tf_op jit(solution)/shard_map/ppermute | solution.py:34
  31.4 5.2 %collective-permute-start.5 = (bf16[128,384]{1,0:T(8,128)(2,1)S(1)}, bf16[128,384]{1,0:T(8,128)(2,1)S(1)}, u32[]{:S(2)}, u32[]{:S(2)}) collective-permute-start(bf16[128,384]{1,0:T(8,128)(2,1)S(1)} %slice.16), channel_id=1, source_target_pairs={{0,8},{4,36},{8,16},{12,44},{16,24},{20,52},{24,0},{28,60},{32,40}... | collective-permute-start | bytes 294920 | tf_op jit(solution)/shard_map/ppermute | solution.py:34
  31.6 5.0 %collective-permute-start.6 = (bf16[128,384]{1,0:T(8,128)(2,1)S(1)}, bf16[128,384]{1,0:T(8,128)(2,1)S(1)}, u32[]{:S(2)}, u32[]{:S(2)}) collective-permute-start(bf16[128,384]{1,0:T(8,128)(2,1)S(1)} %slice.17), channel_id=1, source_target_pairs={{0,24},{4,100},{8,0},{12,108},{16,8},{20,116},{24,16},{28,124},{32... | collective-permute-start | bytes 294920 | tf_op jit(solution)/shard_map/ppermute | solution.py:34
  36.6 12.5 %collective-permute-start.9 = (bf16[1024,384]{1,0:T(8,128)(2,1)S(1)}, bf16[1024,384]{1,0:T(8,128)(2,1)S(1)}, u32[]{:S(2)}, u32[]{:S(2)}) collective-permute-start(bf16[1024,384]{1,0:T(8,128)(2,1)S(1)} %constant_dynamic-update-slice_fusion.w0), channel_id=1, source_target_pairs={{0,32},{4,12},{8,40},{12,20},{16,48},{20,28},{24,56},{28,4},{32,64... | collective-permute-start | bytes 2359304 | tf_op jit(solution)/shard_map/ppermute | solution.py:34
  37.7 11.4 %collective-permute-start.10 = (bf16[1024,384]{1,0:T(8,128)(2,1)S(1)}, bf16[1024,384]{1,0:T(8,128)(2,1)S(1)}, u32[]{:S(2)}, u32[]{:S(2)}) collective-permute-start(bf16[1024,384]{1,0:T(8,128)(2,1)S(1)} %constant_dynamic-update-slice_fusion.w0), channel_id=1, source_target_pairs={{0,96},{4,28},{8,104},{12,4},{16,112},{20,12},{24,120},{28,20},{32... | collective-permute-start | bytes 2359304 | tf_op jit(solution)/shard_map/ppermute | solution.py:34
  39.3 6.9 %collective-permute-start.7 = (bf16[64,512]{1,0:T(8,128)(2,1)S(1)}, bf16[64,512]{1,0:T(8,128)(2,1)S(1)}, u32[]{:S(2)}, u32[]{:S(2)}) collective-permute-start(bf16[64,512]{1,0:T(8,128)(2,1)S(1)} %bitcast.34), channel_id=1, source_target_pairs={{0,0},{1,64},{2,128},{3,192},{4,4},{5,68},{6,132},{7,196},{8,8},{9... | collective-permute-start | bytes 196616 | tf_op jit(solution)/shard_map/ppermute | solution.py:324
  40.0 9.0 %collective-permute-start.8 = (bf16[64,512]{1,0:T(8,128)(2,1)S(1)}, bf16[64,512]{1,0:T(8,128)(2,1)S(1)}, u32[]{:S(2)}, u32[]{:S(2)}) collective-permute-start(bf16[64,512]{1,0:T(8,128)(2,1)S(1)} %bitcast.35), channel_id=1, source_target_pairs={{0,128},{1,192},{2,0},{3,64},{4,132},{5,196},{6,4},{7,68},{8,136},... | collective-permute-start | bytes 196616 | tf_op jit(solution)/shard_map/ppermute | solution.py:324
  50.7 8.0 %collective-permute-start.11 = (bf16[512,384]{1,0:T(8,128)(2,1)}, bf16[512,384]{1,0:T(8,128)(2,1)S(1)}, u32[]{:S(2)}, u32[]{:S(2)}) collective-permute-start(bf16[512,384]{1,0:T(8,128)(2,1)} %slice.18), channel_id=1, source_target_pairs={{0,32},{4,12},{8,40},{12,20},{16,48},{20,28},{24,56},{28,4},{32,64... | collective-permute-start | bytes 1179656 | tf_op jit(solution)/shard_map/ppermute | solution.py:34
  52.5 6.8 %collective-permute-start.12 = (bf16[512,384]{1,0:T(8,128)(2,1)}, bf16[512,384]{1,0:T(8,128)(2,1)S(1)}, u32[]{:S(2)}, u32[]{:S(2)}) collective-permute-start(bf16[512,384]{1,0:T(8,128)(2,1)} %slice.19), channel_id=1, source_target_pairs={{0,96},{4,28},{8,104},{12,4},{16,112},{20,12},{24,120},{28,20},{32... | collective-permute-start | bytes 1179656 | tf_op jit(solution)/shard_map/ppermute | solution.py:34
  59.3 2.2 %copy-start.2 = (bf16[2048,1024]{1,0:T(8,128)(2,1)S(1)}, bf16[2048,1024]{1,0:T(8,128)(2,1)}, u32[]{:S(2)}) copy-start(bf16[2048,1024]{1,0:T(8,128)(2,1)} %all-gather.5.cloned.1.call-done) | copy-start | bytes 12582916
  112.6 2.2 %copy-start.1 = (bf16[64,64,512]{2,1,0:T(8,128)(2,1)S(1)}, bf16[64,64,512]{2,1,0:T(8,128)(2,1)}, u32[]{:S(2)}) copy-start(bf16[64,64,512]{2,1,0:T(8,128)(2,1)} %all-gather.7.cloned.1.call-done) | copy-start | bytes 12582916
Sparse Core Ops, SparseCore 0:
  9.2 48.7 all-gather.4
  60.5 52.0 all-gather.6

commit v3 on v2

--- a/solution.py
+++ b/solution.py
@@ -8,9 +8,10 @@
 from jax.experimental.pallas import tpu as pltpu
 from jax.sharding import Mesh, PartitionSpec as P
 
-AXES = ("zh", "y", "x", "c", "zl")
-SIZES = (2, 4, 4, 2, 4)
-SEQ = ("zh", "y", "x", "c")
+AXES = ("zh", "yh", "yl", "x", "c", "zl")
+SIZES = (2, 2, 2, 4, 2, 4)
+SEQ = AXES[:5]
+PLANE = ("yh", "yl", "x")
 CHIPS = 16
 BLOCK = 256
 HALF = 128
@@ -31,16 +32,11 @@
     for y, x, c in np.ndindex(4, 4, 2):
         target = (y, (x + distance) % 4, c) if c == phase else ((y + distance) % 4, x, c)
         route.append((int(np.ravel_multi_index((y, x, c), (4, 4, 2))), int(np.ravel_multi_index(target, (4, 4, 2)))))
-    return lax.ppermute(block, ("y", "x", "c"), route)
-
-
-def ring(block, phase):
-    half = block.shape[0] // 2
-    low = crossed(block, phase, 1)
-    high = crossed(block, phase, -1)
-    far_low = crossed(low[:half], phase, 1)
-    far_high = crossed(high[half:], phase, -1)
-    return [block, low, high, far_low, far_high]
+    return lax.ppermute(block, PLANE + ("c",), route)
+
+
+def direct(block, phase):
+    return [block] + [crossed(block, phase, distance) for distance in (1, -1, 2)]
 
 
 RING_ORDER = (0, -1, 1, 2)
@@ -255,15 +251,22 @@
 
 
 def out_kernel(pos, gates, weights, out):
-    own_zh = pos[2]
+    own_zh, own_yh = pos[2], pos[0] // 2
     total = jnp.zeros((HALF, 1024), F32)
-    for k in range(2):
-        for half in range(2):
-            zl = (own_zh if k == 0 else 1 - own_zh) * 2 + half
-            parts = [gates[(2 * zh + c) * 4 + zl] for zh in range(2) for c in range(2)]
+    for depth in range(2):
+        for flip in range(2):
+            high = own_zh if depth == 0 else 1 - own_zh
+            zl = high * 2 + (own_yh if flip == 0 else 1 - own_yh)
+            left = [gates[(2 * zh + c) * 4 + zl] for zh in range(2) for c in range(2)]
+            right = [
+                weights[x, yl, c, flip, depth]
+                for yl in range(2)
+                for x in range(4)
+                for c in range(2)
+            ]
             total = total + lax.dot_general(
-                jnp.concatenate(parts, axis=1),
-                weights[16 * half : 16 * (half + 1), k].reshape(1024, 512),
+                jnp.concatenate(left, axis=1),
+                jnp.concatenate(right, axis=0),
                 (((1,), (1,)), ((), ())),
                 preferred_element_type=F32,
             )
@@ -286,17 +289,18 @@
 
 
 def transposed_routes():
-    near, far = [], []
-    for zh, y, x, c, zl in np.ndindex(*SIZES):
-        source = int(np.ravel_multi_index((zh, y, x, c, zl), SIZES))
-        for route, to_zh in ((near, zl // 2), (far, 1 - zl // 2)):
-            target = (to_zh, (zl % 2) * 2 + y % 2, x, c, zh * 2 + y // 2)
-            route.append((source, int(np.ravel_multi_index(target, SIZES))))
-    return near, far
+    routes = [[], []]
+    for zh, yh, yl, x, c, zl in np.ndindex(*SIZES):
+        source = int(np.ravel_multi_index((zh, yh, yl, x, c, zl), SIZES))
+        for flip in range(2):
+            target = ((zl // 2) ^ flip, zl % 2, yl, x, c, zh * 2 + yh)
+            routes[flip].append((source, int(np.ravel_multi_index(target, SIZES))))
+    return routes
 
 
 def shards(tokens, in_weight, short_weight, residues, decay_rates, skip_gain, out_weight):
-    zh, y, x, c = (lax.axis_index(axis) for axis in SEQ)
+    zh, x, c = (lax.axis_index(axis) for axis in ("zh", "x", "c"))
+    y = lax.axis_index(("yh", "yl"))
     pos = jnp.stack([y, x, zh, c]).astype(jnp.int32)
     group = zh * 2 + c
 
@@ -318,19 +322,24 @@
 
     far = in_order(quarter(2), quarter(3))
     near = in_order(quarter(0), quarter(1))
-    gathered_once = jnp.concatenate(ring(jnp.concatenate([near, far], axis=0), 0), axis=0)
-    in_weights = ring(gathered_once, 1)
-
+    gathered_once = jnp.concatenate(direct(jnp.concatenate([near, far], axis=0), 0), axis=0)
+
+    half = gathered_once.shape[0] // 2
+    low = crossed(gathered_once, 1, 1)
+    high = crossed(gathered_once, 1, -1)
     moved = [lax.ppermute(out_weight.T, AXES, route) for route in transposed_routes()]
-    moved[0], moved[1], in_weights[1], in_weights[2] = lax.optimization_barrier(
-        (moved[0], moved[1], in_weights[1], in_weights[2])
-    )
-    gathered = lax.all_gather(
-        jnp.stack(moved),
-        ("y", "x", "c"),
-        axis=0,
-        tiled=False,
-    )
+    low, high, moved = lax.optimization_barrier((low, high, moved))
+    moved = jnp.concatenate(moved, axis=0)
+    far_low = crossed(low[:half], 1, 1)
+    far_high = crossed(high[half:], 1, -1)
+    flipped = lax.ppermute(moved, "yh", [(0, 1), (1, 0)])
+    far_low, far_high, flipped = lax.optimization_barrier((far_low, far_high, flipped))
+    in_weights = [gathered_once, low, high, far_low, far_high]
+
+    slabs, in_weights[3] = lax.optimization_barrier((slabs, in_weights[3]))
+
+    gathered = lax.all_gather(jnp.stack([moved, flipped]), ("x", "yl", "c"), axis=0, tiled=False)
+    gathered = gathered.reshape(4, 2, 2, 2, 2, GROUP, 512)
 
     def own_channels(table, axis):
         return lax.dynamic_slice_in_dim(table, group * LANES, LANES, axis)
@@ -340,7 +349,7 @@
     weights = own_channels(residues, 0).T
     skip = own_channels(skip_gain, 0)[None]
     mixed, gate, sub_states, edges = front(pos, slabs, in_weights, taps, rates, weights, skip)
-    edges = lax.all_to_all(edges, ("y", "x"), split_axis=0, concat_axis=0, tiled=True)
+    edges = lax.all_to_all(edges, PLANE, split_axis=0, concat_axis=0, tiled=True)
     gate_out = back(pos, edges, sub_states, mixed, gate, rates, weights, skip)
     gates = lax.all_to_all(gate_out, ("zh", "c", "zl"), split_axis=0, concat_axis=0, tiled=True)
     return project_out(pos, gates, gathered)

time: 125 us -> 123 us (0.984)
  starting transfers between devices: 27.2 us -> 23.5 us
  waiting for transfers between devices: 22.2 us -> 25 us
  local copies, waits for them, and re-layouts: 8.98 us -> 7.4 us
    ppermute x8, waiting for transfers between devices: 9.21 us -> 14.2 us  [the longest x7 11.8 us: crossed(): return lax.ppermute(block, PLANE + ('c',), route)]
    ppermute x2, starting transfers between devices: 6.9 us -> 2.03 us  [shards(): lax.ppermute(out_weight.T, AXES, route)]
    all_gather x1, waiting for transfers between devices: 2.25 us -> 0.01 us  [shards(): lax.all_gather(jnp.stack([moved, flipped]), ('x', 'yl', 'c'), axis=0, til...]
    slice x4 -> x2, local copies, waits for them, and re-layouts: 1.68 us -> 0.08 us  [the longest x1 0.04 us: shards(): far_high = crossed(high[half:], 1, -1)]
    ppermute x8, starting transfers between devices: 11.3 us -> 12.8 us  [the longest x7 8.8 us: crossed(): return lax.ppermute(block, PLANE + ('c',), route)]
    all_to_all x1, blocking collectives: 24.7 us -> 26.1 us  [shards(): lax.all_to_all(gate_out, ('zh', 'c', 'zl'), split_axis=0, concat_axis=0,...]
  transfers between devices with their start and end apart: 15 -> 15, of which waited for: 9 -> 10; matrix products, arithmetic and copies ran while one was open for 4% -> 3% of each run, Pallas kernels for 4% -> 4%
where the time goes in v3:
time: 123 us; the launch traced here: 122 us
  blocking collectives  44.5 us (36%)
  waiting for transfers between devices  25 us (20%)
  starting transfers between devices  23.5 us (19%)
  between operations  13.6 us (11%)
  local copies, waits for them, and re-layouts  7.4 us (6%)
  Pallas kernels  7.25 us (6%)
    all_to_all x1, blocking collectives, shards(): lax.all_to_all(gate_out, ('zh', 'c', 'zl'), split_axis=0, concat_axis=0,...  26.1 us
    all_to_all x1, blocking collectives, shards(): lax.all_to_all(edges, PLANE, split_axis=0, concat_axis=0, tiled=True)  18.4 us
    ppermute x7, waiting for transfers between devices, crossed(): return lax.ppermute(block, PLANE + ('c',), route)  11.8 us
    ppermute x7, starting transfers between devices, crossed(): return lax.ppermute(block, PLANE + ('c',), route)  8.8 us
    ppermute x3, starting transfers between devices, quarter(): return lax.ppermute(part, ('zh', 'c'), [(i, i ^ flip) for i in range(4)])  8.69 us
    ppermute x3, waiting for transfers between devices, quarter(): return lax.ppermute(part, ('zh', 'c'), [(i, i ^ flip) for i in range(4)])  6.69 us
    unnamed x11, local copies, waits for them, and re-layouts  4.45 us
    ppermute x1, starting transfers between devices, shards(): flipped = lax.ppermute(moved, 'yh', [(0, 1), (1, 0)])  3.96 us
  transfers between devices with their start and end apart: 15, of which 10 were waited for; matrix products, arithmetic and copies ran while one was open for 3% of the time, Pallas kernels for 4%

profile of v3, /device:TPU:1, one launch (start us, length us, event | category | flops | bytes accessed | tf_op | source)
XLA Modules:
  0.0 122.1 jit_solution(4375849805447786754)
XLA Ops:
  6.5 0.0 copy-start
  6.5 0.0 copy-start.3
  6.5 0.0 all-gather.5.cloned.1.call-start
  6.5 0.7 all-gather.5.cloned.1.call-update
  7.3 0.0 all-gather.7.cloned.1.call-start
  7.3 1.0 reshape.16
  8.3 0.2 copy.12
  8.5 0.2 reshape.17
  8.7 3.3 %collective-permute-start = (bf16[64,384]{1,0:T(8,128)(2,1)S(1)}, bf16[64,384]{1,0:T(8,128)(2,1)S(1)}, u32[]{:S(2)}, u32[]{:S(2)}) collective-permute-start(bf16[64,384]{1,0:T(8,128)(2,1)S(1)} %get-tuple-element.41), channel_id=1, source_target_pairs={{0,4},{4,0},{128,132},{132,128},{1,5},{5,1},{129,133},{133,129},{2... | collective-permute-start | bytes 147464 | tf_op jit(solution)/shard_map/ppermute | solution.py:316
  12.0 5.2 %collective-permute-start.2 = (bf16[64,384]{1,0:T(8,128)(2,1)S(1)}, bf16[64,384]{1,0:T(8,128)(2,1)S(1)}, u32[]{:S(2)}, u32[]{:S(2)}) collective-permute-start(bf16[64,384]{1,0:T(8,128)(2,1)S(1)} %get-tuple-element.39), channel_id=1, source_target_pairs={{0,132},{4,128},{128,4},{132,0},{1,133},{5,129},{129,5},{133,1},{2... | collective-permute-start | bytes 147464 | tf_op jit(solution)/shard_map/ppermute | solution.py:316
  17.2 0.2 collective-permute-start.1
  17.4 0.0 collective-permute-done
  17.5 2.0 %collective-permute-done.2 = bf16[64,384]{1,0:T(8,128)(2,1)S(1)} collective-permute-done((bf16[64,384]{1,0:T(8,128)(2,1)S(1)}, bf16[64,384]{1,0:T(8,128)(2,1)S(1)}, u32[]{:S(2)}, u32[]{:S(2)}) %collective-permute-start.2) | collective-permute-done | bytes 49184 | tf_op jit(solution)/shard_map/ppermute | solution.py:316
  19.5 4.7 %collective-permute-done.1 = bf16[64,384]{1,0:T(8,128)(2,1)S(1)} collective-permute-done((bf16[64,384]{1,0:T(8,128)(2,1)S(1)}, bf16[64,384]{1,0:T(8,128)(2,1)S(1)}, u32[]{:S(2)}, u32[]{:S(2)}) %collective-permute-start.1) | collective-permute-done | bytes 49184 | tf_op jit(solution)/shard_map/ppermute | solution.py:316
  24.2 1.4 %collective-permute-start.3 = (bf16[256,384]{1,0:T(8,128)(2,1)S(1)}, bf16[256,384]{1,0:T(8,128)(2,1)S(1)}, u32[]{:S(2)}, u32[]{:S(2)}) collective-permute-start(bf16[256,384]{1,0:T(8,128)(2,1)S(1)} %pad_maximum_fusion.1), channel_id=1, source_target_pairs={{0,8},{4,36},{8,16},{12,44},{16,24},{20,52},{24,0},{28,60},{32,40}... | collective-permute-start | bytes 589832 | tf_op jit(solution)/shard_map/ppermute | solution.py:35
  25.6 1.5 %collective-permute-start.4 = (bf16[256,384]{1,0:T(8,128)(2,1)S(1)}, bf16[256,384]{1,0:T(8,128)(2,1)S(1)}, u32[]{:S(2)}, u32[]{:S(2)}) collective-permute-start(bf16[256,384]{1,0:T(8,128)(2,1)S(1)} %pad_maximum_fusion.1), channel_id=1, source_target_pairs={{0,24},{4,100},{8,0},{12,108},{16,8},{20,116},{24,16},{28,124},{32... | collective-permute-start | bytes 589832 | tf_op jit(solution)/shard_map/ppermute | solution.py:35
  27.1 1.6 %collective-permute-start.5 = (bf16[256,384]{1,0:T(8,128)(2,1)S(1)}, bf16[256,384]{1,0:T(8,128)(2,1)S(1)}, u32[]{:S(2)}, u32[]{:S(2)}) collective-permute-start(bf16[256,384]{1,0:T(8,128)(2,1)S(1)} %pad_maximum_fusion.1), channel_id=1, source_target_pairs={{0,16},{4,68},{8,24},{12,76},{16,0},{20,84},{24,8},{28,92},{32,48}... | collective-permute-start | bytes 589832 | tf_op jit(solution)/shard_map/ppermute | solution.py:35
  28.7 1.8 %collective-permute-done.3 = bf16[256,384]{1,0:T(8,128)(2,1)S(1)} collective-permute-done((bf16[256,384]{1,0:T(8,128)(2,1)S(1)}, bf16[256,384]{1,0:T(8,128)(2,1)S(1)}, u32[]{:S(2)}, u32[]{:S(2)}) %collective-permute-start.3) | collective-permute-done | bytes 196640 | tf_op jit(solution)/shard_map/ppermute | solution.py:35
  30.5 1.3 %collective-permute-done.4 = bf16[256,384]{1,0:T(8,128)(2,1)S(1)} collective-permute-done((bf16[256,384]{1,0:T(8,128)(2,1)S(1)}, bf16[256,384]{1,0:T(8,128)(2,1)S(1)}, u32[]{:S(2)}, u32[]{:S(2)}) %collective-permute-start.4) | collective-permute-done | bytes 196640 | tf_op jit(solution)/shard_map/ppermute | solution.py:35
  31.9 1.5 %collective-permute-done.5 = bf16[256,384]{1,0:T(8,128)(2,1)S(1)} collective-permute-done((bf16[256,384]{1,0:T(8,128)(2,1)S(1)}, bf16[256,384]{1,0:T(8,128)(2,1)S(1)}, u32[]{:S(2)}, u32[]{:S(2)}) %collective-permute-start.5) | collective-permute-done | bytes 196640 | tf_op jit(solution)/shard_map/ppermute | solution.py:35
  33.5 2.8 %collective-permute-start.7 = (bf16[1024,384]{1,0:T(8,128)(2,1)S(1)}, bf16[1024,384]{1,0:T(8,128)(2,1)S(1)}, u32[]{:S(2)}, u32[]{:S(2)}) collective-permute-start(bf16[1024,384]{1,0:T(8,128)(2,1)S(1)} %constant_dynamic-update-slice_fusion.w0), channel_id=1, source_target_pairs={{0,96},{4,28},{8,104},{12,4},{16,112},{20,12},{24,120},{28,20},{32... | collective-permute-start | bytes 2359304 | tf_op jit(solution)/shard_map/ppermute | solution.py:35
  36.3 0.0 collective-permute-start.6
  36.3 0.0 copy-done.3
  36.3 1.4 %collective-permute-start.9 = (bf16[64,512]{1,0:T(8,128)(2,1)S(1)}, bf16[64,512]{1,0:T(8,128)(2,1)S(1)}, u32[]{:S(2)}, u32[]{:S(2)}) collective-permute-start(bf16[64,512]{1,0:T(8,128)(2,1)S(1)} %bitcast.34), channel_id=1, source_target_pairs={{0,128},{1,192},{2,0},{3,64},{4,132},{5,196},{6,4},{7,68},{8,136},... | collective-permute-start | bytes 196616 | tf_op jit(solution)/shard_map/ppermute | solution.py:330
  37.7 0.7 collective-permute-start.8
  38.3 3.4 %collective-permute-done.9 = bf16[64,512]{1,0:T(8,128)(2,1)S(1)} collective-permute-done((bf16[64,512]{1,0:T(8,128)(2,1)S(1)}, bf16[64,512]{1,0:T(8,128)(2,1)S(1)}, u32[]{:S(2)}, u32[]{:S(2)}) %collective-permute-start.9) | collective-permute-done | bytes 65568 | tf_op jit(solution)/shard_map/ppermute | solution.py:330
  41.7 0.0 collective-permute-done.8
  41.7 3.5 %collective-permute-done.7.w2 = bf16[1024,384]{1,0:T(8,128)(2,1)S(1)} collective-permute-done((bf16[1024,384]{1,0:T(8,128)(2,1)S(1)}, bf16[1024,384]{1,0:T(8,128)(2,1)S(1)}, u32[]{:S(2)}, u32[]{:S(2)}) %collective-permute-start.7) | collective-permute-done | bytes 786464 | tf_op jit(solution)/shard_map/ppermute | solution.py:35
  45.2 3.5 %collective-permute-done.6.w1 = bf16[1024,384]{1,0:T(8,128)(2,1)S(1)} collective-permute-done((bf16[1024,384]{1,0:T(8,128)(2,1)S(1)}, bf16[1024,384]{1,0:T(8,128)(2,1)S(1)}, u32[]{:S(2)}, u32[]{:S(2)}) %collective-permute-start.6) | collective-permute-done | bytes 786464 | tf_op jit(solution)/shard_map/ppermute | solution.py:35
  48.8 0.1 collective-permute-start.11
  48.9 1.5 %collective-permute-start.10 = (bf16[512,384]{1,0:T(8,128)(2,1)S(1)}, bf16[512,384]{1,0:T(8,128)(2,1)S(1)}, u32[]{:S(2)}, u32[]{:S(2)}) collective-permute-start(bf16[512,384]{1,0:T(8,128)(2,1)S(1)} %slice.6), channel_id=1, source_target_pairs={{0,32},{4,12},{8,40},{12,20},{16,48},{20,28},{24,56},{28,4},{32,64... | collective-permute-start | bytes 1179656 | tf_op jit(solution)/shard_map/ppermute | solution.py:35
  50.4 4.0 %collective-permute-start.12 = (bf16[128,512]{1,0:T(8,128)(2,1)S(1)}, bf16[128,512]{1,0:T(8,128)(2,1)S(1)}, u32[]{:S(2)}, u32[]{:S(2)}) collective-permute-start(bf16[128,512]{1,0:T(8,128)(2,1)S(1)} %constant_dynamic-update-slice_fusion.7), channel_id=1, source_target_pairs={{0,64},{64,0},{1,65},{65,1},{2,66},{66,2},{3,67},{67,3},{4,68},{68... | collective-permute-start | bytes 393224 | tf_op jit(solution)/shard_map/ppermute | solution.py:335
  54.3 2.4 %collective-permute-done.12 = bf16[128,512]{1,0:T(8,128)(2,1)S(1)} collective-permute-done((bf16[128,512]{1,0:T(8,128)(2,1)S(1)}, bf16[128,512]{1,0:T(8,128)(2,1)S(1)}, u32[]{:S(2)}, u32[]{:S(2)}) %collective-permute-start.12) | collective-permute-done | bytes 131104 | tf_op jit(solution)/shard_map/ppermute | solution.py:335
  56.7 0.0 collective-permute-done.11.w4
  56.7 0.1 collective-permute-done.10.w3
  56.8 0.7 pad_maximum_fusion
  57.6 0.0 all-gather.7.cloned.1.call-update
  57.6 0.0 copy-done
  57.6 0.8 dynamic-slice_bitcast_fusion.5.skip
  58.4 0.1 pad_add_fusion.pos
  58.5 0.7 dynamic-slice_bitcast_fusion.3
  59.2 2.2 %copy-done.2 = bf16[2048,1024]{1,0:T(8,128)(2,1)S(1)} copy-done((bf16[2048,1024]{1,0:T(8,128)(2,1)S(1)}, bf16[2048,1024]{1,0:T(8,128)(2,1)}, u32[]{:S(2)}) %copy-start.2) | copy-done | bytes 4194328
  61.4 3.5 %shard_map.73 = (f32[512,128]{1,0:T(8,128)S(1)}, f32[512,128]{1,0:T(8,128)S(1)}, f32[128,128]{1,0:T(8,128)S(1)}, f32[16,40,128]{2,1,0:T(8,128)S(1)}) custom-call(s32[4]{0:T(128)S(1)} %pad_add_fusion.pos, bf16[2,4,2,128,1024]{4,3,2,1,0:T(8,128)(2,1)S(1)} %bitcast.30, bf16[1024,384]{1,0:T(8,128)(2,1)S(1)} %constant_dynamic-update-slice_fusion.w0, ...), custom_call_target="tpu_custom_call" | custom-call | flops 1610612736 | bytes 6000000 | tf_op jit(solution)/shard_map/pallas_call | solution.py:137
  64.9 18.4 %all_to_all.10.edges = f32[16,40,128]{2,1,0:T(8,128)S(1)} all-to-all(f32[16,40,128]{2,1,0:T(8,128)S(1)} %get-tuple-element.26), channel_id=1, replica_groups=mesh['zh'=2,'yh'=2,'yl'=2,'x'=4,'c'=2,'zl'=4] {'yh','yl','x'}, dimensions={0} | all-to-all | bytes 655360 | tf_op jit(solution)/shard_map/all_to_all | solution.py:352
  83.3 1.0 shard_map.74
  84.4 26.1 %all_to_all.11.gates = bf16[16,128,128]{2,1,0:T(8,128)(2,1)S(1)} all-to-all(bf16[16,128,128]{2,1,0:T(8,128)(2,1)S(1)} %shard_map.74), channel_id=1, replica_groups=mesh['zh'=2,'yh'=2,'yl'=2,'x'=4,'c'=2,'zl'=4] {'zh','c','zl'}, dimensions={0} | all-to-all | bytes 1048576 | tf_op jit(solution)/shard_map/all_to_all | solution.py:354
  110.4 2.2 %copy-done.1 = bf16[32,128,512]{2,1,0:T(8,128)(2,1)S(1)} copy-done((bf16[32,128,512]{2,1,0:T(8,128)(2,1)S(1)}, bf16[32,128,512]{2,1,0:T(8,128)(2,1)}, u32[]{:S(2)}) %copy-start.1) | copy-done | bytes 4194328
  112.6 2.7 %shard_map.75 = bf16[128,1024]{1,0:T(8,128)(2,1)} custom-call(s32[4]{0:T(128)S(1)} %pad_add_fusion.pos, bf16[16,128,128]{2,1,0:T(8,128)(2,1)S(1)} %all_to_all.11.gates, bf16[4,2,2,2,2,64,512]{6,5,4,3,2,1,0:T(8,128)(2,1)S(1)} %bitcast.29), custom_call_target="tpu_custom_call" | custom-call | flops 536870912 | bytes 5000000 | tf_op jit(solution)/shard_map/pallas_call | solution.py:279
  (19 shorter events, 0.4 us)
Async XLA Ops:
  6.5 51.1 %copy-start = (f32[3,3,512]{2,1,0:T(4,128)S(1)}, f32[3,3,512]{2,1,0:T(4,128)}, u32[]{:S(2)}) copy-start(f32[3,3,512]{2,1,0:T(4,128)} %param.9) | copy-start | bytes 55300
  6.5 29.7 %copy-start.3 = (bf16[512,64]{0,1:T(8,128)(2,1)S(1)}, bf16[512,64]{0,1:T(8,128)(2,1)}, u32[]{:S(2)}) copy-start(bf16[512,64]{0,1:T(8,128)(2,1)} %param.13) | copy-start | bytes 196612
  6.5 52.6 %all-gather.5.cloned.1.call-start = ((), (), s32[]{:S(2)}) async-start(), calls=%async_computation.2 | async-start | bytes 4456448 | tf_op jit(solution)/shard_map/all_gather | solution.py:307
  7.3 103.1 %all-gather.7.cloned.1.call-start = ((), (), s32[]{:S(2)}) async-start(), calls=%async_computation.3 | async-start | bytes 4456448 | tf_op jit(solution)/shard_map/all_gather | solution.py:341
  8.7 8.7 %collective-permute-start = (bf16[64,384]{1,0:T(8,128)(2,1)S(1)}, bf16[64,384]{1,0:T(8,128)(2,1)S(1)}, u32[]{:S(2)}, u32[]{:S(2)}) collective-permute-start(bf16[64,384]{1,0:T(8,128)(2,1)S(1)} %get-tuple-element.41), channel_id=1, source_target_pairs={{0,4},{4,0},{128,132},{132,128},{1,5},{5,1},{129,133},{133,129},{2... | collective-permute-start | bytes 147464 | tf_op jit(solution)/shard_map/ppermute | solution.py:316
  12.0 7.5 %collective-permute-start.2 = (bf16[64,384]{1,0:T(8,128)(2,1)S(1)}, bf16[64,384]{1,0:T(8,128)(2,1)S(1)}, u32[]{:S(2)}, u32[]{:S(2)}) collective-permute-start(bf16[64,384]{1,0:T(8,128)(2,1)S(1)} %get-tuple-element.39), channel_id=1, source_target_pairs={{0,132},{4,128},{128,4},{132,0},{1,133},{5,129},{129,5},{133,1},{2... | collective-permute-start | bytes 147464 | tf_op jit(solution)/shard_map/ppermute | solution.py:316
  17.2 7.0 %collective-permute-start.1 = (bf16[64,384]{1,0:T(8,128)(2,1)S(1)}, bf16[64,384]{1,0:T(8,128)(2,1)S(1)}, u32[]{:S(2)}, u32[]{:S(2)}) collective-permute-start(bf16[64,384]{1,0:T(8,128)(2,1)S(1)} %get-tuple-element.40), channel_id=1, source_target_pairs={{0,128},{4,132},{128,0},{132,4},{1,129},{5,133},{129,1},{133,5},{2... | collective-permute-start | bytes 147464 | tf_op jit(solution)/shard_map/ppermute | solution.py:316
  24.2 6.3 %collective-permute-start.3 = (bf16[256,384]{1,0:T(8,128)(2,1)S(1)}, bf16[256,384]{1,0:T(8,128)(2,1)S(1)}, u32[]{:S(2)}, u32[]{:S(2)}) collective-permute-start(bf16[256,384]{1,0:T(8,128)(2,1)S(1)} %pad_maximum_fusion.1), channel_id=1, source_target_pairs={{0,8},{4,36},{8,16},{12,44},{16,24},{20,52},{24,0},{28,60},{32,40}... | collective-permute-start | bytes 589832 | tf_op jit(solution)/shard_map/ppermute | solution.py:35
  25.6 6.3 %collective-permute-start.4 = (bf16[256,384]{1,0:T(8,128)(2,1)S(1)}, bf16[256,384]{1,0:T(8,128)(2,1)S(1)}, u32[]{:S(2)}, u32[]{:S(2)}) collective-permute-start(bf16[256,384]{1,0:T(8,128)(2,1)S(1)} %pad_maximum_fusion.1), channel_id=1, source_target_pairs={{0,24},{4,100},{8,0},{12,108},{16,8},{20,116},{24,16},{28,124},{32... | collective-permute-start | bytes 589832 | tf_op jit(solution)/shard_map/ppermute | solution.py:35
  27.1 6.3 %collective-permute-start.5 = (bf16[256,384]{1,0:T(8,128)(2,1)S(1)}, bf16[256,384]{1,0:T(8,128)(2,1)S(1)}, u32[]{:S(2)}, u32[]{:S(2)}) collective-permute-start(bf16[256,384]{1,0:T(8,128)(2,1)S(1)} %pad_maximum_fusion.1), channel_id=1, source_target_pairs={{0,16},{4,68},{8,24},{12,76},{16,0},{20,84},{24,8},{28,92},{32,48}... | collective-permute-start | bytes 589832 | tf_op jit(solution)/shard_map/ppermute | solution.py:35
  33.5 11.7 %collective-permute-start.7 = (bf16[1024,384]{1,0:T(8,128)(2,1)S(1)}, bf16[1024,384]{1,0:T(8,128)(2,1)S(1)}, u32[]{:S(2)}, u32[]{:S(2)}) collective-permute-start(bf16[1024,384]{1,0:T(8,128)(2,1)S(1)} %constant_dynamic-update-slice_fusion.w0), channel_id=1, source_target_pairs={{0,96},{4,28},{8,104},{12,4},{16,112},{20,12},{24,120},{28,20},{32... | collective-permute-start | bytes 2359304 | tf_op jit(solution)/shard_map/ppermute | solution.py:35
  36.3 12.5 %collective-permute-start.6 = (bf16[1024,384]{1,0:T(8,128)(2,1)S(1)}, bf16[1024,384]{1,0:T(8,128)(2,1)S(1)}, u32[]{:S(2)}, u32[]{:S(2)}) collective-permute-start(bf16[1024,384]{1,0:T(8,128)(2,1)S(1)} %constant_dynamic-update-slice_fusion.w0), channel_id=1, source_target_pairs={{0,32},{4,12},{8,40},{12,20},{16,48},{20,28},{24,56},{28,4},{32,64... | collective-permute-start | bytes 2359304 | tf_op jit(solution)/shard_map/ppermute | solution.py:35
  36.3 5.4 %collective-permute-start.9 = (bf16[64,512]{1,0:T(8,128)(2,1)S(1)}, bf16[64,512]{1,0:T(8,128)(2,1)S(1)}, u32[]{:S(2)}, u32[]{:S(2)}) collective-permute-start(bf16[64,512]{1,0:T(8,128)(2,1)S(1)} %bitcast.34), channel_id=1, source_target_pairs={{0,128},{1,192},{2,0},{3,64},{4,132},{5,196},{6,4},{7,68},{8,136},... | collective-permute-start | bytes 196616 | tf_op jit(solution)/shard_map/ppermute | solution.py:330
  37.7 4.1 %collective-permute-start.8 = (bf16[64,512]{1,0:T(8,128)(2,1)S(1)}, bf16[64,512]{1,0:T(8,128)(2,1)S(1)}, u32[]{:S(2)}, u32[]{:S(2)}) collective-permute-start(bf16[64,512]{1,0:T(8,128)(2,1)S(1)} %bitcast.35), channel_id=1, source_target_pairs={{0,0},{1,64},{2,128},{3,192},{4,4},{5,68},{6,132},{7,196},{8,8},{9... | collective-permute-start | bytes 196616 | tf_op jit(solution)/shard_map/ppermute | solution.py:330
  48.8 7.9 %collective-permute-start.11 = (bf16[512,384]{1,0:T(8,128)(2,1)S(1)}, bf16[512,384]{1,0:T(8,128)(2,1)S(1)}, u32[]{:S(2)}, u32[]{:S(2)}) collective-permute-start(bf16[512,384]{1,0:T(8,128)(2,1)S(1)} %slice.7), channel_id=1, source_target_pairs={{0,96},{4,28},{8,104},{12,4},{16,112},{20,12},{24,120},{28,20},{32... | collective-permute-start | bytes 1179656 | tf_op jit(solution)/shard_map/ppermute | solution.py:35
  48.9 7.9 %collective-permute-start.10 = (bf16[512,384]{1,0:T(8,128)(2,1)S(1)}, bf16[512,384]{1,0:T(8,128)(2,1)S(1)}, u32[]{:S(2)}, u32[]{:S(2)}) collective-permute-start(bf16[512,384]{1,0:T(8,128)(2,1)S(1)} %slice.6), channel_id=1, source_target_pairs={{0,32},{4,12},{8,40},{12,20},{16,48},{20,28},{24,56},{28,4},{32,64... | collective-permute-start | bytes 1179656 | tf_op jit(solution)/shard_map/ppermute | solution.py:35
  50.4 6.3 %collective-permute-start.12 = (bf16[128,512]{1,0:T(8,128)(2,1)S(1)}, bf16[128,512]{1,0:T(8,128)(2,1)S(1)}, u32[]{:S(2)}, u32[]{:S(2)}) collective-permute-start(bf16[128,512]{1,0:T(8,128)(2,1)S(1)} %constant_dynamic-update-slice_fusion.7), channel_id=1, source_target_pairs={{0,64},{64,0},{1,65},{65,1},{2,66},{66,2},{3,67},{67,3},{4,68},{68... | collective-permute-start | bytes 393224 | tf_op jit(solution)/shard_map/ppermute | solution.py:335
  59.2 2.2 %copy-start.2 = (bf16[2048,1024]{1,0:T(8,128)(2,1)S(1)}, bf16[2048,1024]{1,0:T(8,128)(2,1)}, u32[]{:S(2)}) copy-start(bf16[2048,1024]{1,0:T(8,128)(2,1)} %all-gather.5.cloned.1.call-done) | copy-start | bytes 12582916
  110.4 2.2 %copy-start.1 = (bf16[32,128,512]{2,1,0:T(8,128)(2,1)S(1)}, bf16[32,128,512]{2,1,0:T(8,128)(2,1)}, u32[]{:S(2)}) copy-start(bf16[32,128,512]{2,1,0:T(8,128)(2,1)} %all-gather.7.cloned.1.call-done) | copy-start | bytes 12582916
Sparse Core Ops, SparseCore 0:
  9.2 49.8 all-gather.4
  61.0 44.3 all-gather.6

commit v4 on v3

--- a/solution.py
+++ b/solution.py
@@ -30,7 +30,7 @@
 def crossed(block, phase, distance):
     route = []
     for y, x, c in np.ndindex(4, 4, 2):
-        target = (y, (x + distance) % 4, c) if c == phase else ((y + distance) % 4, x, c)
+        target = (y, (x + distance) % 4, c) if c != phase else ((y + distance) % 4, x, c)
         route.append((int(np.ravel_multi_index((y, x, c), (4, 4, 2))), int(np.ravel_multi_index(target, (4, 4, 2)))))
     return lax.ppermute(block, PLANE + ("c",), route)
 
@@ -62,8 +62,8 @@
     def features(outer, inner, half):
         first = RING_ORDER[outer] + 4
         second = RING_ORDER[inner] + 4
-        at_y = lax.rem(own_y + jnp.where(own_c == 0, first, second), 4)
-        at_x = lax.rem(own_x + jnp.where(own_c == 0, second, first), 4)
+        at_y = lax.rem(own_y + jnp.where(own_c == 1, first, second), 4)
+        at_x = lax.rem(own_x + jnp.where(own_c == 1, second, first), 4)
         at_zh = own_zh if half == 0 else 1 - own_zh
         zl = at_zh * 2 + at_y // 2
         lane = pl.multiple_of((lax.rem(at_y, 2) * 4 + at_x) * 128, 128)
@@ -288,6 +288,25 @@
     )(pos, gates, weights)
 
 
+def split_kernel(weight, *parts):
+    group = lax.axis_index("zh") * 2 + lax.axis_index("c")
+    for flip, part in enumerate(parts):
+        lane = pl.multiple_of((group ^ flip) * LANES, LANES)
+        for s in range(3):
+            part[:, s * LANES : (s + 1) * LANES] = weight[s, :, pl.ds(lane, LANES)]
+
+
+def split(in_weight):
+    vmem = pl.BlockSpec(memory_space=pltpu.VMEM)
+    return pl.pallas_call(
+        split_kernel,
+        out_shape=(jax.ShapeDtypeStruct((GROUP, WIDE), BF16),) * 4,
+        in_specs=[vmem],
+        out_specs=(vmem,) * 4,
+        compiler_params=pltpu.CompilerParams(vmem_limit_bytes=8 * 1024 * 1024),
+    )(in_weight)
+
+
 def transposed_routes():
     routes = [[], []]
     for zh, yh, yl, x, c, zl in np.ndindex(*SIZES):
@@ -307,13 +326,12 @@
     slabs = lax.all_gather(tokens, ("zh", "zl", "c"), axis=0, tiled=False)
     slabs = slabs.reshape(2, 4, 2, HALF, 1024)
 
-    quarters = in_weight.reshape(3, GROUP, 4, LANES).transpose(2, 1, 0, 3).reshape(4, GROUP, WIDE)
+    quarters = split(in_weight)
 
     def quarter(flip):
-        part = lax.dynamic_index_in_dim(quarters, group ^ flip, 0, keepdims=False)
         if flip == 0:
-            return part
-        return lax.ppermute(part, ("zh", "c"), [(i, i ^ flip) for i in range(4)])
+            return quarters[0]
+        return lax.ppermute(quarters[flip], ("zh", "c"), [(i, i ^ flip) for i in range(4)])
 
     def in_order(own, other):
         first = jnp.where(c == 0, own, other)
@@ -324,15 +342,26 @@
     near = in_order(quarter(0), quarter(1))
     gathered_once = jnp.concatenate(direct(jnp.concatenate([near, far], axis=0), 0), axis=0)
 
+    def own_channels(table, axis):
+        return lax.dynamic_slice_in_dim(table, group * LANES, LANES, axis)
+
+    taps = own_channels(short_weight, 2).reshape(9, LANES)
+    rates = own_channels(decay_rates, 0).T
+    weights = own_channels(residues, 0).T
+    skip = own_channels(skip_gain, 0)[None]
+
     half = gathered_once.shape[0] // 2
     low = crossed(gathered_once, 1, 1)
     high = crossed(gathered_once, 1, -1)
     moved = [lax.ppermute(out_weight.T, AXES, route) for route in transposed_routes()]
-    low, high, moved = lax.optimization_barrier((low, high, moved))
+    tables = (pos, taps, rates, weights, skip)
+    low, high, moved, tables = lax.optimization_barrier((low, high, moved, tables))
+    pos, taps, rates, weights, skip = tables
     moved = jnp.concatenate(moved, axis=0)
     far_low = crossed(low[:half], 1, 1)
     far_high = crossed(high[half:], 1, -1)
     flipped = lax.ppermute(moved, "yh", [(0, 1), (1, 0)])
+    far_low, far_high, slabs = lax.optimization_barrier((far_low, far_high, slabs))
     far_low, far_high, flipped = lax.optimization_barrier((far_low, far_high, flipped))
     in_weights = [gathered_once, low, high, far_low, far_high]
 
@@ -341,13 +370,6 @@
     gathered = lax.all_gather(jnp.stack([moved, flipped]), ("x", "yl", "c"), axis=0, tiled=False)
     gathered = gathered.reshape(4, 2, 2, 2, 2, GROUP, 512)
 
-    def own_channels(table, axis):
-        return lax.dynamic_slice_in_dim(table, group * LANES, LANES, axis)
-
-    taps = own_channels(short_weight, 2).reshape(9, LANES)
-    rates = own_channels(decay_rates, 0).T
-    weights = own_channels(residues, 0).T
-    skip = own_channels(skip_gain, 0)[None]
     mixed, gate, sub_states, edges = front(pos, slabs, in_weights, taps, rates, weights, skip)
     edges = lax.all_to_all(edges, PLANE, split_axis=0, concat_axis=0, tiled=True)
     gate_out = back(pos, edges, sub_states, mixed, gate, rates, weights, skip)

time: 123 us -> 121 us (0.984)
  blocking collectives: 44.5 us -> 38.2 us
  waiting for transfers between devices: 25 us -> 30.4 us
    ppermute x7, waiting for transfers between devices: 11.8 us -> 20.9 us  [crossed(): return lax.ppermute(block, PLANE + ('c',), route)]
    all_to_all x1, blocking collectives: 26.1 us -> 22.7 us  [shards(): lax.all_to_all(gate_out, ('zh', 'c', 'zl'), split_axis=0, concat_axis=0,...]
    all_to_all x1, blocking collectives: 18.4 us -> 15.5 us  [shards(): lax.all_to_all(edges, PLANE, split_axis=0, concat_axis=0, tiled=True)]
    ppermute x1, starting transfers between devices: 3.96 us -> 1.55 us  [shards(): flipped = lax.ppermute(moved, 'yh', [(0, 1), (1, 0)])]
    ppermute x1, waiting for transfers between devices: 2.36 us -> 0.01 us  [shards(): flipped = lax.ppermute(moved, 'yh', [(0, 1), (1, 0)])]
    ppermute x2, waiting for transfers between devices: 3.39 us -> 1.61 us  [shards(): lax.ppermute(out_weight.T, AXES, route)]
    reshape x3 -> x0, local copies, waits for them, and re-layouts: 1.32 us -> none  [shards(): in_weight.reshape(3, GROUP, 4, LANES).transpose(2, 1, 0, 3)]
  transfers between devices with their start and end apart: 15 -> 15, of which waited for: 10 -> 10; matrix products, arithmetic and copies ran while one was open for 3% -> 2% of each run, Pallas kernels for 4% -> 4%
where the time goes in v4:
time: 121 us; the launch traced here: 120 us
  blocking collectives  38.2 us (32%)
  waiting for transfers between devices  30.4 us (25%)
  starting transfers between devices  22.3 us (18%)
  between operations  13.5 us (11%)
  Pallas kernels  7.29 us (6%)
  local copies, waits for them, and re-layouts  6.96 us (6%)
    all_to_all x1, blocking collectives, shards(): lax.all_to_all(gate_out, ('zh', 'c', 'zl'), split_axis=0, concat_axis=0,...  22.7 us
    ppermute x7, waiting for transfers between devices, crossed(): return lax.ppermute(block, PLANE + ('c',), route)  20.9 us
    all_to_all x1, blocking collectives, shards(): lax.all_to_all(edges, PLANE, split_axis=0, concat_axis=0, tiled=True)  15.5 us
    ppermute x7, starting transfers between devices, crossed(): return lax.ppermute(block, PLANE + ('c',), route)  9.45 us
    ppermute x3, starting transfers between devices, quarter(): lax.ppermute(quarters[flip], ('zh', 'c'), [(i, i ^ flip) for i in range(4)])  8.97 us
    ppermute x3, waiting for transfers between devices, quarter(): lax.ppermute(quarters[flip], ('zh', 'c'), [(i, i ^ flip) for i in range(4)])  7.23 us
    unnamed x11, local copies, waits for them, and re-layouts  5.36 us
    pallas_call x1, Pallas kernels, front(): pl.pallas_call(front_kernel, out_shape=(jax.ShapeDtypeStruct((2 * BLOCK,...  3.54 us
  transfers between devices with their start and end apart: 15, of which 10 were waited for; matrix products, arithmetic and copies ran while one was open for 2% of the time, Pallas kernels for 4%

profile of v4, /device:TPU:1, one launch (start us, length us, event | category | flops | bytes accessed | tf_op | source)
XLA Modules:
  0.0 119.7 jit_solution(14273602413055423739)
XLA Ops:
  6.5 0.0 copy-start
  6.5 0.0 all-gather.5.cloned.1.call-start
  6.5 0.7 all-gather.5.cloned.1.call-update
  7.3 0.0 all-gather.7.cloned.1.call-start
  7.3 0.0 copy-start.3
  7.3 0.9 copy-done.3
  8.3 3.3 %collective-permute-start = (bf16[64,384]{1,0:T(8,128)(2,1)S(1)}, bf16[64,384]{1,0:T(8,128)(2,1)S(1)}, u32[]{:S(2)}, u32[]{:S(2)}) collective-permute-start(bf16[64,384]{1,0:T(8,128)(2,1)S(1)} %get-tuple-element.31), channel_id=1, source_target_pairs={{0,4},{4,0},{128,132},{132,128},{1,5},{5,1},{129,133},{133,129},{2... | collective-permute-start | bytes 147464 | tf_op jit(solution)/shard_map/ppermute | solution.py:334
  11.6 5.2 %collective-permute-start.1 = (bf16[64,384]{1,0:T(8,128)(2,1)S(1)}, bf16[64,384]{1,0:T(8,128)(2,1)S(1)}, u32[]{:S(2)}, u32[]{:S(2)}) collective-permute-start(bf16[64,384]{1,0:T(8,128)(2,1)S(1)} %get-tuple-element.32), channel_id=1, source_target_pairs={{0,128},{4,132},{128,0},{132,4},{1,129},{5,133},{129,1},{133,5},{2... | collective-permute-start | bytes 147464 | tf_op jit(solution)/shard_map/ppermute | solution.py:334
  16.8 0.4 collective-permute-start.2
  17.2 0.0 collective-permute-done
  17.3 1.3 %collective-permute-done.1 = bf16[64,384]{1,0:T(8,128)(2,1)S(1)} collective-permute-done((bf16[64,384]{1,0:T(8,128)(2,1)S(1)}, bf16[64,384]{1,0:T(8,128)(2,1)S(1)}, u32[]{:S(2)}, u32[]{:S(2)}) %collective-permute-start.1) | collective-permute-done | bytes 49184 | tf_op jit(solution)/shard_map/ppermute | solution.py:334
  18.6 5.9 %collective-permute-done.2 = bf16[64,384]{1,0:T(8,128)(2,1)S(1)} collective-permute-done((bf16[64,384]{1,0:T(8,128)(2,1)S(1)}, bf16[64,384]{1,0:T(8,128)(2,1)S(1)}, u32[]{:S(2)}, u32[]{:S(2)}) %collective-permute-start.2) | collective-permute-done | bytes 49184 | tf_op jit(solution)/shard_map/ppermute | solution.py:334
  24.6 1.4 %collective-permute-start.3 = (bf16[256,384]{1,0:T(8,128)(2,1)S(1)}, bf16[256,384]{1,0:T(8,128)(2,1)S(1)}, u32[]{:S(2)}, u32[]{:S(2)}) collective-permute-start(bf16[256,384]{1,0:T(8,128)(2,1)S(1)} %pad_maximum_fusion.1), channel_id=1, source_target_pairs={{0,32},{4,12},{8,40},{12,20},{16,48},{20,28},{24,56},{28,4},{32,64... | collective-permute-start | bytes 589832 | tf_op jit(solution)/shard_map/ppermute | solution.py:35
  26.0 1.4 %collective-permute-start.4 = (bf16[256,384]{1,0:T(8,128)(2,1)S(1)}, bf16[256,384]{1,0:T(8,128)(2,1)S(1)}, u32[]{:S(2)}, u32[]{:S(2)}) collective-permute-start(bf16[256,384]{1,0:T(8,128)(2,1)S(1)} %pad_maximum_fusion.1), channel_id=1, source_target_pairs={{0,96},{4,28},{8,104},{12,4},{16,112},{20,12},{24,120},{28,20},{32... | collective-permute-start | bytes 589832 | tf_op jit(solution)/shard_map/ppermute | solution.py:35
  27.4 1.6 %collective-permute-start.5 = (bf16[256,384]{1,0:T(8,128)(2,1)S(1)}, bf16[256,384]{1,0:T(8,128)(2,1)S(1)}, u32[]{:S(2)}, u32[]{:S(2)}) collective-permute-start(bf16[256,384]{1,0:T(8,128)(2,1)S(1)} %pad_maximum_fusion.1), channel_id=1, source_target_pairs={{0,64},{4,20},{8,72},{12,28},{16,80},{20,4},{24,88},{28,12},{32,96... | collective-permute-start | bytes 589832 | tf_op jit(solution)/shard_map/ppermute | solution.py:35
  29.0 1.8 %collective-permute-done.3 = bf16[256,384]{1,0:T(8,128)(2,1)S(1)} collective-permute-done((bf16[256,384]{1,0:T(8,128)(2,1)S(1)}, bf16[256,384]{1,0:T(8,128)(2,1)S(1)}, u32[]{:S(2)}, u32[]{:S(2)}) %collective-permute-start.3) | collective-permute-done | bytes 196640 | tf_op jit(solution)/shard_map/ppermute | solution.py:35
  30.8 0.1 collective-permute-done.4
  31.0 2.9 %collective-permute-done.5 = bf16[256,384]{1,0:T(8,128)(2,1)S(1)} collective-permute-done((bf16[256,384]{1,0:T(8,128)(2,1)S(1)}, bf16[256,384]{1,0:T(8,128)(2,1)S(1)}, u32[]{:S(2)}, u32[]{:S(2)}) %collective-permute-start.5) | collective-permute-done | bytes 196640 | tf_op jit(solution)/shard_map/ppermute | solution.py:35
  34.0 2.8 %collective-permute-start.7 = (bf16[1024,384]{1,0:T(8,128)(2,1)S(1)}, bf16[1024,384]{1,0:T(8,128)(2,1)S(1)}, u32[]{:S(2)}, u32[]{:S(2)}) collective-permute-start(bf16[1024,384]{1,0:T(8,128)(2,1)S(1)} %constant_dynamic-update-slice_fusion.w0), channel_id=1, source_target_pairs={{0,24},{4,100},{8,0},{12,108},{16,8},{20,116},{24,16},{28,124},{32... | collective-permute-start | bytes 2359304 | tf_op jit(solution)/shard_map/ppermute | solution.py:35
  36.8 0.0 collective-permute-start.6
  36.8 0.8 collective-permute-start.9
  37.6 1.5 %collective-permute-start.8 = (bf16[64,512]{1,0:T(8,128)(2,1)}, bf16[64,512]{1,0:T(8,128)(2,1)S(1)}, u32[]{:S(2)}, u32[]{:S(2)}) collective-permute-start(bf16[64,512]{1,0:T(8,128)(2,1)} %bitcast.20), channel_id=1, source_target_pairs={{0,0},{1,64},{2,128},{3,192},{4,4},{5,68},{6,132},{7,196},{8,8},{9... | collective-permute-start | bytes 196616 | tf_op jit(solution)/shard_map/ppermute | solution.py:356
  39.1 0.0 copy-done
  39.1 0.8 dynamic-slice_bitcast_fusion.2.skip
  39.9 0.7 dynamic-slice_bitcast_fusion
  40.6 0.1 pad_add_fusion.pos
  40.7 1.6 %collective-permute-done.9 = bf16[64,512]{1,0:T(8,128)(2,1)S(1)} collective-permute-done((bf16[64,512]{1,0:T(8,128)(2,1)}, bf16[64,512]{1,0:T(8,128)(2,1)S(1)}, u32[]{:S(2)}, u32[]{:S(2)}) %collective-permute-start.9) | collective-permute-done | bytes 65568 | tf_op jit(solution)/shard_map/ppermute | solution.py:356
  42.3 0.0 collective-permute-done.8
  42.3 5.6 %collective-permute-done.7.w2 = bf16[1024,384]{1,0:T(8,128)(2,1)S(1)} collective-permute-done((bf16[1024,384]{1,0:T(8,128)(2,1)S(1)}, bf16[1024,384]{1,0:T(8,128)(2,1)S(1)}, u32[]{:S(2)}, u32[]{:S(2)}) %collective-permute-start.7) | collective-permute-done | bytes 786464 | tf_op jit(solution)/shard_map/ppermute | solution.py:35
  47.9 1.4 %collective-permute-done.6.w1 = bf16[1024,384]{1,0:T(8,128)(2,1)S(1)} collective-permute-done((bf16[1024,384]{1,0:T(8,128)(2,1)S(1)}, bf16[1024,384]{1,0:T(8,128)(2,1)S(1)}, u32[]{:S(2)}, u32[]{:S(2)}) %collective-permute-start.6) | collective-permute-done | bytes 786464 | tf_op jit(solution)/shard_map/ppermute | solution.py:35
  49.3 2.2 %collective-permute-start.11 = (bf16[512,384]{1,0:T(8,128)(2,1)S(1)}, bf16[512,384]{1,0:T(8,128)(2,1)S(1)}, u32[]{:S(2)}, u32[]{:S(2)}) collective-permute-start(bf16[512,384]{1,0:T(8,128)(2,1)S(1)} %slice.7), channel_id=1, source_target_pairs={{0,24},{4,100},{8,0},{12,108},{16,8},{20,116},{24,16},{28,124},{32... | collective-permute-start | bytes 1179656 | tf_op jit(solution)/shard_map/ppermute | solution.py:35
  51.5 0.0 collective-permute-start.10
  51.6 1.6 %collective-permute-start.12 = (bf16[128,512]{1,0:T(8,128)(2,1)S(1)}, bf16[128,512]{1,0:T(8,128)(2,1)S(1)}, u32[]{:S(2)}, u32[]{:S(2)}) collective-permute-start(bf16[128,512]{1,0:T(8,128)(2,1)S(1)} %constant_dynamic-update-slice_fusion.7), channel_id=1, source_target_pairs={{0,64},{64,0},{1,65},{65,1},{2,66},{66,2},{3,67},{67,3},{4,68},{68... | collective-permute-start | bytes 393224 | tf_op jit(solution)/shard_map/ppermute | solution.py:363
  53.1 4.5 %collective-permute-done.11.w4 = bf16[512,384]{1,0:T(8,128)(2,1)S(1)} collective-permute-done((bf16[512,384]{1,0:T(8,128)(2,1)S(1)}, bf16[512,384]{1,0:T(8,128)(2,1)S(1)}, u32[]{:S(2)}, u32[]{:S(2)}) %collective-permute-start.11) | collective-permute-done | bytes 393248 | tf_op jit(solution)/shard_map/ppermute | solution.py:35
  57.7 4.5 %collective-permute-done.10.w3 = bf16[512,384]{1,0:T(8,128)(2,1)S(1)} collective-permute-done((bf16[512,384]{1,0:T(8,128)(2,1)S(1)}, bf16[512,384]{1,0:T(8,128)(2,1)S(1)}, u32[]{:S(2)}, u32[]{:S(2)}) %collective-permute-start.10) | collective-permute-done | bytes 393248 | tf_op jit(solution)/shard_map/ppermute | solution.py:35
  62.2 0.0 all-gather.5.cloned.1.call-done
  62.2 0.0 collective-permute-done.12
  62.2 0.7 pad_maximum_fusion
  62.9 0.0 all-gather.7.cloned.1.call-update
  62.9 0.0 copy-start.2
  62.9 2.2 %copy-done.2 = bf16[2048,1024]{1,0:T(8,128)(2,1)S(1)} copy-done((bf16[2048,1024]{1,0:T(8,128)(2,1)S(1)}, bf16[2048,1024]{1,0:T(8,128)(2,1)}, u32[]{:S(2)}) %copy-start.2) | copy-done | bytes 4194328
  65.1 3.5 %shard_map.74 = (f32[512,128]{1,0:T(8,128)S(1)}, f32[512,128]{1,0:T(8,128)S(1)}, f32[128,128]{1,0:T(8,128)S(1)}, f32[16,40,128]{2,1,0:T(8,128)S(1)}) custom-call(s32[4]{0:T(128)S(1)} %pad_add_fusion.pos, bf16[2,4,2,128,1024]{4,3,2,1,0:T(8,128)(2,1)S(1)} %bitcast.16, bf16[1024,384]{1,0:T(8,128)(2,1)S(1)} %constant_dynamic-update-slice_fusion.w0, ...), custom_call_target="tpu_custom_call" | custom-call | flops 1610612736 | bytes 6000000 | tf_op jit(solution)/shard_map/pallas_call | solution.py:137
  68.7 15.5 %all_to_all.10.edges = f32[16,40,128]{2,1,0:T(8,128)S(1)} all-to-all(f32[16,40,128]{2,1,0:T(8,128)S(1)} %get-tuple-element.50), channel_id=1, replica_groups=mesh['zh'=2,'yh'=2,'yl'=2,'x'=4,'c'=2,'zl'=4] {'yh','yl','x'}, dimensions={0} | all-to-all | bytes 655360 | tf_op jit(solution)/shard_map/all_to_all | solution.py:374
  84.2 1.0 shard_map.75
  85.2 22.7 %all_to_all.11.gates = bf16[16,128,128]{2,1,0:T(8,128)(2,1)S(1)} all-to-all(bf16[16,128,128]{2,1,0:T(8,128)(2,1)S(1)} %shard_map.75), channel_id=1, replica_groups=mesh['zh'=2,'yh'=2,'yl'=2,'x'=4,'c'=2,'zl'=4] {'zh','c','zl'}, dimensions={0} | all-to-all | bytes 1048576 | tf_op jit(solution)/shard_map/all_to_all | solution.py:376
  107.9 0.0 all-gather.7.cloned.1.call-done
  107.9 2.2 %copy-done.1 = bf16[32,128,512]{2,1,0:T(8,128)(2,1)S(1)} copy-done((bf16[32,128,512]{2,1,0:T(8,128)(2,1)S(1)}, bf16[32,128,512]{2,1,0:T(8,128)(2,1)}, u32[]{:S(2)}) %copy-start.1) | copy-done | bytes 4194328
  110.1 2.7 %shard_map.76 = bf16[128,1024]{1,0:T(8,128)(2,1)} custom-call(s32[4]{0:T(128)S(1)} %pad_add_fusion.pos, bf16[16,128,128]{2,1,0:T(8,128)(2,1)S(1)} %all_to_all.11.gates, bf16[4,2,2,2,2,64,512]{6,5,4,3,2,1,0:T(8,128)(2,1)S(1)} %bitcast.15), custom_call_target="tpu_custom_call" | custom-call | flops 536870912 | bytes 5000000 | tf_op jit(solution)/shard_map/pallas_call | solution.py:279
  (16 shorter events, 0.4 us)
Async XLA Ops:
  6.5 32.6 %copy-start = (f32[3,3,512]{2,1,0:T(4,128)S(1)}, f32[3,3,512]{2,1,0:T(4,128)}, u32[]{:S(2)}) copy-start(f32[3,3,512]{2,1,0:T(4,128)} %param.9) | copy-start | bytes 55300
  6.5 55.6 %all-gather.5.cloned.1.call-start = ((), (), s32[]{:S(2)}) async-start(), calls=%async_computation.2 | async-start | bytes 4456448 | tf_op jit(solution)/shard_map/all_gather | solution.py:326
  7.3 100.7 %all-gather.7.cloned.1.call-start = ((), (), s32[]{:S(2)}) async-start(), calls=%async_computation.3 | async-start | bytes 4456448 | tf_op jit(solution)/shard_map/all_gather | solution.py:370
  7.3 0.9 copy-start.3
  8.3 9.0 %collective-permute-start = (bf16[64,384]{1,0:T(8,128)(2,1)S(1)}, bf16[64,384]{1,0:T(8,128)(2,1)S(1)}, u32[]{:S(2)}, u32[]{:S(2)}) collective-permute-start(bf16[64,384]{1,0:T(8,128)(2,1)S(1)} %get-tuple-element.31), channel_id=1, source_target_pairs={{0,4},{4,0},{128,132},{132,128},{1,5},{5,1},{129,133},{133,129},{2... | collective-permute-start | bytes 147464 | tf_op jit(solution)/shard_map/ppermute | solution.py:334
  11.6 7.0 %collective-permute-start.1 = (bf16[64,384]{1,0:T(8,128)(2,1)S(1)}, bf16[64,384]{1,0:T(8,128)(2,1)S(1)}, u32[]{:S(2)}, u32[]{:S(2)}) collective-permute-start(bf16[64,384]{1,0:T(8,128)(2,1)S(1)} %get-tuple-element.32), channel_id=1, source_target_pairs={{0,128},{4,132},{128,0},{132,4},{1,129},{5,133},{129,1},{133,5},{2... | collective-permute-start | bytes 147464 | tf_op jit(solution)/shard_map/ppermute | solution.py:334
  16.8 7.7 %collective-permute-start.2 = (bf16[64,384]{1,0:T(8,128)(2,1)S(1)}, bf16[64,384]{1,0:T(8,128)(2,1)S(1)}, u32[]{:S(2)}, u32[]{:S(2)}) collective-permute-start(bf16[64,384]{1,0:T(8,128)(2,1)S(1)} %get-tuple-element.33), channel_id=1, source_target_pairs={{0,132},{4,128},{128,4},{132,0},{1,133},{5,129},{129,5},{133,1},{2... | collective-permute-start | bytes 147464 | tf_op jit(solution)/shard_map/ppermute | solution.py:334
  24.6 6.2 %collective-permute-start.3 = (bf16[256,384]{1,0:T(8,128)(2,1)S(1)}, bf16[256,384]{1,0:T(8,128)(2,1)S(1)}, u32[]{:S(2)}, u32[]{:S(2)}) collective-permute-start(bf16[256,384]{1,0:T(8,128)(2,1)S(1)} %pad_maximum_fusion.1), channel_id=1, source_target_pairs={{0,32},{4,12},{8,40},{12,20},{16,48},{20,28},{24,56},{28,4},{32,64... | collective-permute-start | bytes 589832 | tf_op jit(solution)/shard_map/ppermute | solution.py:35
  26.0 4.9 %collective-permute-start.4 = (bf16[256,384]{1,0:T(8,128)(2,1)S(1)}, bf16[256,384]{1,0:T(8,128)(2,1)S(1)}, u32[]{:S(2)}, u32[]{:S(2)}) collective-permute-start(bf16[256,384]{1,0:T(8,128)(2,1)S(1)} %pad_maximum_fusion.1), channel_id=1, source_target_pairs={{0,96},{4,28},{8,104},{12,4},{16,112},{20,12},{24,120},{28,20},{32... | collective-permute-start | bytes 589832 | tf_op jit(solution)/shard_map/ppermute | solution.py:35
  27.4 6.5 %collective-permute-start.5 = (bf16[256,384]{1,0:T(8,128)(2,1)S(1)}, bf16[256,384]{1,0:T(8,128)(2,1)S(1)}, u32[]{:S(2)}, u32[]{:S(2)}) collective-permute-start(bf16[256,384]{1,0:T(8,128)(2,1)S(1)} %pad_maximum_fusion.1), channel_id=1, source_target_pairs={{0,64},{4,20},{8,72},{12,28},{16,80},{20,4},{24,88},{28,12},{32,96... | collective-permute-start | bytes 589832 | tf_op jit(solution)/shard_map/ppermute | solution.py:35
  34.0 13.9 %collective-permute-start.7 = (bf16[1024,384]{1,0:T(8,128)(2,1)S(1)}, bf16[1024,384]{1,0:T(8,128)(2,1)S(1)}, u32[]{:S(2)}, u32[]{:S(2)}) collective-permute-start(bf16[1024,384]{1,0:T(8,128)(2,1)S(1)} %constant_dynamic-update-slice_fusion.w0), channel_id=1, source_target_pairs={{0,24},{4,100},{8,0},{12,108},{16,8},{20,116},{24,16},{28,124},{32... | collective-permute-start | bytes 2359304 | tf_op jit(solution)/shard_map/ppermute | solution.py:35
  36.8 12.5 %collective-permute-start.6 = (bf16[1024,384]{1,0:T(8,128)(2,1)S(1)}, bf16[1024,384]{1,0:T(8,128)(2,1)S(1)}, u32[]{:S(2)}, u32[]{:S(2)}) collective-permute-start(bf16[1024,384]{1,0:T(8,128)(2,1)S(1)} %constant_dynamic-update-slice_fusion.w0), channel_id=1, source_target_pairs={{0,8},{4,36},{8,16},{12,44},{16,24},{20,52},{24,0},{28,60},{32,40}... | collective-permute-start | bytes 2359304 | tf_op jit(solution)/shard_map/ppermute | solution.py:35
  36.8 5.5 %collective-permute-start.9 = (bf16[64,512]{1,0:T(8,128)(2,1)}, bf16[64,512]{1,0:T(8,128)(2,1)S(1)}, u32[]{:S(2)}, u32[]{:S(2)}) collective-permute-start(bf16[64,512]{1,0:T(8,128)(2,1)} %bitcast.19), channel_id=1, source_target_pairs={{0,128},{1,192},{2,0},{3,64},{4,132},{5,196},{6,4},{7,68},{8,136},... | collective-permute-start | bytes 196616 | tf_op jit(solution)/shard_map/ppermute | solution.py:356
  37.6 4.7 %collective-permute-start.8 = (bf16[64,512]{1,0:T(8,128)(2,1)}, bf16[64,512]{1,0:T(8,128)(2,1)S(1)}, u32[]{:S(2)}, u32[]{:S(2)}) collective-permute-start(bf16[64,512]{1,0:T(8,128)(2,1)} %bitcast.20), channel_id=1, source_target_pairs={{0,0},{1,64},{2,128},{3,192},{4,4},{5,68},{6,132},{7,196},{8,8},{9... | collective-permute-start | bytes 196616 | tf_op jit(solution)/shard_map/ppermute | solution.py:356
  49.3 8.3 %collective-permute-start.11 = (bf16[512,384]{1,0:T(8,128)(2,1)S(1)}, bf16[512,384]{1,0:T(8,128)(2,1)S(1)}, u32[]{:S(2)}, u32[]{:S(2)}) collective-permute-start(bf16[512,384]{1,0:T(8,128)(2,1)S(1)} %slice.7), channel_id=1, source_target_pairs={{0,24},{4,100},{8,0},{12,108},{16,8},{20,116},{24,16},{28,124},{32... | collective-permute-start | bytes 1179656 | tf_op jit(solution)/shard_map/ppermute | solution.py:35
  51.5 10.6 %collective-permute-start.10 = (bf16[512,384]{1,0:T(8,128)(2,1)S(1)}, bf16[512,384]{1,0:T(8,128)(2,1)S(1)}, u32[]{:S(2)}, u32[]{:S(2)}) collective-permute-start(bf16[512,384]{1,0:T(8,128)(2,1)S(1)} %slice.6), channel_id=1, source_target_pairs={{0,8},{4,36},{8,16},{12,44},{16,24},{20,52},{24,0},{28,60},{32,40}... | collective-permute-start | bytes 1179656 | tf_op jit(solution)/shard_map/ppermute | solution.py:35
  51.6 10.6 %collective-permute-start.12 = (bf16[128,512]{1,0:T(8,128)(2,1)S(1)}, bf16[128,512]{1,0:T(8,128)(2,1)S(1)}, u32[]{:S(2)}, u32[]{:S(2)}) collective-permute-start(bf16[128,512]{1,0:T(8,128)(2,1)S(1)} %constant_dynamic-update-slice_fusion.7), channel_id=1, source_target_pairs={{0,64},{64,0},{1,65},{65,1},{2,66},{66,2},{3,67},{67,3},{4,68},{68... | collective-permute-start | bytes 393224 | tf_op jit(solution)/shard_map/ppermute | solution.py:363
  62.9 2.2 %copy-start.2 = (bf16[2048,1024]{1,0:T(8,128)(2,1)S(1)}, bf16[2048,1024]{1,0:T(8,128)(2,1)}, u32[]{:S(2)}) copy-start(bf16[2048,1024]{1,0:T(8,128)(2,1)} %all-gather.5.cloned.1.call-done) | copy-start | bytes 12582916
  107.9 2.2 %copy-start.1 = (bf16[32,128,512]{2,1,0:T(8,128)(2,1)S(1)}, bf16[32,128,512]{2,1,0:T(8,128)(2,1)}, u32[]{:S(2)}) copy-start(bf16[32,128,512]{2,1,0:T(8,128)(2,1)} %all-gather.7.cloned.1.call-done) | copy-start | bytes 12582916
Sparse Core Ops, SparseCore 0:
  9.2 49.8 all-gather.4
  63.1 40.2 all-gather.6

commit v5 on v4

--- a/solution.py
+++ b/solution.py
@@ -20,8 +20,8 @@
 MODES = 8
 SUB = 8
 STEPS = BLOCK // SUB
-EDGE = 2 * MODES
-EDGE_ROWS = 40
+EDGE = 4 * MODES
+EDGE_ROWS = 56
 GROUP = 64
 F32 = jnp.float32
 BF16 = jnp.bfloat16
@@ -56,6 +56,7 @@
     edge_out,
     proj,
     gated,
+    edge,
 ):
     own_y, own_x, own_zh, own_c = pos[0], pos[1], pos[2], pos[3]
 
@@ -86,7 +87,6 @@
     gain = skip[...]
     for zh in range(2):
         streams = []
-        edges = []
         for s in range(3):
             lanes = slice(s * LANES, (s + 1) * LANES)
             tap = [taps[3 * s + m : 3 * s + m + 1, :] for m in range(3)]
@@ -94,16 +94,13 @@
             for m in range(3):
                 total = total + tap[m] * proj[zh, 8 - m : 8 - m + BLOCK, lanes]
             streams.append(total)
-            before = proj[zh, BLOCK + 6 : BLOCK + 7, lanes]
-            last = proj[zh, BLOCK + 7 : BLOCK + 8, lanes]
-            edges.append([tap[1] * last + tap[2] * before, tap[2] * last])
         gated[zh * BLOCK : (zh + 1) * BLOCK, :] = streams[0] * streams[2]
         gate_out[zh * BLOCK : (zh + 1) * BLOCK, :] = streams[1]
-        rows = [streams[0][0:1], streams[0][1:2], streams[2][0:1], streams[2][1:2]]
-        rows = rows + edges[0] + edges[2] + edges[1]
-        for chip in range(CHIPS):
-            for k, row in enumerate(rows):
-                edge_out[chip, EDGE + zh * 10 + k : EDGE + zh * 10 + k + 1, :] = row
+        for k, (s, row) in enumerate(((0, 8), (2, 8), (0, -2), (2, -2), (1, -2))):
+            row = row if row > 0 else 8 + BLOCK + row
+            start = EDGE + 10 * zh + 2 * k
+            edge[start : start + 2, :] = proj[zh, row : row + 2, s * LANES : (s + 1) * LANES]
+    edge[EDGE + 20 :, :] = jnp.zeros((EDGE_ROWS - EDGE - 20, LANES), F32)
     rate = rates[...]
     decay = jnp.exp(-rate)
     weight = residues[...]
@@ -127,8 +124,12 @@
         for sub in range(SUB):
             start = zh * SUB * MODES + sub * MODES
             total = long_decay * total + sub_out[start : start + MODES, :]
-        for chip in range(CHIPS):
-            edge_out[chip, zh * MODES : (zh + 1) * MODES, :] = total
+        upper = total.astype(BF16).astype(F32)
+        edge[zh * MODES : (zh + 1) * MODES, :] = upper
+        edge[(2 + zh) * MODES : (3 + zh) * MODES, :] = total - upper
+    sent = edge[...].astype(BF16)
+    for chip in range(CHIPS):
+        edge_out[chip] = sent
 
 
 def front(pos, slabs, weights, taps, rates, residues, skip):
@@ -140,13 +141,14 @@
             jax.ShapeDtypeStruct((2 * BLOCK, LANES), F32),
             jax.ShapeDtypeStruct((2 * BLOCK, LANES), F32),
             jax.ShapeDtypeStruct((2 * SUB * MODES, LANES), F32),
-            jax.ShapeDtypeStruct((CHIPS, EDGE_ROWS, LANES), F32),
+            jax.ShapeDtypeStruct((CHIPS, EDGE_ROWS, LANES), BF16),
         ),
         in_specs=[smem] + [vmem] * 10,
         out_specs=(vmem,) * 4,
         scratch_shapes=[
             pltpu.VMEM((2, 8 + BLOCK, WIDE), F32),
             pltpu.VMEM((2 * BLOCK, LANES), F32),
+            pltpu.VMEM((EDGE_ROWS, LANES), F32),
         ],
         compiler_params=pltpu.CompilerParams(vmem_limit_bytes=40 * 1024 * 1024),
         cost_estimate=pl.CostEstimate(
@@ -156,9 +158,12 @@
 
 
 def back_kernel(
-    pos, edges, sub_states, y_in, gate_in, rates, residues, skip, out, carried, mixed, head
+    pos, sent, sub_states, y_in, gate_in, taps, rates, residues, skip,
+    out, edges, carried, mixed, head,
 ):
     block = pos[0] * 4 + pos[1]
+    edges[...] = sent[...].astype(F32)
+    tap = [[taps[3 * s + m : 3 * s + m + 1, :] for m in range(3)] for s in range(3)]
     rate = rates[...]
     weight = residues[...]
     decay = jnp.exp(-rate)
@@ -168,9 +173,18 @@
     def rows(chip, zh, start, count):
         return edges[chip, EDGE + 10 * zh + start : EDGE + 10 * zh + start + count, :]
 
+    def own(s, pair):
+        return tap[s][0] * pair[0:1], tap[s][0] * pair[1:2] + tap[s][1] * pair[0:1]
+
+    def ahead_of(s, pair):
+        return tap[s][1] * pair[1:2] + tap[s][2] * pair[0:1], tap[s][2] * pair[1:2]
+
     def late(chip, zh, tails):
-        first, second = rows(chip, zh, 0, 2), rows(chip, zh, 2, 2)
-        return (first + tails[0:2]) * (second + tails[2:4]) - first * second
+        first, second = own(0, rows(chip, zh, 0, 2)), own(2, rows(chip, zh, 2, 2))
+        one, two = ahead_of(0, tails[0:2]), ahead_of(2, tails[2:4])
+        return [
+            (first[k] + one[k]) * (second[k] + two[k]) - first[k] * second[k] for k in range(2)
+        ]
 
     carry = [jnp.zeros((MODES, LANES), F32) for _ in range(2)]
     for other in range(CHIPS):
@@ -180,11 +194,14 @@
         far = jnp.exp(-rate * ((distance + CHIPS).astype(F32) * float(BLOCK)))
         states = []
         for zh in range(2):
-            state = edges[other, zh * MODES : (zh + 1) * MODES, :]
+            state = (
+                edges[other, zh * MODES : (zh + 1) * MODES, :]
+                + edges[other, (2 + zh) * MODES : (3 + zh) * MODES, :]
+            )
             if other > 0 or zh == 1:
                 ahead = (other - 1, zh) if other > 0 else (CHIPS - 1, 0)
                 added = late(other, zh, rows(*ahead, 4, 4))
-                state = state + last[0] * added[0:1] + last[1] * added[1:2]
+                state = state + last[0] * added[0] + last[1] * added[1]
             states.append(state)
         carry[0] = carry[0] + near * states[0]
         carry[1] = carry[1] + near * states[1] + far * states[0]
@@ -199,7 +216,7 @@
         else:
             tails = jnp.where(block == 0, rows(CHIPS - 1, 0, 4, 6), tails)
         added = late(block, zh, tails)
-        state = carry[zh] + growth * (added[0:1] + growth * added[1:2])
+        state = carry[zh] + growth * (added[0] + growth * added[1])
         for sub in range(SUB):
             start = zh * SUB * MODES + sub * MODES
             carried[start : start + MODES, :] = weight * state
@@ -214,12 +231,13 @@
             while len(sums) > 1:
                 sums = [sums[k] + sums[k + 1] for k in range(0, len(sums), 2)]
             mixed[at, :] = y_in[at, :] + sums[0]
-        early = jnp.sum(weight * growth, axis=0, keepdims=True) * added[1:2]
+        early = jnp.sum(weight * growth, axis=0, keepdims=True) * added[1]
         start = zh * BLOCK
-        mixed[start : start + 1, :] = mixed[start : start + 1, :] + gain * added[0:1] - early
-        mixed[start + 1 : start + 2, :] = mixed[start + 1 : start + 2, :] + gain * added[1:2]
+        mixed[start : start + 1, :] = mixed[start : start + 1, :] + gain * added[0] - early
+        mixed[start + 1 : start + 2, :] = mixed[start + 1 : start + 2, :] + gain * added[1]
         head[...] = gate_in[start : start + 16, :]
-        head[0:2, :] = head[0:2, :] + tails[4:6]
+        for k, row in enumerate(ahead_of(1, tails[4:6])):
+            head[k : k + 1, :] = head[k : k + 1, :] + row
         for c in range(2):
             at = slice(start + c * HALF, start + (c + 1) * HALF)
             gate_rows = (gate_in[at, :] * mixed[at, :]).astype(BF16)
@@ -230,15 +248,16 @@
             out[2 * zh * 4 + zl, 0:16, :] = first_rows
 
 
-def back(pos, edges, sub_states, y, gate, rates, residues, skip):
+def back(pos, edges, sub_states, y, gate, taps, rates, residues, skip):
     vmem = pl.BlockSpec(memory_space=pltpu.VMEM)
     smem = pl.BlockSpec(memory_space=pltpu.SMEM)
     return pl.pallas_call(
         back_kernel,
         out_shape=jax.ShapeDtypeStruct((16, HALF, LANES), BF16),
-        in_specs=[smem] + [vmem] * 7,
+        in_specs=[smem] + [vmem] * 8,
         out_specs=vmem,
         scratch_shapes=[
+            pltpu.VMEM((CHIPS, EDGE_ROWS, LANES), F32),
             pltpu.VMEM((2 * SUB * MODES, LANES), F32),
             pltpu.VMEM((2 * BLOCK, LANES), F32),
             pltpu.VMEM((16, LANES), F32),
@@ -247,7 +266,7 @@
         cost_estimate=pl.CostEstimate(
             flops=4_000_000, bytes_accessed=800_000, transcendentals=40_000
         ),
-    )(pos, edges, sub_states, y, gate, rates, residues, skip)
+    )(pos, edges, sub_states, y, gate, taps, rates, residues, skip)
 
 
 def out_kernel(pos, gates, weights, out):
@@ -259,7 +278,7 @@
             zl = high * 2 + (own_yh if flip == 0 else 1 - own_yh)
             left = [gates[(2 * zh + c) * 4 + zl] for zh in range(2) for c in range(2)]
             right = [
-                weights[x, yl, c, flip, depth]
+                weights[yl, x, c, flip, depth]
                 for yl in range(2)
                 for x in range(4)
                 for c in range(2)
@@ -367,12 +386,12 @@
 
     slabs, in_weights[3] = lax.optimization_barrier((slabs, in_weights[3]))
 
-    gathered = lax.all_gather(jnp.stack([moved, flipped]), ("x", "yl", "c"), axis=0, tiled=False)
-    gathered = gathered.reshape(4, 2, 2, 2, 2, GROUP, 512)
+    gathered = lax.all_gather(jnp.stack([moved, flipped]), ("yl", "x", "c"), axis=0, tiled=False)
+    gathered = gathered.reshape(2, 4, 2, 2, 2, GROUP, 512)
 
     mixed, gate, sub_states, edges = front(pos, slabs, in_weights, taps, rates, weights, skip)
     edges = lax.all_to_all(edges, PLANE, split_axis=0, concat_axis=0, tiled=True)
-    gate_out = back(pos, edges, sub_states, mixed, gate, rates, weights, skip)
+    gate_out = back(pos, edges, sub_states, mixed, gate, taps, rates, weights, skip)
     gates = lax.all_to_all(gate_out, ("zh", "c", "zl"), split_axis=0, concat_axis=0, tiled=True)
     return project_out(pos, gates, gathered)
 

time: 121 us -> 119 us (0.983)
  blocking collectives: 38.2 us -> 36.2 us
    all_to_all x1, blocking collectives: 15.5 us -> 13.7 us  [shards(): lax.all_to_all(edges, PLANE, split_axis=0, concat_axis=0, tiled=True)]
where the time goes in v5:
time: 119 us; the launch traced here: 118 us
  blocking collectives  36.2 us (30%)
  waiting for transfers between devices  30.4 us (26%)
  starting transfers between devices  22.3 us (19%)
  between operations  13.5 us (11%)
  Pallas kernels  7.43 us (6%)
  local copies, waits for them, and re-layouts  6.96 us (6%)
    all_to_all x1, blocking collectives, shards(): lax.all_to_all(gate_out, ('zh', 'c', 'zl'), split_axis=0, concat_axis=0,...  22.4 us
    ppermute x7, waiting for transfers between devices, crossed(): return lax.ppermute(block, PLANE + ('c',), route)  20.9 us
    all_to_all x1, blocking collectives, shards(): lax.all_to_all(edges, PLANE, split_axis=0, concat_axis=0, tiled=True)  13.7 us
    ppermute x7, starting transfers between devices, crossed(): return lax.ppermute(block, PLANE + ('c',), route)  9.45 us
    ppermute x3, starting transfers between devices, quarter(): lax.ppermute(quarters[flip], ('zh', 'c'), [(i, i ^ flip) for i in range(4)])  8.97 us
    ppermute x3, waiting for transfers between devices, quarter(): lax.ppermute(quarters[flip], ('zh', 'c'), [(i, i ^ flip) for i in range(4)])  7.23 us
    unnamed x11, local copies, waits for them, and re-layouts  5.36 us
    pallas_call x1, Pallas kernels, front(): pl.pallas_call(front_kernel, out_shape=(jax.ShapeDtypeStruct((2 * BLOCK,...  3.53 us
  transfers between devices with their start and end apart: 15, of which 10 were waited for; matrix products, arithmetic and copies ran while one was open for 2% of the time, Pallas kernels for 4%

profile of v5, /device:TPU:1, one launch (start us, length us, event | category | flops | bytes accessed | tf_op | source)
XLA Modules:
  0.0 117.7 jit_solution(2043175788154241193)
XLA Ops:
  6.5 0.0 copy-start
  6.5 0.0 all-gather.5.cloned.1.call-start
  6.5 0.7 all-gather.5.cloned.1.call-update
  7.3 0.0 all-gather.7.cloned.1.call-start
  7.3 0.0 copy-start.3
  7.3 0.9 copy-done.3
  8.3 3.3 %collective-permute-start = (bf16[64,384]{1,0:T(8,128)(2,1)S(1)}, bf16[64,384]{1,0:T(8,128)(2,1)S(1)}, u32[]{:S(2)}, u32[]{:S(2)}) collective-permute-start(bf16[64,384]{1,0:T(8,128)(2,1)S(1)} %get-tuple-element.31), channel_id=1, source_target_pairs={{0,4},{4,0},{128,132},{132,128},{1,5},{5,1},{129,133},{133,129},{2... | collective-permute-start | bytes 147464 | tf_op jit(solution)/shard_map/ppermute | solution.py:353
  11.6 5.2 %collective-permute-start.1 = (bf16[64,384]{1,0:T(8,128)(2,1)S(1)}, bf16[64,384]{1,0:T(8,128)(2,1)S(1)}, u32[]{:S(2)}, u32[]{:S(2)}) collective-permute-start(bf16[64,384]{1,0:T(8,128)(2,1)S(1)} %get-tuple-element.32), channel_id=1, source_target_pairs={{0,128},{4,132},{128,0},{132,4},{1,129},{5,133},{129,1},{133,5},{2... | collective-permute-start | bytes 147464 | tf_op jit(solution)/shard_map/ppermute | solution.py:353
  16.8 0.4 collective-permute-start.2
  17.2 0.0 collective-permute-done
  17.3 1.3 %collective-permute-done.1 = bf16[64,384]{1,0:T(8,128)(2,1)S(1)} collective-permute-done((bf16[64,384]{1,0:T(8,128)(2,1)S(1)}, bf16[64,384]{1,0:T(8,128)(2,1)S(1)}, u32[]{:S(2)}, u32[]{:S(2)}) %collective-permute-start.1) | collective-permute-done | bytes 49184 | tf_op jit(solution)/shard_map/ppermute | solution.py:353
  18.6 5.9 %collective-permute-done.2 = bf16[64,384]{1,0:T(8,128)(2,1)S(1)} collective-permute-done((bf16[64,384]{1,0:T(8,128)(2,1)S(1)}, bf16[64,384]{1,0:T(8,128)(2,1)S(1)}, u32[]{:S(2)}, u32[]{:S(2)}) %collective-permute-start.2) | collective-permute-done | bytes 49184 | tf_op jit(solution)/shard_map/ppermute | solution.py:353
  24.6 1.4 %collective-permute-start.3 = (bf16[256,384]{1,0:T(8,128)(2,1)S(1)}, bf16[256,384]{1,0:T(8,128)(2,1)S(1)}, u32[]{:S(2)}, u32[]{:S(2)}) collective-permute-start(bf16[256,384]{1,0:T(8,128)(2,1)S(1)} %pad_maximum_fusion.1), channel_id=1, source_target_pairs={{0,32},{4,12},{8,40},{12,20},{16,48},{20,28},{24,56},{28,4},{32,64... | collective-permute-start | bytes 589832 | tf_op jit(solution)/shard_map/ppermute | solution.py:35
  26.0 1.4 %collective-permute-start.4 = (bf16[256,384]{1,0:T(8,128)(2,1)S(1)}, bf16[256,384]{1,0:T(8,128)(2,1)S(1)}, u32[]{:S(2)}, u32[]{:S(2)}) collective-permute-start(bf16[256,384]{1,0:T(8,128)(2,1)S(1)} %pad_maximum_fusion.1), channel_id=1, source_target_pairs={{0,96},{4,28},{8,104},{12,4},{16,112},{20,12},{24,120},{28,20},{32... | collective-permute-start | bytes 589832 | tf_op jit(solution)/shard_map/ppermute | solution.py:35
  27.4 1.6 %collective-permute-start.5 = (bf16[256,384]{1,0:T(8,128)(2,1)S(1)}, bf16[256,384]{1,0:T(8,128)(2,1)S(1)}, u32[]{:S(2)}, u32[]{:S(2)}) collective-permute-start(bf16[256,384]{1,0:T(8,128)(2,1)S(1)} %pad_maximum_fusion.1), channel_id=1, source_target_pairs={{0,64},{4,20},{8,72},{12,28},{16,80},{20,4},{24,88},{28,12},{32,96... | collective-permute-start | bytes 589832 | tf_op jit(solution)/shard_map/ppermute | solution.py:35
  29.0 1.8 %collective-permute-done.3 = bf16[256,384]{1,0:T(8,128)(2,1)S(1)} collective-permute-done((bf16[256,384]{1,0:T(8,128)(2,1)S(1)}, bf16[256,384]{1,0:T(8,128)(2,1)S(1)}, u32[]{:S(2)}, u32[]{:S(2)}) %collective-permute-start.3) | collective-permute-done | bytes 196640 | tf_op jit(solution)/shard_map/ppermute | solution.py:35
  30.8 0.1 collective-permute-done.4
  31.0 2.9 %collective-permute-done.5 = bf16[256,384]{1,0:T(8,128)(2,1)S(1)} collective-permute-done((bf16[256,384]{1,0:T(8,128)(2,1)S(1)}, bf16[256,384]{1,0:T(8,128)(2,1)S(1)}, u32[]{:S(2)}, u32[]{:S(2)}) %collective-permute-start.5) | collective-permute-done | bytes 196640 | tf_op jit(solution)/shard_map/ppermute | solution.py:35
  34.0 2.8 %collective-permute-start.7 = (bf16[1024,384]{1,0:T(8,128)(2,1)S(1)}, bf16[1024,384]{1,0:T(8,128)(2,1)S(1)}, u32[]{:S(2)}, u32[]{:S(2)}) collective-permute-start(bf16[1024,384]{1,0:T(8,128)(2,1)S(1)} %constant_dynamic-update-slice_fusion.w0), channel_id=1, source_target_pairs={{0,24},{4,100},{8,0},{12,108},{16,8},{20,116},{24,16},{28,124},{32... | collective-permute-start | bytes 2359304 | tf_op jit(solution)/shard_map/ppermute | solution.py:35
  36.8 0.0 collective-permute-start.6
  36.8 0.8 collective-permute-start.9
  37.6 1.5 %collective-permute-start.8 = (bf16[64,512]{1,0:T(8,128)(2,1)}, bf16[64,512]{1,0:T(8,128)(2,1)S(1)}, u32[]{:S(2)}, u32[]{:S(2)}) collective-permute-start(bf16[64,512]{1,0:T(8,128)(2,1)} %bitcast.20), channel_id=1, source_target_pairs={{0,0},{1,64},{2,128},{3,192},{4,4},{5,68},{6,132},{7,196},{8,8},{9... | collective-permute-start | bytes 196616 | tf_op jit(solution)/shard_map/ppermute | solution.py:375
  39.1 0.0 copy-done
  39.1 0.8 dynamic-slice_bitcast_fusion.2.skip
  39.9 0.7 dynamic-slice_bitcast_fusion
  40.6 0.1 pad_add_fusion.pos
  40.7 1.6 %collective-permute-done.9 = bf16[64,512]{1,0:T(8,128)(2,1)S(1)} collective-permute-done((bf16[64,512]{1,0:T(8,128)(2,1)}, bf16[64,512]{1,0:T(8,128)(2,1)S(1)}, u32[]{:S(2)}, u32[]{:S(2)}) %collective-permute-start.9) | collective-permute-done | bytes 65568 | tf_op jit(solution)/shard_map/ppermute | solution.py:375
  42.3 0.0 collective-permute-done.8
  42.3 5.6 %collective-permute-done.7.w2 = bf16[1024,384]{1,0:T(8,128)(2,1)S(1)} collective-permute-done((bf16[1024,384]{1,0:T(8,128)(2,1)S(1)}, bf16[1024,384]{1,0:T(8,128)(2,1)S(1)}, u32[]{:S(2)}, u32[]{:S(2)}) %collective-permute-start.7) | collective-permute-done | bytes 786464 | tf_op jit(solution)/shard_map/ppermute | solution.py:35
  47.9 1.4 %collective-permute-done.6.w1 = bf16[1024,384]{1,0:T(8,128)(2,1)S(1)} collective-permute-done((bf16[1024,384]{1,0:T(8,128)(2,1)S(1)}, bf16[1024,384]{1,0:T(8,128)(2,1)S(1)}, u32[]{:S(2)}, u32[]{:S(2)}) %collective-permute-start.6) | collective-permute-done | bytes 786464 | tf_op jit(solution)/shard_map/ppermute | solution.py:35
  49.3 2.2 %collective-permute-start.11 = (bf16[512,384]{1,0:T(8,128)(2,1)S(1)}, bf16[512,384]{1,0:T(8,128)(2,1)S(1)}, u32[]{:S(2)}, u32[]{:S(2)}) collective-permute-start(bf16[512,384]{1,0:T(8,128)(2,1)S(1)} %slice.7), channel_id=1, source_target_pairs={{0,24},{4,100},{8,0},{12,108},{16,8},{20,116},{24,16},{28,124},{32... | collective-permute-start | bytes 1179656 | tf_op jit(solution)/shard_map/ppermute | solution.py:35
  51.5 0.0 collective-permute-start.10
  51.6 1.6 %collective-permute-start.12 = (bf16[128,512]{1,0:T(8,128)(2,1)S(1)}, bf16[128,512]{1,0:T(8,128)(2,1)S(1)}, u32[]{:S(2)}, u32[]{:S(2)}) collective-permute-start(bf16[128,512]{1,0:T(8,128)(2,1)S(1)} %constant_dynamic-update-slice_fusion.7), channel_id=1, source_target_pairs={{0,64},{64,0},{1,65},{65,1},{2,66},{66,2},{3,67},{67,3},{4,68},{68... | collective-permute-start | bytes 393224 | tf_op jit(solution)/shard_map/ppermute | solution.py:382
  53.1 4.5 %collective-permute-done.11.w4 = bf16[512,384]{1,0:T(8,128)(2,1)S(1)} collective-permute-done((bf16[512,384]{1,0:T(8,128)(2,1)S(1)}, bf16[512,384]{1,0:T(8,128)(2,1)S(1)}, u32[]{:S(2)}, u32[]{:S(2)}) %collective-permute-start.11) | collective-permute-done | bytes 393248 | tf_op jit(solution)/shard_map/ppermute | solution.py:35
  57.7 4.5 %collective-permute-done.10.w3 = bf16[512,384]{1,0:T(8,128)(2,1)S(1)} collective-permute-done((bf16[512,384]{1,0:T(8,128)(2,1)S(1)}, bf16[512,384]{1,0:T(8,128)(2,1)S(1)}, u32[]{:S(2)}, u32[]{:S(2)}) %collective-permute-start.10) | collective-permute-done | bytes 393248 | tf_op jit(solution)/shard_map/ppermute | solution.py:35
  62.2 0.0 all-gather.5.cloned.1.call-done
  62.2 0.0 collective-permute-done.12
  62.2 0.7 pad_maximum_fusion
  62.9 0.0 all-gather.7.cloned.1.call-update
  62.9 0.0 copy-start.2
  62.9 2.2 %copy-done.2 = bf16[2048,1024]{1,0:T(8,128)(2,1)S(1)} copy-done((bf16[2048,1024]{1,0:T(8,128)(2,1)S(1)}, bf16[2048,1024]{1,0:T(8,128)(2,1)}, u32[]{:S(2)}) %copy-start.2) | copy-done | bytes 4194328
  65.1 3.5 %shard_map.74 = (f32[512,128]{1,0:T(8,128)S(1)}, f32[512,128]{1,0:T(8,128)S(1)}, f32[128,128]{1,0:T(8,128)S(1)}, bf16[16,56,128]{2,1,0:T(8,128)(2,1)S(1)}) custom-call(s32[4]{0:T(128)S(1)} %pad_add_fusion.pos, bf16[2,4,2,128,1024]{4,3,2,1,0:T(8,128)(2,1)S(1)} %bitcast.16, bf16[1024,384]{1,0:T(8,128)(2,1)S(1)} %constant_dynamic-update-slice_fusion.w0, ...), custom_call_target="tpu_custom_call" | custom-call | flops 1610612736 | bytes 6000000 | tf_op jit(solution)/shard_map/pallas_call | solution.py:138
  68.7 13.7 %all_to_all.10.sent = bf16[16,56,128]{2,1,0:T(8,128)(2,1)S(1)} all-to-all(bf16[16,56,128]{2,1,0:T(8,128)(2,1)S(1)} %get-tuple-element.50), channel_id=1, replica_groups=mesh['zh'=2,'yh'=2,'yl'=2,'x'=4,'c'=2,'zl'=4] {'yh','yl','x'}, dimensions={0} | all-to-all | bytes 458752 | tf_op jit(solution)/shard_map/all_to_all | solution.py:393
  82.4 1.1 shard_map.75
  83.5 22.4 %all_to_all.11.gates = bf16[16,128,128]{2,1,0:T(8,128)(2,1)S(1)} all-to-all(bf16[16,128,128]{2,1,0:T(8,128)(2,1)S(1)} %shard_map.75), channel_id=1, replica_groups=mesh['zh'=2,'yh'=2,'yl'=2,'x'=4,'c'=2,'zl'=4] {'zh','c','zl'}, dimensions={0} | all-to-all | bytes 1048576 | tf_op jit(solution)/shard_map/all_to_all | solution.py:395
  106.0 0.0 all-gather.7.cloned.1.call-done
  106.0 2.2 %copy-done.1 = bf16[32,128,512]{2,1,0:T(8,128)(2,1)S(1)} copy-done((bf16[32,128,512]{2,1,0:T(8,128)(2,1)S(1)}, bf16[32,128,512]{2,1,0:T(8,128)(2,1)}, u32[]{:S(2)}) %copy-start.1) | copy-done | bytes 4194328
  108.2 2.7 %shard_map.76 = bf16[128,1024]{1,0:T(8,128)(2,1)} custom-call(s32[4]{0:T(128)S(1)} %pad_add_fusion.pos, bf16[16,128,128]{2,1,0:T(8,128)(2,1)S(1)} %all_to_all.11.gates, bf16[2,4,2,2,2,64,512]{6,5,4,3,2,1,0:T(8,128)(2,1)S(1)} %bitcast.15), custom_call_target="tpu_custom_call" | custom-call | flops 536870912 | bytes 5000000 | tf_op jit(solution)/shard_map/pallas_call | solution.py:298
  (16 shorter events, 0.4 us)
Async XLA Ops:
  6.5 32.6 %copy-start = (f32[3,3,512]{2,1,0:T(4,128)S(1)}, f32[3,3,512]{2,1,0:T(4,128)}, u32[]{:S(2)}) copy-start(f32[3,3,512]{2,1,0:T(4,128)} %param.9) | copy-start | bytes 55300
  6.5 55.6 %all-gather.5.cloned.1.call-start = ((), (), s32[]{:S(2)}) async-start(), calls=%async_computation.2 | async-start | bytes 4456448 | tf_op jit(solution)/shard_map/all_gather | solution.py:345
  7.3 98.7 %all-gather.7.cloned.1.call-start = ((), (), s32[]{:S(2)}) async-start(), calls=%async_computation.3 | async-start | bytes 4456448 | tf_op jit(solution)/shard_map/all_gather | solution.py:389
  7.3 0.9 copy-start.3
  8.3 9.0 %collective-permute-start = (bf16[64,384]{1,0:T(8,128)(2,1)S(1)}, bf16[64,384]{1,0:T(8,128)(2,1)S(1)}, u32[]{:S(2)}, u32[]{:S(2)}) collective-permute-start(bf16[64,384]{1,0:T(8,128)(2,1)S(1)} %get-tuple-element.31), channel_id=1, source_target_pairs={{0,4},{4,0},{128,132},{132,128},{1,5},{5,1},{129,133},{133,129},{2... | collective-permute-start | bytes 147464 | tf_op jit(solution)/shard_map/ppermute | solution.py:353
  11.6 7.0 %collective-permute-start.1 = (bf16[64,384]{1,0:T(8,128)(2,1)S(1)}, bf16[64,384]{1,0:T(8,128)(2,1)S(1)}, u32[]{:S(2)}, u32[]{:S(2)}) collective-permute-start(bf16[64,384]{1,0:T(8,128)(2,1)S(1)} %get-tuple-element.32), channel_id=1, source_target_pairs={{0,128},{4,132},{128,0},{132,4},{1,129},{5,133},{129,1},{133,5},{2... | collective-permute-start | bytes 147464 | tf_op jit(solution)/shard_map/ppermute | solution.py:353
  16.8 7.7 %collective-permute-start.2 = (bf16[64,384]{1,0:T(8,128)(2,1)S(1)}, bf16[64,384]{1,0:T(8,128)(2,1)S(1)}, u32[]{:S(2)}, u32[]{:S(2)}) collective-permute-start(bf16[64,384]{1,0:T(8,128)(2,1)S(1)} %get-tuple-element.33), channel_id=1, source_target_pairs={{0,132},{4,128},{128,4},{132,0},{1,133},{5,129},{129,5},{133,1},{2... | collective-permute-start | bytes 147464 | tf_op jit(solution)/shard_map/ppermute | solution.py:353
  24.6 6.2 %collective-permute-start.3 = (bf16[256,384]{1,0:T(8,128)(2,1)S(1)}, bf16[256,384]{1,0:T(8,128)(2,1)S(1)}, u32[]{:S(2)}, u32[]{:S(2)}) collective-permute-start(bf16[256,384]{1,0:T(8,128)(2,1)S(1)} %pad_maximum_fusion.1), channel_id=1, source_target_pairs={{0,32},{4,12},{8,40},{12,20},{16,48},{20,28},{24,56},{28,4},{32,64... | collective-permute-start | bytes 589832 | tf_op jit(solution)/shard_map/ppermute | solution.py:35
  26.0 4.9 %collective-permute-start.4 = (bf16[256,384]{1,0:T(8,128)(2,1)S(1)}, bf16[256,384]{1,0:T(8,128)(2,1)S(1)}, u32[]{:S(2)}, u32[]{:S(2)}) collective-permute-start(bf16[256,384]{1,0:T(8,128)(2,1)S(1)} %pad_maximum_fusion.1), channel_id=1, source_target_pairs={{0,96},{4,28},{8,104},{12,4},{16,112},{20,12},{24,120},{28,20},{32... | collective-permute-start | bytes 589832 | tf_op jit(solution)/shard_map/ppermute | solution.py:35
  27.4 6.5 %collective-permute-start.5 = (bf16[256,384]{1,0:T(8,128)(2,1)S(1)}, bf16[256,384]{1,0:T(8,128)(2,1)S(1)}, u32[]{:S(2)}, u32[]{:S(2)}) collective-permute-start(bf16[256,384]{1,0:T(8,128)(2,1)S(1)} %pad_maximum_fusion.1), channel_id=1, source_target_pairs={{0,64},{4,20},{8,72},{12,28},{16,80},{20,4},{24,88},{28,12},{32,96... | collective-permute-start | bytes 589832 | tf_op jit(solution)/shard_map/ppermute | solution.py:35
  34.0 13.9 %collective-permute-start.7 = (bf16[1024,384]{1,0:T(8,128)(2,1)S(1)}, bf16[1024,384]{1,0:T(8,128)(2,1)S(1)}, u32[]{:S(2)}, u32[]{:S(2)}) collective-permute-start(bf16[1024,384]{1,0:T(8,128)(2,1)S(1)} %constant_dynamic-update-slice_fusion.w0), channel_id=1, source_target_pairs={{0,24},{4,100},{8,0},{12,108},{16,8},{20,116},{24,16},{28,124},{32... | collective-permute-start | bytes 2359304 | tf_op jit(solution)/shard_map/ppermute | solution.py:35
  36.8 12.5 %collective-permute-start.6 = (bf16[1024,384]{1,0:T(8,128)(2,1)S(1)}, bf16[1024,384]{1,0:T(8,128)(2,1)S(1)}, u32[]{:S(2)}, u32[]{:S(2)}) collective-permute-start(bf16[1024,384]{1,0:T(8,128)(2,1)S(1)} %constant_dynamic-update-slice_fusion.w0), channel_id=1, source_target_pairs={{0,8},{4,36},{8,16},{12,44},{16,24},{20,52},{24,0},{28,60},{32,40}... | collective-permute-start | bytes 2359304 | tf_op jit(solution)/shard_map/ppermute | solution.py:35
  36.8 5.5 %collective-permute-start.9 = (bf16[64,512]{1,0:T(8,128)(2,1)}, bf16[64,512]{1,0:T(8,128)(2,1)S(1)}, u32[]{:S(2)}, u32[]{:S(2)}) collective-permute-start(bf16[64,512]{1,0:T(8,128)(2,1)} %bitcast.19), channel_id=1, source_target_pairs={{0,128},{1,192},{2,0},{3,64},{4,132},{5,196},{6,4},{7,68},{8,136},... | collective-permute-start | bytes 196616 | tf_op jit(solution)/shard_map/ppermute | solution.py:375
  37.6 4.7 %collective-permute-start.8 = (bf16[64,512]{1,0:T(8,128)(2,1)}, bf16[64,512]{1,0:T(8,128)(2,1)S(1)}, u32[]{:S(2)}, u32[]{:S(2)}) collective-permute-start(bf16[64,512]{1,0:T(8,128)(2,1)} %bitcast.20), channel_id=1, source_target_pairs={{0,0},{1,64},{2,128},{3,192},{4,4},{5,68},{6,132},{7,196},{8,8},{9... | collective-permute-start | bytes 196616 | tf_op jit(solution)/shard_map/ppermute | solution.py:375
  49.3 8.3 %collective-permute-start.11 = (bf16[512,384]{1,0:T(8,128)(2,1)S(1)}, bf16[512,384]{1,0:T(8,128)(2,1)S(1)}, u32[]{:S(2)}, u32[]{:S(2)}) collective-permute-start(bf16[512,384]{1,0:T(8,128)(2,1)S(1)} %slice.7), channel_id=1, source_target_pairs={{0,24},{4,100},{8,0},{12,108},{16,8},{20,116},{24,16},{28,124},{32... | collective-permute-start | bytes 1179656 | tf_op jit(solution)/shard_map/ppermute | solution.py:35
  51.5 10.6 %collective-permute-start.10 = (bf16[512,384]{1,0:T(8,128)(2,1)S(1)}, bf16[512,384]{1,0:T(8,128)(2,1)S(1)}, u32[]{:S(2)}, u32[]{:S(2)}) collective-permute-start(bf16[512,384]{1,0:T(8,128)(2,1)S(1)} %slice.6), channel_id=1, source_target_pairs={{0,8},{4,36},{8,16},{12,44},{16,24},{20,52},{24,0},{28,60},{32,40}... | collective-permute-start | bytes 1179656 | tf_op jit(solution)/shard_map/ppermute | solution.py:35
  51.6 10.6 %collective-permute-start.12 = (bf16[128,512]{1,0:T(8,128)(2,1)S(1)}, bf16[128,512]{1,0:T(8,128)(2,1)S(1)}, u32[]{:S(2)}, u32[]{:S(2)}) collective-permute-start(bf16[128,512]{1,0:T(8,128)(2,1)S(1)} %constant_dynamic-update-slice_fusion.7), channel_id=1, source_target_pairs={{0,64},{64,0},{1,65},{65,1},{2,66},{66,2},{3,67},{67,3},{4,68},{68... | collective-permute-start | bytes 393224 | tf_op jit(solution)/shard_map/ppermute | solution.py:382
  62.9 2.2 %copy-start.2 = (bf16[2048,1024]{1,0:T(8,128)(2,1)S(1)}, bf16[2048,1024]{1,0:T(8,128)(2,1)}, u32[]{:S(2)}) copy-start(bf16[2048,1024]{1,0:T(8,128)(2,1)} %all-gather.5.cloned.1.call-done) | copy-start | bytes 12582916
  106.0 2.2 %copy-start.1 = (bf16[32,128,512]{2,1,0:T(8,128)(2,1)S(1)}, bf16[32,128,512]{2,1,0:T(8,128)(2,1)}, u32[]{:S(2)}) copy-start(bf16[32,128,512]{2,1,0:T(8,128)(2,1)} %all-gather.7.cloned.1.call-done) | copy-start | bytes 12582916
Sparse Core Ops, SparseCore 0:
  9.2 49.8 all-gather.4
  63.1 39.6 all-gather.6

commit v6 on v5

--- a/solution.py
+++ b/solution.py
@@ -278,7 +278,7 @@
             zl = high * 2 + (own_yh if flip == 0 else 1 - own_yh)
             left = [gates[(2 * zh + c) * 4 + zl] for zh in range(2) for c in range(2)]
             right = [
-                weights[yl, x, c, flip, depth]
+                weights[yl, x, c, flip, depth ^ c]
                 for yl in range(2)
                 for x in range(4)
                 for c in range(2)
@@ -331,7 +331,7 @@
     for zh, yh, yl, x, c, zl in np.ndindex(*SIZES):
         source = int(np.ravel_multi_index((zh, yh, yl, x, c, zl), SIZES))
         for flip in range(2):
-            target = ((zl // 2) ^ flip, zl % 2, yl, x, c, zh * 2 + yh)
+            target = ((zl // 2) ^ flip ^ c, zl % 2, yl, x, c, zh * 2 + yh)
             routes[flip].append((source, int(np.ravel_multi_index(target, SIZES))))
     return routes
 

time: 119 us -> 122 us (1.025)
  starting transfers between devices: 22.3 us -> 30.8 us
  waiting for transfers between devices: 30.4 us -> 24.5 us
    ppermute x7, waiting for transfers between devices: 20.9 us -> 13.6 us  [crossed(): return lax.ppermute(block, PLANE + ('c',), route)]
    ppermute x2, starting transfers between devices: 2.3 us -> 8.38 us  [shards(): lax.ppermute(out_weight.T, AXES, route)]
    all_to_all x1, blocking collectives: 22.4 us -> 25.3 us  [shards(): lax.all_to_all(gate_out, ('zh', 'c', 'zl'), split_axis=0, concat_axis=0,...]
    all_to_all x1, blocking collectives: 13.7 us -> 11.6 us  [shards(): lax.all_to_all(edges, PLANE, split_axis=0, concat_axis=0, tiled=True)]
    ppermute x7, starting transfers between devices: 9.45 us -> 11.6 us  [crossed(): return lax.ppermute(block, PLANE + ('c',), route)]
    ppermute x2, waiting for transfers between devices: 1.61 us -> 2.88 us  [shards(): lax.ppermute(out_weight.T, AXES, route)]
  transfers between devices with their start and end apart: 15 -> 15, of which waited for: 10 -> 8; matrix products, arithmetic and copies ran while one was open for 2% -> 2% of each run, Pallas kernels for 4% -> 4%
where the time goes in v6:
time: 122 us; the launch traced here: 121 us
  blocking collectives  36.8 us (30%)
  starting transfers between devices  30.8 us (25%)
  waiting for transfers between devices  24.5 us (20%)
  between operations  13.6 us (11%)
  Pallas kernels  7.41 us (6%)
  local copies, waits for them, and re-layouts  6.97 us (6%)
    all_to_all x1, blocking collectives, shards(): lax.all_to_all(gate_out, ('zh', 'c', 'zl'), split_axis=0, concat_axis=0,...  25.3 us
    ppermute x7, waiting for transfers between devices, crossed(): return lax.ppermute(block, PLANE + ('c',), route)  13.6 us
    all_to_all x1, blocking collectives, shards(): lax.all_to_all(edges, PLANE, split_axis=0, concat_axis=0, tiled=True)  11.6 us
    ppermute x7, starting transfers between devices, crossed(): return lax.ppermute(block, PLANE + ('c',), route)  11.6 us
    ppermute x3, starting transfers between devices, quarter(): lax.ppermute(quarters[flip], ('zh', 'c'), [(i, i ^ flip) for i in range(4)])  8.97 us
    ppermute x2, starting transfers between devices, shards(): lax.ppermute(out_weight.T, AXES, route)  8.38 us
    ppermute x3, waiting for transfers between devices, quarter(): lax.ppermute(quarters[flip], ('zh', 'c'), [(i, i ^ flip) for i in range(4)])  7.23 us
    unnamed x11, local copies, waits for them, and re-layouts  5.36 us
  transfers between devices with their start and end apart: 15, of which 8 were waited for; matrix products, arithmetic and copies ran while one was open for 2% of the time, Pallas kernels for 4%

profile of v6, /device:TPU:1, one launch (start us, length us, event | category | flops | bytes accessed | tf_op | source)
XLA Modules:
  0.0 120.9 jit_solution(16795512158575204176)
XLA Ops:
  6.5 0.0 copy-start
  6.5 0.0 all-gather.5.cloned.1.call-start
  6.5 0.7 all-gather.5.cloned.1.call-update
  7.3 0.0 all-gather.7.cloned.1.call-start
  7.3 0.0 copy-start.3
  7.3 0.9 copy-done.3
  8.3 3.3 %collective-permute-start = (bf16[64,384]{1,0:T(8,128)(2,1)S(1)}, bf16[64,384]{1,0:T(8,128)(2,1)S(1)}, u32[]{:S(2)}, u32[]{:S(2)}) collective-permute-start(bf16[64,384]{1,0:T(8,128)(2,1)S(1)} %get-tuple-element.31), channel_id=1, source_target_pairs={{0,4},{4,0},{128,132},{132,128},{1,5},{5,1},{129,133},{133,129},{2... | collective-permute-start | bytes 147464 | tf_op jit(solution)/shard_map/ppermute | solution.py:353
  11.6 5.2 %collective-permute-start.1 = (bf16[64,384]{1,0:T(8,128)(2,1)S(1)}, bf16[64,384]{1,0:T(8,128)(2,1)S(1)}, u32[]{:S(2)}, u32[]{:S(2)}) collective-permute-start(bf16[64,384]{1,0:T(8,128)(2,1)S(1)} %get-tuple-element.32), channel_id=1, source_target_pairs={{0,128},{4,132},{128,0},{132,4},{1,129},{5,133},{129,1},{133,5},{2... | collective-permute-start | bytes 147464 | tf_op jit(solution)/shard_map/ppermute | solution.py:353
  16.8 0.4 collective-permute-start.2
  17.2 0.0 collective-permute-done
  17.3 1.3 %collective-permute-done.1 = bf16[64,384]{1,0:T(8,128)(2,1)S(1)} collective-permute-done((bf16[64,384]{1,0:T(8,128)(2,1)S(1)}, bf16[64,384]{1,0:T(8,128)(2,1)S(1)}, u32[]{:S(2)}, u32[]{:S(2)}) %collective-permute-start.1) | collective-permute-done | bytes 49184 | tf_op jit(solution)/shard_map/ppermute | solution.py:353
  18.6 5.9 %collective-permute-done.2 = bf16[64,384]{1,0:T(8,128)(2,1)S(1)} collective-permute-done((bf16[64,384]{1,0:T(8,128)(2,1)S(1)}, bf16[64,384]{1,0:T(8,128)(2,1)S(1)}, u32[]{:S(2)}, u32[]{:S(2)}) %collective-permute-start.2) | collective-permute-done | bytes 49184 | tf_op jit(solution)/shard_map/ppermute | solution.py:353
  24.6 1.4 %collective-permute-start.3 = (bf16[256,384]{1,0:T(8,128)(2,1)S(1)}, bf16[256,384]{1,0:T(8,128)(2,1)S(1)}, u32[]{:S(2)}, u32[]{:S(2)}) collective-permute-start(bf16[256,384]{1,0:T(8,128)(2,1)S(1)} %pad_maximum_fusion.1), channel_id=1, source_target_pairs={{0,32},{4,12},{8,40},{12,20},{16,48},{20,28},{24,56},{28,4},{32,64... | collective-permute-start | bytes 589832 | tf_op jit(solution)/shard_map/ppermute | solution.py:35
  26.0 1.4 %collective-permute-start.4 = (bf16[256,384]{1,0:T(8,128)(2,1)S(1)}, bf16[256,384]{1,0:T(8,128)(2,1)S(1)}, u32[]{:S(2)}, u32[]{:S(2)}) collective-permute-start(bf16[256,384]{1,0:T(8,128)(2,1)S(1)} %pad_maximum_fusion.1), channel_id=1, source_target_pairs={{0,96},{4,28},{8,104},{12,4},{16,112},{20,12},{24,120},{28,20},{32... | collective-permute-start | bytes 589832 | tf_op jit(solution)/shard_map/ppermute | solution.py:35
  27.4 1.6 %collective-permute-start.5 = (bf16[256,384]{1,0:T(8,128)(2,1)S(1)}, bf16[256,384]{1,0:T(8,128)(2,1)S(1)}, u32[]{:S(2)}, u32[]{:S(2)}) collective-permute-start(bf16[256,384]{1,0:T(8,128)(2,1)S(1)} %pad_maximum_fusion.1), channel_id=1, source_target_pairs={{0,64},{4,20},{8,72},{12,28},{16,80},{20,4},{24,88},{28,12},{32,96... | collective-permute-start | bytes 589832 | tf_op jit(solution)/shard_map/ppermute | solution.py:35
  29.0 1.8 %collective-permute-done.3 = bf16[256,384]{1,0:T(8,128)(2,1)S(1)} collective-permute-done((bf16[256,384]{1,0:T(8,128)(2,1)S(1)}, bf16[256,384]{1,0:T(8,128)(2,1)S(1)}, u32[]{:S(2)}, u32[]{:S(2)}) %collective-permute-start.3) | collective-permute-done | bytes 196640 | tf_op jit(solution)/shard_map/ppermute | solution.py:35
  30.8 0.1 collective-permute-done.4
  31.0 2.9 %collective-permute-done.5 = bf16[256,384]{1,0:T(8,128)(2,1)S(1)} collective-permute-done((bf16[256,384]{1,0:T(8,128)(2,1)S(1)}, bf16[256,384]{1,0:T(8,128)(2,1)S(1)}, u32[]{:S(2)}, u32[]{:S(2)}) %collective-permute-start.5) | collective-permute-done | bytes 196640 | tf_op jit(solution)/shard_map/ppermute | solution.py:35
  34.0 2.8 %collective-permute-start.7 = (bf16[1024,384]{1,0:T(8,128)(2,1)S(1)}, bf16[1024,384]{1,0:T(8,128)(2,1)S(1)}, u32[]{:S(2)}, u32[]{:S(2)}) collective-permute-start(bf16[1024,384]{1,0:T(8,128)(2,1)S(1)} %constant_dynamic-update-slice_fusion.w0), channel_id=1, source_target_pairs={{0,24},{4,100},{8,0},{12,108},{16,8},{20,116},{24,16},{28,124},{32... | collective-permute-start | bytes 2359304 | tf_op jit(solution)/shard_map/ppermute | solution.py:35
  36.8 0.0 collective-permute-start.6
  36.8 1.5 %collective-permute-start.9 = (bf16[64,512]{1,0:T(8,128)(2,1)}, bf16[64,512]{1,0:T(8,128)(2,1)S(1)}, u32[]{:S(2)}, u32[]{:S(2)}) collective-permute-start(bf16[64,512]{1,0:T(8,128)(2,1)} %bitcast.19), channel_id=1, source_target_pairs={{0,128},{1,192},{2,0},{3,64},{4,4},{5,68},{6,132},{7,196},{8,136},... | collective-permute-start | bytes 196616 | tf_op jit(solution)/shard_map/ppermute | solution.py:375
  38.3 6.9 %collective-permute-start.8 = (bf16[64,512]{1,0:T(8,128)(2,1)}, bf16[64,512]{1,0:T(8,128)(2,1)S(1)}, u32[]{:S(2)}, u32[]{:S(2)}) collective-permute-start(bf16[64,512]{1,0:T(8,128)(2,1)} %bitcast.20), channel_id=1, source_target_pairs={{0,0},{1,64},{2,128},{3,192},{4,132},{5,196},{6,4},{7,68},{8,8},{9... | collective-permute-start | bytes 196616 | tf_op jit(solution)/shard_map/ppermute | solution.py:375
  45.2 0.0 copy-done
  45.3 0.8 dynamic-slice_bitcast_fusion.2.skip
  46.0 0.7 dynamic-slice_bitcast_fusion
  46.7 0.1 pad_add_fusion.pos
  46.8 0.0 collective-permute-done.9
  46.8 2.9 %collective-permute-done.8 = bf16[64,512]{1,0:T(8,128)(2,1)S(1)} collective-permute-done((bf16[64,512]{1,0:T(8,128)(2,1)}, bf16[64,512]{1,0:T(8,128)(2,1)S(1)}, u32[]{:S(2)}, u32[]{:S(2)}) %collective-permute-start.8) | collective-permute-done | bytes 65568 | tf_op jit(solution)/shard_map/ppermute | solution.py:375
  49.7 0.0 collective-permute-done.7.w2
  49.7 0.0 collective-permute-done.6.w1
  49.8 4.3 %collective-permute-start.11 = (bf16[512,384]{1,0:T(8,128)(2,1)S(1)}, bf16[512,384]{1,0:T(8,128)(2,1)S(1)}, u32[]{:S(2)}, u32[]{:S(2)}) collective-permute-start(bf16[512,384]{1,0:T(8,128)(2,1)S(1)} %slice.7), channel_id=1, source_target_pairs={{0,24},{4,100},{8,0},{12,108},{16,8},{20,116},{24,16},{28,124},{32... | collective-permute-start | bytes 1179656 | tf_op jit(solution)/shard_map/ppermute | solution.py:35
  54.1 0.0 collective-permute-start.10
  54.1 1.8 %collective-permute-start.12 = (bf16[128,512]{1,0:T(8,128)(2,1)S(1)}, bf16[128,512]{1,0:T(8,128)(2,1)S(1)}, u32[]{:S(2)}, u32[]{:S(2)}) collective-permute-start(bf16[128,512]{1,0:T(8,128)(2,1)S(1)} %constant_dynamic-update-slice_fusion.7), channel_id=1, source_target_pairs={{0,64},{64,0},{1,65},{65,1},{2,66},{66,2},{3,67},{67,3},{4,68},{68... | collective-permute-start | bytes 393224 | tf_op jit(solution)/shard_map/ppermute | solution.py:382
  55.9 4.3 %collective-permute-done.11.w4 = bf16[512,384]{1,0:T(8,128)(2,1)S(1)} collective-permute-done((bf16[512,384]{1,0:T(8,128)(2,1)S(1)}, bf16[512,384]{1,0:T(8,128)(2,1)S(1)}, u32[]{:S(2)}, u32[]{:S(2)}) %collective-permute-start.11) | collective-permute-done | bytes 393248 | tf_op jit(solution)/shard_map/ppermute | solution.py:35
  60.2 4.5 %collective-permute-done.10.w3 = bf16[512,384]{1,0:T(8,128)(2,1)S(1)} collective-permute-done((bf16[512,384]{1,0:T(8,128)(2,1)S(1)}, bf16[512,384]{1,0:T(8,128)(2,1)S(1)}, u32[]{:S(2)}, u32[]{:S(2)}) %collective-permute-start.10) | collective-permute-done | bytes 393248 | tf_op jit(solution)/shard_map/ppermute | solution.py:35
  64.7 0.0 all-gather.5.cloned.1.call-done
  64.7 0.0 collective-permute-done.12
  64.7 0.7 pad_maximum_fusion
  65.5 0.0 all-gather.7.cloned.1.call-update
  65.5 0.0 copy-start.2
  65.5 2.2 %copy-done.2 = bf16[2048,1024]{1,0:T(8,128)(2,1)S(1)} copy-done((bf16[2048,1024]{1,0:T(8,128)(2,1)S(1)}, bf16[2048,1024]{1,0:T(8,128)(2,1)}, u32[]{:S(2)}) %copy-start.2) | copy-done | bytes 4194328
  67.7 3.5 %shard_map.74 = (f32[512,128]{1,0:T(8,128)S(1)}, f32[512,128]{1,0:T(8,128)S(1)}, f32[128,128]{1,0:T(8,128)S(1)}, bf16[16,56,128]{2,1,0:T(8,128)(2,1)S(1)}) custom-call(s32[4]{0:T(128)S(1)} %pad_add_fusion.pos, bf16[2,4,2,128,1024]{4,3,2,1,0:T(8,128)(2,1)S(1)} %bitcast.16, bf16[1024,384]{1,0:T(8,128)(2,1)S(1)} %constant_dynamic-update-slice_fusion.w0, ...), custom_call_target="tpu_custom_call" | custom-call | flops 1610612736 | bytes 6000000 | tf_op jit(solution)/shard_map/pallas_call | solution.py:138
  71.2 11.6 %all_to_all.10.sent = bf16[16,56,128]{2,1,0:T(8,128)(2,1)S(1)} all-to-all(bf16[16,56,128]{2,1,0:T(8,128)(2,1)S(1)} %get-tuple-element.50), channel_id=1, replica_groups=mesh['zh'=2,'yh'=2,'yl'=2,'x'=4,'c'=2,'zl'=4] {'yh','yl','x'}, dimensions={0} | all-to-all | bytes 458752 | tf_op jit(solution)/shard_map/all_to_all | solution.py:393
  82.8 1.1 shard_map.75
  83.9 25.3 %all_to_all.11.gates = bf16[16,128,128]{2,1,0:T(8,128)(2,1)S(1)} all-to-all(bf16[16,128,128]{2,1,0:T(8,128)(2,1)S(1)} %shard_map.75), channel_id=1, replica_groups=mesh['zh'=2,'yh'=2,'yl'=2,'x'=4,'c'=2,'zl'=4] {'zh','c','zl'}, dimensions={0} | all-to-all | bytes 1048576 | tf_op jit(solution)/shard_map/all_to_all | solution.py:395
  109.2 0.0 all-gather.7.cloned.1.call-done
  109.2 2.2 %copy-done.1 = bf16[32,128,512]{2,1,0:T(8,128)(2,1)S(1)} copy-done((bf16[32,128,512]{2,1,0:T(8,128)(2,1)S(1)}, bf16[32,128,512]{2,1,0:T(8,128)(2,1)}, u32[]{:S(2)}) %copy-start.1) | copy-done | bytes 4194328
  111.4 2.7 %shard_map.76 = bf16[128,1024]{1,0:T(8,128)(2,1)} custom-call(s32[4]{0:T(128)S(1)} %pad_add_fusion.pos, bf16[16,128,128]{2,1,0:T(8,128)(2,1)S(1)} %all_to_all.11.gates, bf16[2,4,2,2,2,64,512]{6,5,4,3,2,1,0:T(8,128)(2,1)S(1)} %bitcast.15), custom_call_target="tpu_custom_call" | custom-call | flops 536870912 | bytes 5000000 | tf_op jit(solution)/shard_map/pallas_call | solution.py:298
  (16 shorter events, 0.4 us)
Async XLA Ops:
  6.5 38.7 %copy-start = (f32[3,3,512]{2,1,0:T(4,128)S(1)}, f32[3,3,512]{2,1,0:T(4,128)}, u32[]{:S(2)}) copy-start(f32[3,3,512]{2,1,0:T(4,128)} %param.9) | copy-start | bytes 55300
  6.5 58.2 %all-gather.5.cloned.1.call-start = ((), (), s32[]{:S(2)}) async-start(), calls=%async_computation.2 | async-start | bytes 4456448 | tf_op jit(solution)/shard_map/all_gather | solution.py:345
  7.3 102.0 %all-gather.7.cloned.1.call-start = ((), (), s32[]{:S(2)}) async-start(), calls=%async_computation.3 | async-start | bytes 4456448 | tf_op jit(solution)/shard_map/all_gather | solution.py:389
  7.3 0.9 copy-start.3
  8.3 9.0 %collective-permute-start = (bf16[64,384]{1,0:T(8,128)(2,1)S(1)}, bf16[64,384]{1,0:T(8,128)(2,1)S(1)}, u32[]{:S(2)}, u32[]{:S(2)}) collective-permute-start(bf16[64,384]{1,0:T(8,128)(2,1)S(1)} %get-tuple-element.31), channel_id=1, source_target_pairs={{0,4},{4,0},{128,132},{132,128},{1,5},{5,1},{129,133},{133,129},{2... | collective-permute-start | bytes 147464 | tf_op jit(solution)/shard_map/ppermute | solution.py:353
  11.6 7.0 %collective-permute-start.1 = (bf16[64,384]{1,0:T(8,128)(2,1)S(1)}, bf16[64,384]{1,0:T(8,128)(2,1)S(1)}, u32[]{:S(2)}, u32[]{:S(2)}) collective-permute-start(bf16[64,384]{1,0:T(8,128)(2,1)S(1)} %get-tuple-element.32), channel_id=1, source_target_pairs={{0,128},{4,132},{128,0},{132,4},{1,129},{5,133},{129,1},{133,5},{2... | collective-permute-start | bytes 147464 | tf_op jit(solution)/shard_map/ppermute | solution.py:353
  16.8 7.7 %collective-permute-start.2 = (bf16[64,384]{1,0:T(8,128)(2,1)S(1)}, bf16[64,384]{1,0:T(8,128)(2,1)S(1)}, u32[]{:S(2)}, u32[]{:S(2)}) collective-permute-start(bf16[64,384]{1,0:T(8,128)(2,1)S(1)} %get-tuple-element.33), channel_id=1, source_target_pairs={{0,132},{4,128},{128,4},{132,0},{1,133},{5,129},{129,5},{133,1},{2... | collective-permute-start | bytes 147464 | tf_op jit(solution)/shard_map/ppermute | solution.py:353
  24.6 6.2 %collective-permute-start.3 = (bf16[256,384]{1,0:T(8,128)(2,1)S(1)}, bf16[256,384]{1,0:T(8,128)(2,1)S(1)}, u32[]{:S(2)}, u32[]{:S(2)}) collective-permute-start(bf16[256,384]{1,0:T(8,128)(2,1)S(1)} %pad_maximum_fusion.1), channel_id=1, source_target_pairs={{0,32},{4,12},{8,40},{12,20},{16,48},{20,28},{24,56},{28,4},{32,64... | collective-permute-start | bytes 589832 | tf_op jit(solution)/shard_map/ppermute | solution.py:35
  26.0 4.9 %collective-permute-start.4 = (bf16[256,384]{1,0:T(8,128)(2,1)S(1)}, bf16[256,384]{1,0:T(8,128)(2,1)S(1)}, u32[]{:S(2)}, u32[]{:S(2)}) collective-permute-start(bf16[256,384]{1,0:T(8,128)(2,1)S(1)} %pad_maximum_fusion.1), channel_id=1, source_target_pairs={{0,96},{4,28},{8,104},{12,4},{16,112},{20,12},{24,120},{28,20},{32... | collective-permute-start | bytes 589832 | tf_op jit(solution)/shard_map/ppermute | solution.py:35
  27.4 6.5 %collective-permute-start.5 = (bf16[256,384]{1,0:T(8,128)(2,1)S(1)}, bf16[256,384]{1,0:T(8,128)(2,1)S(1)}, u32[]{:S(2)}, u32[]{:S(2)}) collective-permute-start(bf16[256,384]{1,0:T(8,128)(2,1)S(1)} %pad_maximum_fusion.1), channel_id=1, source_target_pairs={{0,64},{4,20},{8,72},{12,28},{16,80},{20,4},{24,88},{28,12},{32,96... | collective-permute-start | bytes 589832 | tf_op jit(solution)/shard_map/ppermute | solution.py:35
  34.0 15.7 %collective-permute-start.7 = (bf16[1024,384]{1,0:T(8,128)(2,1)S(1)}, bf16[1024,384]{1,0:T(8,128)(2,1)S(1)}, u32[]{:S(2)}, u32[]{:S(2)}) collective-permute-start(bf16[1024,384]{1,0:T(8,128)(2,1)S(1)} %constant_dynamic-update-slice_fusion.w0), channel_id=1, source_target_pairs={{0,24},{4,100},{8,0},{12,108},{16,8},{20,116},{24,16},{28,124},{32... | collective-permute-start | bytes 2359304 | tf_op jit(solution)/shard_map/ppermute | solution.py:35
  36.8 12.9 %collective-permute-start.6 = (bf16[1024,384]{1,0:T(8,128)(2,1)S(1)}, bf16[1024,384]{1,0:T(8,128)(2,1)S(1)}, u32[]{:S(2)}, u32[]{:S(2)}) collective-permute-start(bf16[1024,384]{1,0:T(8,128)(2,1)S(1)} %constant_dynamic-update-slice_fusion.w0), channel_id=1, source_target_pairs={{0,8},{4,36},{8,16},{12,44},{16,24},{20,52},{24,0},{28,60},{32,40}... | collective-permute-start | bytes 2359304 | tf_op jit(solution)/shard_map/ppermute | solution.py:35
  36.8 10.0 %collective-permute-start.9 = (bf16[64,512]{1,0:T(8,128)(2,1)}, bf16[64,512]{1,0:T(8,128)(2,1)S(1)}, u32[]{:S(2)}, u32[]{:S(2)}) collective-permute-start(bf16[64,512]{1,0:T(8,128)(2,1)} %bitcast.19), channel_id=1, source_target_pairs={{0,128},{1,192},{2,0},{3,64},{4,4},{5,68},{6,132},{7,196},{8,136},... | collective-permute-start | bytes 196616 | tf_op jit(solution)/shard_map/ppermute | solution.py:375
  38.3 11.4 %collective-permute-start.8 = (bf16[64,512]{1,0:T(8,128)(2,1)}, bf16[64,512]{1,0:T(8,128)(2,1)S(1)}, u32[]{:S(2)}, u32[]{:S(2)}) collective-permute-start(bf16[64,512]{1,0:T(8,128)(2,1)} %bitcast.20), channel_id=1, source_target_pairs={{0,0},{1,64},{2,128},{3,192},{4,132},{5,196},{6,4},{7,68},{8,8},{9... | collective-permute-start | bytes 196616 | tf_op jit(solution)/shard_map/ppermute | solution.py:375
  49.8 10.4 %collective-permute-start.11 = (bf16[512,384]{1,0:T(8,128)(2,1)S(1)}, bf16[512,384]{1,0:T(8,128)(2,1)S(1)}, u32[]{:S(2)}, u32[]{:S(2)}) collective-permute-start(bf16[512,384]{1,0:T(8,128)(2,1)S(1)} %slice.7), channel_id=1, source_target_pairs={{0,24},{4,100},{8,0},{12,108},{16,8},{20,116},{24,16},{28,124},{32... | collective-permute-start | bytes 1179656 | tf_op jit(solution)/shard_map/ppermute | solution.py:35
  54.1 10.6 %collective-permute-start.10 = (bf16[512,384]{1,0:T(8,128)(2,1)S(1)}, bf16[512,384]{1,0:T(8,128)(2,1)S(1)}, u32[]{:S(2)}, u32[]{:S(2)}) collective-permute-start(bf16[512,384]{1,0:T(8,128)(2,1)S(1)} %slice.6), channel_id=1, source_target_pairs={{0,8},{4,36},{8,16},{12,44},{16,24},{20,52},{24,0},{28,60},{32,40}... | collective-permute-start | bytes 1179656 | tf_op jit(solution)/shard_map/ppermute | solution.py:35
  54.1 10.6 %collective-permute-start.12 = (bf16[128,512]{1,0:T(8,128)(2,1)S(1)}, bf16[128,512]{1,0:T(8,128)(2,1)S(1)}, u32[]{:S(2)}, u32[]{:S(2)}) collective-permute-start(bf16[128,512]{1,0:T(8,128)(2,1)S(1)} %constant_dynamic-update-slice_fusion.7), channel_id=1, source_target_pairs={{0,64},{64,0},{1,65},{65,1},{2,66},{66,2},{3,67},{67,3},{4,68},{68... | collective-permute-start | bytes 393224 | tf_op jit(solution)/shard_map/ppermute | solution.py:382
  65.5 2.2 %copy-start.2 = (bf16[2048,1024]{1,0:T(8,128)(2,1)S(1)}, bf16[2048,1024]{1,0:T(8,128)(2,1)}, u32[]{:S(2)}) copy-start(bf16[2048,1024]{1,0:T(8,128)(2,1)} %all-gather.5.cloned.1.call-done) | copy-start | bytes 12582916
  109.2 2.2 %copy-start.1 = (bf16[32,128,512]{2,1,0:T(8,128)(2,1)S(1)}, bf16[32,128,512]{2,1,0:T(8,128)(2,1)}, u32[]{:S(2)}) copy-start(bf16[32,128,512]{2,1,0:T(8,128)(2,1)} %all-gather.7.cloned.1.call-done) | copy-start | bytes 12582916
Sparse Core Ops, SparseCore 0:
  9.2 49.1 all-gather.4
  65.6 40.0 all-gather.6
